TPU v7x, 32 devices: a whole 2x2x4 slice. The times are simulated.
32 devices in a mesh: section: 2 (over x), expert: 4 (over z), shard: 4 (over y, core).
Axes of the slice: x: 2, y: 2, z: 4, core: 2. Of those that a mesh axis runs over, the one named last changes fastest.
Arguments:
- inputs: bfloat16 [4, 2048, 1536], P(None, ('expert', 'shard')), may hold values from -6 to 6
- segments: int32 [4, 4, 512], P(None, 'expert'), may hold values from 0 to 63, as said below
- routes: int32 [4, 2048, 4], P(None, ('expert', 'shard')), may hold values from 0 to 15, all different within a row; in each aligned block of 128 rows (0 to 127, 128 to 255, ..., all dimensions but the last counted through in order) at most 40 rows name the same one
- gate_weights: float32 [4, 2048, 4], P(None, ('expert', 'shard')), may hold values from 0.1 to 0.4
- query_weight: float32 [2, 1536, 1536], P('section', ('expert', 'shard')), may hold values from -0.21875 to 0.21875
- key_value_weight: float32 [2, 1536, 512], P('section', ('expert', 'shard')), may hold values from -0.21875 to 0.21875
- output_weight: float32 [2, 1536, 1536], P('section', ('expert', 'shard')), may hold values from -0.875 to 0.875
- norm_gains: float32 [2, 2, 1536], P('section', None, ('expert', 'shard')), may hold values from 0.5 to 1.5
- expert_gate_up: float32 [2, 16, 1536, 1536], P('section', 'expert', 'shard'), may hold values from -0.15625 to 0.15625
- expert_down: float32 [2, 16, 768, 1536], P('section', 'expert', 'shard'), may hold values from -0.21875 to 0.21875
- cotangent: bfloat16 [4, 2048, 1536], P(None, ('expert', 'shard')), may hold values from -6 to 6
Outputs:
- output: float32 [4, 2048, 1536], P('section', ('expert', 'shard'))
- input_grad: float32 [4, 2048, 1536], P('section', ('expert', 'shard'))
- query_grad: float32 [2, 1536, 1536], P('section', ('expert', 'shard'))
- key_value_grad: float32 [2, 1536, 512], P('section', ('expert', 'shard'))
- output_weight_grad: float32 [2, 1536, 1536], P('section', ('expert', 'shard'))
- gain_grad: float32 [2, 2, 1536], P('section', None, ('expert', 'shard'))
- gate_up_grad: float32 [2, 16, 1536, 1536], P('section', 'expert', 'shard')
- down_grad: float32 [2, 16, 768, 1536], P('section', 'expert', 'shard')
Inputs may be any that keep to these rules, and one draw needn't show every extreme that they name: `routes`: each row names 4 different experts. In each block of 128 rows (the rows of one device in one micro-batch), no expert is named by more than 40 rows, and in some blocks one is named by exactly 40. `segments`: along each sequence the numbers start at 0 and never fall.
All inputs are finite; a program needn't handle non-finite values.
Results may differ from a plain program's by a relative error of at most 0.025.
The roundings to bfloat16 on the way count: a program that leaves them out, or rounds other values in their place, can miss the bound.
Values may be sent and summed in bfloat16 or wider, within the bound.
A program may use at most 320 MiB of HBM per device.

v0:
```python
import jax
import jax.numpy as jnp
from jax import lax
from jax.sharding import PartitionSpec as P

D = 1536
HEADS = 12
KV_HEADS = 2
HD = 128
FF = 768
TOPK = 4
EXP_DEV = 4
MICRO = 4


epsilon = 1e-06
rope_base = 10000.0


def passed_along(value, axis, steps):
    count = lax.axis_size(axis)
    initial, last = (max(0, -steps), min(count, count - steps))
    return lax.ppermute(value, axis, [(source, source + steps) for source in range(initial, last)])


def from_partner(value, axis, bit):
    mask = 2**bit
    pairs = [(source, source ^ mask) for source in range(lax.axis_size(axis))]
    return lax.ppermute(value, axis, pairs)


def norm_forward(hidden, gain_row):
    inverse = lax.rsqrt(jnp.mean(hidden * hidden, axis=-1, keepdims=True) + epsilon)
    return (hidden * inverse * gain_row, inverse)


def norm_backward(hidden, inverse, gain_row, grad_normed):
    scaled = grad_normed * gain_row
    gain_term = jnp.sum(grad_normed * hidden * inverse, axis=0)
    row_inner = jnp.mean(scaled * hidden, axis=-1, keepdims=True)
    return (inverse * scaled - hidden * inverse * inverse * inverse * row_inner, gain_term)


def rotate(values, cosine, sine_table):
    width_half = values.shape[-1] // 2
    first_part = values[..., :width_half]
    second_part = values[..., width_half:]
    return jnp.concatenate(
        [
            first_part * cosine - second_part * sine_table,
            second_part * cosine + first_part * sine_table,
        ],
        axis=-1,
    )


def route_plan(routes_now, gates_now, experts, capacity):
    flat_routes = routes_now.reshape(-1)
    one_hot = (flat_routes[:, None] == jnp.arange(experts, dtype=jnp.int32)[None, :]).astype(
        jnp.int32
    )
    slot_rank = jnp.sum((jnp.cumsum(one_hot, axis=0) - one_hot) * one_hot, axis=1)
    slot_place = flat_routes * capacity + slot_rank
    source = jnp.arange(flat_routes.shape[0], dtype=jnp.int32) // TOPK
    anchor = jnp.zeros((experts * capacity,), jnp.int32).at[slot_place].set(source)
    filled = jnp.zeros((experts * capacity,), jnp.bfloat16).at[slot_place].set(1.0)
    slot_gate = (
        jnp.zeros((experts * capacity,), jnp.float32).at[slot_place].set(gates_now.reshape(-1))
    )
    return (slot_place, anchor, filled, slot_gate)


def shards(
    inputs,
    segments,
    routes,
    gate_weights,
    query_weight,
    key_value_weight,
    output_weight,
    norm_gains,
    expert_gate_up,
    expert_down,
    cotangent,
):
    section_index = lax.axis_index("section")
    first_section = section_index == 0
    shard_index = lax.axis_index("shard")
    tokens = inputs.shape[1]
    length = tokens * lax.axis_size("shard")
    experts = EXP_DEV * lax.axis_size("expert")
    capacity = 5 * tokens * TOPK // (4 * experts)
    group_size = HEADS // KV_HEADS
    width_q = HEADS * HD
    width_kv = KV_HEADS * HD
    score_scale = HD ** (-0.5)
    layer_parts = (
        lax.all_gather(query_weight.astype(jnp.bfloat16), ("expert", "shard"), axis=1, tiled=True),
        lax.all_gather(
            key_value_weight.astype(jnp.bfloat16), ("expert", "shard"), axis=1, tiled=True
        ),
        lax.all_gather(output_weight.astype(jnp.bfloat16), ("expert", "shard"), axis=1, tiled=True),
        lax.all_gather(norm_gains.astype(jnp.bfloat16), ("expert", "shard"), axis=2, tiled=True),
    )
    weight_q = layer_parts[0][0]
    weight_kv = layer_parts[1][0]
    weight_o = layer_parts[2][0]
    gain_pair = layer_parts[3][0].astype(jnp.float32)
    expert_parts = (
        lax.all_gather(expert_gate_up.astype(jnp.bfloat16), "shard", axis=2, tiled=True),
        lax.all_gather(expert_down.astype(jnp.bfloat16), "shard", axis=2, tiled=True),
    )
    weight_in = expert_parts[0][0]
    weight_down = expert_parts[1][0]
    offset = shard_index * tokens
    position = (offset + jnp.arange(tokens, dtype=jnp.int32)).astype(jnp.float32)
    frequency = rope_base ** (-jnp.arange(HD // 2, dtype=jnp.float32) / (HD // 2))
    angles = position[:, None] * frequency[None, :]
    cosine = jnp.cos(angles)[:, None, :]
    sine_table = jnp.sin(angles)[:, None, :]
    query_place = jnp.tile(offset + jnp.arange(tokens, dtype=jnp.int32), group_size)
    key_place = jnp.arange(length, dtype=jnp.int32)

    def allowed_of(micro_index):
        segment_all = lax.dynamic_index_in_dim(segments, micro_index, 0, keepdims=False)[0]
        segment_own = lax.dynamic_slice_in_dim(segment_all, offset, tokens)
        query_segment = jnp.tile(segment_own, group_size)
        return (query_segment[:, None] == segment_all[None, :]) & (
            query_place[:, None] >= key_place[None, :]
        )

    def micro_data(micro_index):
        routes_now = lax.dynamic_index_in_dim(routes, micro_index, 0, keepdims=False)
        gates_now = lax.dynamic_index_in_dim(gate_weights, micro_index, 0, keepdims=False)
        return (route_plan(routes_now, gates_now, experts, capacity), gates_now)

    def score_rows(queries_low, all_kv, allowed):
        stacked = (
            queries_low.reshape(tokens, KV_HEADS, group_size, HD)
            .transpose(1, 2, 0, 3)
            .reshape(KV_HEADS, group_size * tokens, HD)
        )
        key_rows = all_kv[:, :width_kv].reshape(length, KV_HEADS, HD)
        raw_scores = jnp.einsum(
            "hqd,khd->hqk", stacked, key_rows, preferred_element_type=jnp.float32
        )
        return (stacked, key_rows, jnp.where(allowed[None], raw_scores * score_scale, -1e30))

    forward_saved = []
    forward_results = []
    received = jnp.zeros((tokens, D), jnp.float32)
    for step_index in range(MICRO + 1):
        micro_index = jnp.clip(step_index - section_index, 0, MICRO - 1)
        own_input = inputs[min(step_index, MICRO - 1)].astype(jnp.float32)
        start = jnp.where(first_section, own_input, received)
        forward_allowed = allowed_of(micro_index)
        (slot_place, anchor, filled, slot_gate), forward_gates_now = micro_data(micro_index)
        normed_one, inverse_one = norm_forward(start, gain_pair[0])
        normed_low = normed_one.astype(jnp.bfloat16)
        queries = jnp.dot(normed_low, weight_q, preferred_element_type=jnp.float32)
        keys_values = jnp.dot(normed_low, weight_kv, preferred_element_type=jnp.float32)
        forward_queries_low = (
            rotate(queries.reshape(tokens, HEADS, HD), cosine, sine_table)
            .reshape(tokens, width_q)
            .astype(jnp.bfloat16)
        )
        key_rot = rotate(
            keys_values[:, :width_kv].reshape(tokens, KV_HEADS, HD), cosine, sine_table
        ).reshape(tokens, width_kv)
        local_kv = jnp.concatenate([key_rot, keys_values[:, width_kv:]], axis=1).astype(
            jnp.bfloat16
        )
        forward_all_kv = lax.all_gather(local_kv, "shard", axis=0, tiled=True)
        forward_stacked, forward_key_rows, scores = score_rows(
            forward_queries_low, forward_all_kv, forward_allowed
        )
        row_max = jnp.max(scores, axis=-1, keepdims=True)
        weights = jnp.exp(scores - row_max)
        row_sum = jnp.sum(weights, axis=-1, keepdims=True)
        probs_low = (weights / row_sum).astype(jnp.bfloat16)
        value_rows = forward_all_kv[:, width_kv:].reshape(length, KV_HEADS, HD)
        mixed_rows = jnp.einsum(
            "hqk,khd->hqd", probs_low, value_rows, preferred_element_type=jnp.float32
        )
        mixed_low = (
            mixed_rows.reshape(KV_HEADS, group_size, tokens, HD)
            .transpose(2, 0, 1, 3)
            .reshape(tokens, width_q)
            .astype(jnp.bfloat16)
        )
        middle = start + jnp.dot(mixed_low, weight_o, preferred_element_type=jnp.float32)
        normed_two, inverse_two = norm_forward(middle, gain_pair[1])
        outgoing = (normed_two.astype(jnp.bfloat16)[anchor] * filled[:, None]).reshape(
            experts, capacity, D
        )
        incoming = lax.all_to_all(outgoing, "expert", split_axis=0, concat_axis=1, tiled=True)
        gate_up = jnp.einsum(
            "erd,edf->erf", incoming, weight_in, preferred_element_type=jnp.float32
        )
        hidden_low = (jax.nn.silu(gate_up[..., :FF]) * gate_up[..., FF:]).astype(jnp.bfloat16)
        produced = jnp.einsum(
            "erf,efd->erd", hidden_low, weight_down, preferred_element_type=jnp.float32
        ).astype(jnp.bfloat16)
        returned = lax.all_to_all(produced, "expert", split_axis=1, concat_axis=0, tiled=True)
        picked = (
            returned.reshape(experts * capacity, D)[slot_place]
            .astype(jnp.float32)
            .reshape(tokens, TOPK, D)
        )
        result = middle + jnp.sum(picked * forward_gates_now[:, :, None], axis=1)
        saved = (
            start,
            inverse_one,
            normed_low,
            forward_queries_low,
            forward_all_kv,
            row_max,
            row_sum,
            mixed_low,
            middle,
            inverse_two,
            incoming,
            gate_up,
            hidden_low,
        )
        result, saved = (result, saved)
        forward_saved.append(saved)
        forward_results.append(result)
        if step_index < MICRO:
            received = passed_along(result.astype(jnp.bfloat16), "section", 1).astype(jnp.float32)
    pending = jnp.zeros((tokens, D), jnp.float32)
    grads_input = []
    layer_total = None
    expert_total = None
    for step_index in range(MICRO + 1):
        micro_raw = step_index - 1 + section_index
        micro_index = jnp.clip(micro_raw, 0, MICRO - 1)
        valid_flag = ((micro_raw >= 0) & (micro_raw < MICRO)).astype(jnp.float32)
        earlier = forward_saved[max(step_index - 1, 0)]
        later = forward_saved[min(step_index + 1, MICRO)]
        saved = jax.tree.map(
            lambda earlier_part, later_part: jnp.where(first_section, earlier_part, later_part),
            earlier,
            later,
        )
        seed_grad = cotangent[min(step_index, MICRO - 1)].astype(jnp.float32)
        grad_out = jnp.where(first_section, pending, seed_grad)
        (
            backward_hidden,
            backward_inverse_one,
            backward_normed_low,
            backward_queries_low,
            backward_all_kv,
            backward_row_max,
            backward_row_sum,
            backward_mixed_low,
            backward_middle,
            backward_inverse_two,
            backward_incoming,
            backward_gate_up,
            backward_hidden_low,
        ) = saved
        backward_allowed = allowed_of(micro_index)
        (
            backward_slot_place,
            backward_anchor,
            backward_filled,
            backward_slot_gate,
        ), backward_gates_now = micro_data(micro_index)
        slot_grad = (
            (grad_out[backward_anchor] * backward_slot_gate[:, None])
            .astype(jnp.bfloat16)
            .reshape(experts, capacity, D)
        )
        grad_incoming = lax.all_to_all(slot_grad, "expert", split_axis=0, concat_axis=1, tiled=True)
        grad_hidden = jnp.einsum(
            "erd,efd->erf", grad_incoming, weight_down, preferred_element_type=jnp.float32
        )
        down_term = jnp.einsum(
            "erf,erd->efd", backward_hidden_low, grad_incoming, preferred_element_type=jnp.float32
        )
        gate_part = backward_gate_up[..., :FF]
        up_part = backward_gate_up[..., FF:]
        sigmoid_gate = jax.nn.sigmoid(gate_part)
        grad_gate = grad_hidden * up_part * sigmoid_gate * (1.0 + gate_part * (1.0 - sigmoid_gate))
        grad_up = grad_hidden * gate_part * sigmoid_gate
        grad_both = jnp.concatenate([grad_gate, grad_up], axis=-1).astype(jnp.bfloat16)
        in_term = jnp.einsum(
            "erd,erf->edf", backward_incoming, grad_both, preferred_element_type=jnp.float32
        )
        grad_rows = jnp.einsum(
            "erf,edf->erd", grad_both, weight_in, preferred_element_type=jnp.float32
        ).astype(jnp.bfloat16)
        grad_returned = lax.all_to_all(grad_rows, "expert", split_axis=1, concat_axis=0, tiled=True)
        grad_moe = (
            grad_returned.reshape(experts * capacity, D)[backward_slot_place]
            .astype(jnp.float32)
            .reshape(tokens, TOPK, D)
            .sum(axis=1)
        )
        grad_from_two, gain_two = norm_backward(
            backward_middle, backward_inverse_two, gain_pair[1], grad_moe
        )
        grad_middle = grad_out + grad_from_two
        grad_branch = grad_middle.astype(jnp.bfloat16)
        out_term = jnp.einsum(
            "tq,td->qd", backward_mixed_low, grad_branch, preferred_element_type=jnp.float32
        )
        grad_mixed = jnp.einsum(
            "td,qd->tq", grad_branch, weight_o, preferred_element_type=jnp.float32
        ).astype(jnp.bfloat16)
        grad_stacked = (
            grad_mixed.reshape(tokens, KV_HEADS, group_size, HD)
            .transpose(1, 2, 0, 3)
            .reshape(KV_HEADS, group_size * tokens, HD)
        )
        backward_stacked, backward_key_rows, backward_scores = score_rows(
            backward_queries_low, backward_all_kv, backward_allowed
        )
        backward_value_rows = backward_all_kv[:, width_kv:].reshape(length, KV_HEADS, HD)
        probs_full = jnp.exp(backward_scores - backward_row_max) / backward_row_sum
        backward_probs_low = probs_full.astype(jnp.bfloat16)
        grad_probs = jnp.einsum(
            "hqd,khd->hqk", grad_stacked, backward_value_rows, preferred_element_type=jnp.float32
        )
        row_inner = jnp.sum(grad_probs * probs_full, axis=-1, keepdims=True)
        grad_raw = (probs_full * (grad_probs - row_inner) * score_scale).astype(jnp.bfloat16)
        grad_queries = jnp.einsum(
            "hqk,khd->hqd", grad_raw, backward_key_rows, preferred_element_type=jnp.float32
        )
        grad_keys = jnp.einsum(
            "hqk,hqd->khd", grad_raw, backward_stacked, preferred_element_type=jnp.float32
        )
        grad_values = jnp.einsum(
            "hqk,hqd->khd", backward_probs_low, grad_stacked, preferred_element_type=jnp.float32
        )
        partial_kv = jnp.concatenate(
            [grad_keys.reshape(length, width_kv), grad_values.reshape(length, width_kv)], axis=1
        )
        grad_kv = lax.psum_scatter(
            partial_kv.astype(jnp.bfloat16), "shard", scatter_dimension=0, tiled=True
        ).astype(jnp.float32)
        grad_queries = (
            grad_queries.reshape(KV_HEADS, group_size, tokens, HD)
            .transpose(2, 0, 1, 3)
            .reshape(tokens, HEADS, HD)
        )
        grad_q_low = (
            rotate(grad_queries, cosine, -sine_table).reshape(tokens, width_q).astype(jnp.bfloat16)
        )
        grad_k = rotate(
            grad_kv[:, :width_kv].reshape(tokens, KV_HEADS, HD), cosine, -sine_table
        ).reshape(tokens, width_kv)
        grad_kv_low = jnp.concatenate([grad_k, grad_kv[:, width_kv:]], axis=1).astype(jnp.bfloat16)
        query_term = jnp.einsum(
            "td,tq->dq", backward_normed_low, grad_q_low, preferred_element_type=jnp.float32
        )
        kv_term = jnp.einsum(
            "td,tk->dk", backward_normed_low, grad_kv_low, preferred_element_type=jnp.float32
        )
        grad_normed = jnp.einsum(
            "tq,dq->td", grad_q_low, weight_q, preferred_element_type=jnp.float32
        )
        grad_normed = grad_normed + jnp.einsum(
            "tk,dk->td", grad_kv_low, weight_kv, preferred_element_type=jnp.float32
        )
        grad_from_one, gain_one = norm_backward(
            backward_hidden, backward_inverse_one, gain_pair[0], grad_normed
        )
        grad_input = grad_middle + grad_from_one
        grad_input, layer_terms, expert_terms = (
            grad_input,
            (query_term, kv_term, out_term, jnp.stack([gain_one, gain_two])),
            (in_term, down_term),
        )
        layer_terms = jax.tree.map(lambda term_part: term_part * valid_flag, layer_terms)
        expert_terms = jax.tree.map(lambda term_part: term_part * valid_flag, expert_terms)
        if layer_total is None:
            layer_total = layer_terms
            expert_total = expert_terms
        else:
            layer_total = jax.tree.map(jnp.add, layer_total, layer_terms)
            expert_total = jax.tree.map(jnp.add, expert_total, expert_terms)
        grads_input.append(grad_input)
        if step_index < MICRO:
            pending = passed_along(grad_input.astype(jnp.bfloat16), "section", -1).astype(
                jnp.float32
            )
    gate_up_grad, down_grad = (
        lax.psum_scatter(
            expert_total[0][None].astype(jnp.bfloat16), "shard", scatter_dimension=2, tiled=True
        ).astype(jnp.float32),
        lax.psum_scatter(
            expert_total[1][None].astype(jnp.bfloat16), "shard", scatter_dimension=2, tiled=True
        ).astype(jnp.float32),
    )
    query_grad, key_value_grad, output_weight_grad, gain_grad = (
        lax.psum_scatter(
            layer_total[0][None], ("expert", "shard"), scatter_dimension=1, tiled=True
        ),
        lax.psum_scatter(
            layer_total[1][None], ("expert", "shard"), scatter_dimension=1, tiled=True
        ),
        lax.psum_scatter(
            layer_total[2][None], ("expert", "shard"), scatter_dimension=1, tiled=True
        ),
        lax.psum_scatter(
            layer_total[3][None], ("expert", "shard"), scatter_dimension=2, tiled=True
        ),
    )
    half_micro = MICRO // 2
    outputs_all = jnp.stack(forward_results[1:])
    grads_all = jnp.stack(grads_input[1:])
    payload = jnp.where(first_section, grads_all[half_micro:], outputs_all[:half_micro])
    arrived = from_partner(payload.astype(jnp.bfloat16), "section", 0).astype(payload.dtype)
    output = jnp.where(first_section, arrived, outputs_all[half_micro:])
    input_grad = jnp.where(first_section, grads_all[:half_micro], arrived)
    return (
        output,
        input_grad,
        query_grad,
        key_value_grad,
        output_weight_grad,
        gain_grad,
        gate_up_grad,
        down_grad,
    )


def solution(mesh):
    placed = (
        P(None, ("expert", "shard"), None),
        P(None, "expert", None),
        P(None, ("expert", "shard"), None),
        P(None, ("expert", "shard"), None),
        P("section", ("expert", "shard"), None),
        P("section", ("expert", "shard"), None),
        P("section", ("expert", "shard"), None),
        P("section", None, ("expert", "shard")),
        P("section", "expert", "shard", None),
        P("section", "expert", "shard", None),
        P(None, ("expert", "shard"), None),
    )
    return jax.shard_map(
        shards,
        mesh=mesh,
        in_specs=placed,
        out_specs=(
            P("section", ("expert", "shard"), None),
            P("section", ("expert", "shard"), None),
            P("section", ("expert", "shard"), None),
            P("section", ("expert", "shard"), None),
            P("section", ("expert", "shard"), None),
            P("section", None, ("expert", "shard")),
            P("section", "expert", "shard", None),
            P("section", "expert", "shard", None),
        ),
        check_vma=False,
    )
```

profile of v0, /device:TPU:0, one launch (start us, length us, event | category | flops | bytes accessed | tf_op | source)
XLA Modules:
  0.0 2615.7 jit_solution(3814132537158881257)
XLA Ops:
  24.9 25.7 all_gather.33
  67.0 25.1 slice_reduce_fusion
  94.7 8.7 all_gather.36
  104.3 9.5 all-gather.6.cloned.1.call-done
  128.9 39.7 %all-gather.10.cloned.1.call-done = bf16[1,1536,1536]{2,1,0:T(8,128)(2,1)} async-done(((bf16[1,96,1536]{2,1,0:T(8,128)(2,1)}), bf16[1,1536,1536]{2,1,0:T(8,128)(2,1)}) %all-gather.10.cloned.1.call-update) | async-done | bytes 4718608 | tf_op jit(solution)/shard_map/all_gather | solution.py:102
  178.5 48.7 %all_to_all.330 = bf16[16,40,1536]{2,1,0:T(8,128)(2,1)S(1)} all-to-all(bf16[16,40,1536]{2,1,0:T(8,128)(2,1)S(1)} %broadcast_multiply_fusion.4), channel_id=1, replica_groups=mesh['section'=2,'expert'=4,'shard'=4] {'expert'}, dimensions={0} | all-to-all | bytes 3932160 | tf_op jit(solution)/shard_map/all_to_all | solution.py:196
  227.4 61.1 %all-gather.12.cloned.1.call-done = bf16[1,4,1536,1536]{3,2,1,0:T(8,128)(2,1)} async-done(((bf16[1,4,384,1536]{3,2,1,0:T(8,128)(2,1)}), bf16[1,4,1536,1536]{3,2,1,0:T(8,128)(2,1)}) %all-gather.12.cloned.1.call-update) | async-done | bytes 18874384 | tf_op jit(solution)/shard_map/all_gather | solution.py:110
  288.5 8.1 fusion.29
  300.2 54.0 %all-gather.14.cloned.1.call-done = bf16[1,4,768,1536]{3,2,1,0:T(8,128)(2,1)} async-done(((bf16[1,4,192,1536]{3,2,1,0:T(8,128)(2,1)}), bf16[1,4,768,1536]{3,2,1,0:T(8,128)(2,1)}) %all-gather.14.cloned.1.call-update) | async-done | bytes 9437200 | tf_op jit(solution)/shard_map/all_gather | solution.py:111
  471.1 51.1 %all_to_all.331 = bf16[16,40,1536]{2,1,0:T(8,128)(2,1)S(1)} all-to-all(bf16[16,40,1536]{2,1,0:T(8,128)(2,1)S(1)} %broadcast_multiply_fusion.3), channel_id=1, replica_groups=mesh['section'=2,'expert'=4,'shard'=4] {'expert'}, dimensions={0} | all-to-all | bytes 3932160 | tf_op jit(solution)/shard_map/all_to_all | solution.py:196
  522.3 8.9 fusion.27
  576.8 8.4 all-to-all-done.5
  620.5 7.0 all_gather.41
  662.3 32.2 %all-to-all-done.7 = bf16[16,40,1536]{2,1,0:T(8,128)(2,1)} async-done(((bf16[16,40,1536]{2,1,0:T(8,128)(2,1)}), bf16[16,40,1536]{2,1,0:T(8,128)(2,1)}, u32[]{:S(2)}, u32[]{:S(2)}) %all-to-all-start.7) | async-done | bytes 1966112 | tf_op jit(solution)/shard_map/all_to_all | solution.py:196
  701.6 15.3 broadcast_select_fusion.3
  728.3 16.1 all-to-all-done.2
  751.9 7.2 fusion.229
  759.1 11.1 fusion.111
  773.1 21.0 all-to-all-done.9
  822.7 20.8 all-to-all-done.4
  885.8 6.8 fusion.185
  937.7 46.8 %all_to_all.332 = bf16[16,40,1536]{2,1,0:T(8,128)(2,1)S(1)} all-to-all(bf16[16,40,1536]{2,1,0:T(8,128)(2,1)S(1)} %multiply_convert_fusion.3), channel_id=1, replica_groups=mesh['section'=2,'expert'=4,'shard'=4] {'expert'}, dimensions={0} | all-to-all | bytes 3932160 | tf_op jit(solution)/shard_map/all_to_all | solution.py:275
  984.7 7.9 fusion.225
  992.6 11.1 fusion.114
  1023.6 30.9 %all-to-all-done.8 = bf16[4,160,1536]{2,0,1:T(4,128)(2,1)S(1)} async-done(((bf16[4,160,1536]{2,0,1:T(4,128)(2,1)}), bf16[4,160,1536]{2,0,1:T(4,128)(2,1)S(1)}, u32[]{:S(2)}, u32[]{:S(2)}) %all-to-all-start.8) | async-done | bytes 1966112 | tf_op jit(solution)/shard_map/all_to_all | solution.py:294
  1097.8 9.2 reduce-scatter.36.cloned.1.call-done
  1110.2 6.8 all_gather.42
  1130.9 50.9 %all_to_all.333 = bf16[16,40,1536]{2,1,0:T(8,128)(2,1)S(1)} all-to-all(bf16[16,40,1536]{2,1,0:T(8,128)(2,1)S(1)} %broadcast_multiply_fusion.1), channel_id=1, replica_groups=mesh['section'=2,'expert'=4,'shard'=4] {'expert'}, dimensions={0} | all-to-all | bytes 3932160 | tf_op jit(solution)/shard_map/all_to_all | solution.py:196
  1182.0 8.8 fusion.19
  1247.1 6.8 fusion.191
  1296.7 6.8 all_gather.43
  1347.5 24.2 all-to-all-done.15
  1378.3 19.8 broadcast_select_fusion
  1398.1 23.6 all-to-all-done.10
  1424.4 7.2 fusion.221
  1431.6 11.1 fusion.117
  1461.5 33.7 %all-to-all-done.12 = bf16[4,160,1536]{2,0,1:T(4,128)(2,1)} async-done(((bf16[4,160,1536]{2,0,1:T(4,128)(2,1)}), bf16[4,160,1536]{2,0,1:T(4,128)(2,1)}, u32[]{:S(2)}, u32[]{:S(2)}) %all-to-all-start.12) | async-done | bytes 1966112 | tf_op jit(solution)/shard_map/all_to_all | solution.py:294
  1537.8 7.3 reduce-scatter.38.cloned.1.call-done
  1582.2 49.2 %all_to_all.334 = bf16[16,40,1536]{2,1,0:T(8,128)(2,1)S(1)} all-to-all(bf16[16,40,1536]{2,1,0:T(8,128)(2,1)S(1)} %multiply_convert_fusion.1), channel_id=1, replica_groups=mesh['section'=2,'expert'=4,'shard'=4] {'expert'}, dimensions={0} | all-to-all | bytes 3932160 | tf_op jit(solution)/shard_map/all_to_all | solution.py:275
  1631.6 7.9 fusion.217
  1639.5 11.1 fusion.120
  1664.6 36.8 %all-to-all-done.16 = bf16[4,160,1536]{2,0,1:T(4,128)(2,1)S(1)} async-done(((bf16[4,160,1536]{2,0,1:T(4,128)(2,1)}), bf16[4,160,1536]{2,0,1:T(4,128)(2,1)S(1)}, u32[]{:S(2)}, u32[]{:S(2)}) %all-to-all-start.16) | async-done | bytes 1966112 | tf_op jit(solution)/shard_map/all_to_all | solution.py:294
  1746.6 6.7 reduce-scatter.40.cloned.1.call-done
  1806.7 33.4 %all-to-all-done.17 = bf16[16,40,1536]{2,1,0:T(8,128)(2,1)} async-done(((bf16[16,40,1536]{2,1,0:T(8,128)(2,1)}), bf16[16,40,1536]{2,1,0:T(8,128)(2,1)}, u32[]{:S(2)}, u32[]{:S(2)}) %all-to-all-start.17) | async-done | bytes 1966112 | tf_op jit(solution)/shard_map/all_to_all | solution.py:275
  1848.2 8.8 fusion.214
  1857.0 10.8 fusion.123
  1870.7 18.8 all-to-all-done.19
  1894.0 9.8 fusion.334
  1905.0 7.8 fusion.332
  1917.5 7.9 fusion.330
  1976.2 9.7 fusion.328
  2009.4 30.8 %fusion.58 = bf16[1,4,768,1536]{3,2,1,0:T(8,128)(2,1)} fusion(f32[]{:T(128)S(6)} %convert_element_type.856, f32[4,768,1536]{2,1,0:T(8,128)} %fusion.328, f32[]{:T(128)S(6)} %convert_element_type.855, f32[4,768,1536]{2,1,0:T(8,128)} %fusion.330, f32[]{:T(128)S(6)} %convert_element_type.854, f32[4,768,1536]{2,1,0:T(8,128)} %fusion.332, ...), kind=kOutput, calls=%fused_computation.114 | convolution fusion | flops 1557626880 | bytes 88866840 | tf_op jit(solution)/shard_map/erf,erd->efd/dot_general | solution.py:279
  2041.8 16.2 convolution_multiply_fusion.4
  2058.0 29.5 %fusion.8 = f32[4,1536,1536]{2,1,0:T(8,128)} fusion(f32[4,1536,1536]{2,1,0:T(8,128)} %convolution_multiply_fusion.4, f32[]{:T(128)S(6)} %convert_element_type.853, bf16[4,160,1536]{2,1,0:T(8,128)(2,1)S(1)} %bitcast.1090, bf16[4,160,1536]{2,1,0:T(8,128)(2,1)} %bitcast.1101, pred[]{:T(512)S(6)} %eq.463, bf16[4,160,768]{2,1,0:T(8,128)(2,1)} %copy-done.198, ...), kind=kOutput, calls=%fused_computation.52 | convolution fusion | flops 3043688448 | bytes 81395720 | tf_op jit(solution)/shard_map/erd,erf->edf/dot_general | solution.py:288
  2087.5 29.4 %fusion.7 = f32[4,1536,1536]{2,1,0:T(8,128)} fusion(f32[4,1536,1536]{2,1,0:T(8,128)} %fusion.8, f32[]{:T(128)S(6)} %convert_element_type.854, bf16[4,160,1536]{2,1,0:T(8,128)(2,1)} %bitcast.1093, bf16[4,160,1536]{2,1,0:T(8,128)(2,1)} %bitcast.1095, pred[]{:T(512)S(6)} %eq.463, bf16[4,160,768]{2,1,0:T(8,128)(2,1)} %copy-done.200, ...), kind=kOutput, calls=%fused_computation.50 | convolution fusion | flops 3043688448 | bytes 81395720 | tf_op jit(solution)/shard_map/erd,erf->edf/dot_general | solution.py:288
  2116.9 28.9 %fusion.6 = f32[4,1536,1536]{2,1,0:T(8,128)} fusion(f32[4,1536,1536]{2,1,0:T(8,128)} %fusion.7, f32[]{:T(128)S(6)} %convert_element_type.855, bf16[4,160,1536]{2,1,0:T(8,128)(2,1)} %bitcast.1102, bf16[4,160,1536]{2,1,0:T(8,128)(2,1)} %bitcast.1098, pred[]{:T(512)S(6)} %eq.463, bf16[4,160,768]{2,1,0:T(8,128)(2,1)} %copy-done.202, ...), kind=kOutput, calls=%fused_computation.48 | convolution fusion | flops 3043688448 | bytes 81395720 | tf_op jit(solution)/shard_map/erd,erf->edf/dot_general | solution.py:288
  2145.8 21.6 fusion.10
  2177.7 7.1 fusion.32
  2226.8 16.7 collective-permute-done.8
  2251.5 55.2 %reduce-scatter.30.cloned.1.call-done = bf16[1,4,384,1536]{3,2,1,0:T(8,128)(2,1)} async-done(((bf16[1,4,1536,1536]{3,2,1,0:T(8,128)(2,1)}), bf16[1,4,384,1536]{3,2,1,0:T(8,128)(2,1)}) %reduce-scatter.30.cloned.1.call-update) | async-done | bytes 4718608 | tf_op jit(solution)/shard_map/reduce_scatter | solution.py:390
  2306.7 7.4 convert_element_type.859
  2314.1 63.6 %reduce-scatter.26.cloned.1.call-done = f32[1,96,512]{2,1,0:T(8,128)} async-done(((f32[1,1536,512]{2,1,0:T(8,128)}), f32[1,96,512]{2,1,0:T(8,128)}) %reduce-scatter.26.cloned.1.call-update) | async-done | bytes 196624 | tf_op jit(solution)/shard_map/reduce_scatter | solution.py:401
  2377.6 115.4 %reduce-scatter.24.cloned.1.call-done = f32[1,96,1536]{2,1,0:T(8,128)} async-done(((f32[1,1536,1536]{2,1,0:T(8,128)}), f32[1,96,1536]{2,1,0:T(8,128)}) %reduce-scatter.24.cloned.1.call-update) | async-done | bytes 589840 | tf_op jit(solution)/shard_map/reduce_scatter | solution.py:398
  2493.1 115.7 %reduce-scatter.28.cloned.1.call-done = f32[1,96,1536]{2,1,0:T(8,128)} async-done(((f32[1,1536,1536]{2,1,0:T(8,128)}), f32[1,96,1536]{2,1,0:T(8,128)}) %reduce-scatter.28.cloned.1.call-update) | async-done | bytes 589840 | tf_op jit(solution)/shard_map/reduce_scatter | solution.py:404
  (1470 shorter events, 1039.7 us)
Async XLA Ops:
  7.2 85.0 %all-gather.8.cloned.1.call-start = ((), (), s32[]{:S(2)}) async-start(), calls=%async_computation.32 | async-start | bytes 1671168 | tf_op jit(solution)/shard_map/all_gather | solution.py:99
  8.8 105.0 %all-gather.6.cloned.1.call-start = ((), (), s32[]{:S(2)}) async-start(), calls=%async_computation.31 | async-start | bytes 5013504 | tf_op jit(solution)/shard_map/all_gather | solution.py:98
  10.7 158.0 %all-gather.10.cloned.1.call-start = ((), (), s32[]{:S(2)}) async-start(), calls=%async_computation.33 | async-start | bytes 5013504 | tf_op jit(solution)/shard_map/all_gather | solution.py:102
  12.6 275.9 %all-gather.12.cloned.1.call-start = ((), (), s32[]{:S(2)}) async-start(), calls=%async_computation.34 | async-start | bytes 23592960 | tf_op jit(solution)/shard_map/all_gather | solution.py:110
  19.1 335.0 %all-gather.14.cloned.1.call-start = ((), (), s32[]{:S(2)}) async-start(), calls=%async_computation.35 | async-start | bytes 11796480 | tf_op jit(solution)/shard_map/all_gather | solution.py:111
  23.2 41.1 %copy-start.254 = (s32[4,1,512]{2,1,0:T(1,128)S(1)}, s32[4,1,512]{2,1,0:T(1,128)}, u32[]{:S(2)}) copy-start(s32[4,1,512]{2,1,0:T(1,128)} %param.12) | copy-start | bytes 24580
  23.2 42.4 %copy-start.2 = (bf16[4,128,1536]{2,1,0:T(8,128)(2,1)S(1)}, bf16[4,128,1536]{2,1,0:T(8,128)(2,1)}, u32[]{:S(2)}) copy-start(bf16[4,128,1536]{2,1,0:T(8,128)(2,1)} %param.11) | copy-start | bytes 4718596
  52.3 72.1 %copy-start.111 = (f32[128,64]{0,1:T(8,128)}, f32[128,64]{0,1:T(8,128)S(1)}, u32[]{:S(2)}) copy-start(f32[128,64]{0,1:T(8,128)S(1)} %get-tuple-element.252) | copy-start | bytes 98308
  52.3 72.1 %copy-start.172 = (f32[128,64]{0,1:T(8,128)}, f32[128,64]{0,1:T(8,128)S(1)}, u32[]{:S(2)}) copy-start(f32[128,64]{0,1:T(8,128)S(1)} %get-tuple-element.251) | copy-start | bytes 98308
  52.4 41.8 %copy-start.160 = (f32[128,64]{1,0:T(8,128)}, f32[128,64]{1,0:T(8,128)S(1)}, u32[]{:S(2)}) copy-start(f32[128,64]{1,0:T(8,128)S(1)} %copy.691) | copy-start | bytes 98308
  52.5 41.7 %copy-start.105 = (f32[128,64]{1,0:T(8,128)}, f32[128,64]{1,0:T(8,128)S(1)}, u32[]{:S(2)}) copy-start(f32[128,64]{1,0:T(8,128)S(1)} %copy.690) | copy-start | bytes 98308
  55.8 38.3 %copy-start.368 = (s32[512]{0:T(512)}, s32[512]{0:T(512)S(1)}, u32[]{:S(2)}) copy-start(s32[512]{0:T(512)S(1)} %add_select_fusion) | copy-start | bytes 6148
  56.6 37.5 %copy-start.330 = (s32[512,1]{0,1:T(1,128)}, s32[512,1]{0,1:T(1,128)S(1)}, u32[]{:S(2)}) copy-start(s32[512,1]{0,1:T(1,128)S(1)} %get-tuple-element.304) | copy-start | bytes 6148
  59.1 35.0 %copy-start.374 = (bf16[512]{0:T(512)(128)(2,1)}, bf16[512]{0:T(512)(128)(2,1)S(1)}, u32[]{:S(2)}) copy-start(bf16[512]{0:T(512)(128)(2,1)S(1)} %broadcast.1248) | copy-start | bytes 3076
  128.7 40.0 %copy-start.213 = (bf16[2,768,128]{2,1,0:T(8,128)(2,1)}, bf16[2,768,128]{2,1,0:T(8,128)(2,1)S(1)}, u32[]{:S(2)}) copy-start(bf16[2,768,128]{2,1,0:T(8,128)(2,1)S(1)} %fusion.296) | copy-start | bytes 1179652
  227.4 69.2 %copy-start.17 = (bf16[4,4,40,1536]{3,2,1,0:T(8,128)(2,1)}, bf16[4,4,40,1536]{3,2,1,0:T(8,128)(2,1)S(1)}, u32[]{:S(2)}) copy-start(bf16[4,4,40,1536]{3,2,1,0:T(8,128)(2,1)S(1)} %copy.700) | copy-start | bytes 5898244
  362.7 51.1 %all-to-all-start.1 = ((bf16[4,160,1536]{2,0,1:T(4,128)(2,1)}), bf16[4,160,1536]{2,0,1:T(4,128)(2,1)S(1)}, u32[]{:S(2)}, u32[]{:S(2)}) async-start(bf16[4,160,1536]{2,0,1:T(4,128)(2,1)} %copy.701), calls=%async_computation.1 | async-start | bytes 3932160 | tf_op jit(solution)/shard_map/all_to_all | solution.py:204
  428.7 12.1 collective-permute-start
  536.5 48.6 %all-to-all-start.5 = ((bf16[4,160,1536]{2,0,1:T(4,128)(2,1)}), bf16[4,160,1536]{2,0,1:T(4,128)(2,1)S(1)}, u32[]{:S(2)}, u32[]{:S(2)}) async-start(bf16[4,160,1536]{2,0,1:T(4,128)(2,1)} %copy.739), calls=%async_computation.5 | async-start | bytes 3932160 | tf_op jit(solution)/shard_map/all_to_all | solution.py:204
  600.9 12.6 collective-permute-start.2
  627.5 180.8 %copy-start.85 = (bf16[512,512]{1,0:T(8,128)(2,1)}, bf16[512,512]{1,0:T(8,128)(2,1)S(1)}, u32[]{:S(2)}) copy-start(bf16[512,512]{1,0:T(8,128)(2,1)S(1)} %all_gather.41) | copy-start | bytes 1572868
  643.6 50.9 %all-to-all-start.7 = ((bf16[16,40,1536]{2,1,0:T(8,128)(2,1)}), bf16[16,40,1536]{2,1,0:T(8,128)(2,1)}, u32[]{:S(2)}, u32[]{:S(2)}) async-start(bf16[16,40,1536]{2,1,0:T(8,128)(2,1)} %broadcast_multiply_fusion.2), calls=%async_computation.7 | async-start | bytes 3932160 | tf_op jit(solution)/shard_map/all_to_all | solution.py:196
  694.5 49.9 %all-to-all-start.2 = ((bf16[16,40,1536]{2,1,0:T(8,128)(2,1)}), bf16[16,40,1536]{2,1,0:T(8,128)(2,1)}, u32[]{:S(2)}, u32[]{:S(2)}) async-start(bf16[16,40,1536]{2,1,0:T(8,128)(2,1)} %multiply_convert_fusion.4), calls=%async_computation.2 | async-start | bytes 3932160 | tf_op jit(solution)/shard_map/all_to_all | solution.py:275
  744.4 49.8 %all-to-all-start.9 = ((bf16[4,160,1536]{2,0,1:T(4,128)(2,1)}), bf16[4,160,1536]{2,0,1:T(4,128)(2,1)}, u32[]{:S(2)}, u32[]{:S(2)}) async-start(bf16[4,160,1536]{2,0,1:T(4,128)(2,1)} %copy.776), calls=%async_computation.9 | async-start | bytes 3932160 | tf_op jit(solution)/shard_map/all_to_all | solution.py:204
  773.1 34.6 %copy-start.256 = (f32[2,768]{1,0:T(2,128)S(1)}, f32[2,768]{1,0:T(2,128)}, u32[]{:S(2)}) copy-start(f32[2,768]{1,0:T(2,128)} %copy-done.255) | copy-start | bytes 18436
  773.1 35.2 %copy-start.83 = (bf16[512,512]{1,0:T(8,128)(2,1)S(1)}, bf16[512,512]{1,0:T(8,128)(2,1)}, u32[]{:S(2)}) copy-start(bf16[512,512]{1,0:T(8,128)(2,1)} %copy-done.82) | copy-start | bytes 1572868
  773.1 35.2 %copy-start.121 = (bf16[512,512]{1,0:T(8,128)(2,1)S(1)}, bf16[512,512]{1,0:T(8,128)(2,1)}, u32[]{:S(2)}) copy-start(bf16[512,512]{1,0:T(8,128)(2,1)} %copy-done.120) | copy-start | bytes 1572868
  794.1 49.4 %all-to-all-start.4 = ((bf16[4,160,1536]{2,0,1:T(4,128)(2,1)}), bf16[4,160,1536]{2,0,1:T(4,128)(2,1)}, u32[]{:S(2)}, u32[]{:S(2)}) async-start(bf16[4,160,1536]{2,0,1:T(4,128)(2,1)} %copy.720), calls=%async_computation.4 | async-start | bytes 3932160 | tf_op jit(solution)/shard_map/all_to_all | solution.py:294
  798.6 101.5 %reduce-scatter.34.cloned.1.call-start = ((), (), s32[]{:S(2)}) async-start(), calls=%async_computation.41 | async-start | bytes 655360
  881.5 31.4 %collective-permute-start.4 = (bf16[128,1536]{1,0:T(8,128)(2,1)}, bf16[128,1536]{1,0:T(8,128)(2,1)}, u32[]{:S(2)}, u32[]{:S(2)}) collective-permute-start(bf16[128,1536]{1,0:T(8,128)(2,1)} %add_convert_fusion.9), channel_id=1, source_target_pairs={{0,16},{1,17},{2,18},{3,19},{4,20},{5,21},{6,22},{7,23},{8,24},{9,... | collective-permute-start | bytes 1179656 | tf_op jit(solution)/shard_map/ppermute | solution.py:23
  918.6 11.7 collective-permute-start.1
  937.7 47.0 %copy-start.129 = (f32[4,160,1536]{2,1,0:T(8,128)S(1)}, f32[4,160,1536]{2,1,0:T(8,128)}, u32[]{:S(2)}) copy-start(f32[4,160,1536]{2,1,0:T(8,128)} %get-tuple-element.76) | copy-start | bytes 11796484
  1006.5 48.0 %all-to-all-start.8 = ((bf16[4,160,1536]{2,0,1:T(4,128)(2,1)}), bf16[4,160,1536]{2,0,1:T(4,128)(2,1)S(1)}, u32[]{:S(2)}, u32[]{:S(2)}) async-start(bf16[4,160,1536]{2,0,1:T(4,128)(2,1)} %copy.758), calls=%async_computation.8 | async-start | bytes 3932160 | tf_op jit(solution)/shard_map/all_to_all | solution.py:294
  1010.3 96.8 %reduce-scatter.36.cloned.1.call-start = ((), (), s32[]{:S(2)}) async-start(), calls=%async_computation.42 | async-start | bytes 655360
  1130.9 60.6 %slice-start.3 = ((s8[9437184]{0:T(1024)(128)(4,1)}), s8[4194304]{0:T(1024)(128)(4,1)S(1)}, s32[]{:S(2)}) async-start(s8[9437184]{0:T(1024)(128)(4,1)} %bitcast.1068), calls=%async_computation.50 | async-start | bytes 8388608
  1196.1 62.1 %all-to-all-start.13 = ((bf16[4,160,1536]{2,0,1:T(4,128)(2,1)}), bf16[4,160,1536]{2,0,1:T(4,128)(2,1)S(1)}, u32[]{:S(2)}, u32[]{:S(2)}) async-start(bf16[4,160,1536]{2,0,1:T(4,128)(2,1)} %copy.813), calls=%async_computation.13 | async-start | bytes 3932160 | tf_op jit(solution)/shard_map/all_to_all | solution.py:204
  1274.1 14.1 collective-permute-start.6
  1320.8 50.9 %all-to-all-start.15 = ((bf16[16,40,1536]{2,1,0:T(8,128)(2,1)}), bf16[16,40,1536]{2,1,0:T(8,128)(2,1)S(1)}, u32[]{:S(2)}, u32[]{:S(2)}) async-start(bf16[16,40,1536]{2,1,0:T(8,128)(2,1)} %broadcast_multiply_fusion), calls=%async_computation.15 | async-start | bytes 3932160 | tf_op jit(solution)/shard_map/all_to_all | solution.py:196
  1325.8 13.0 collective-permute-start.3
  1371.7 49.9 %all-to-all-start.10 = ((bf16[16,40,1536]{2,1,0:T(8,128)(2,1)}), bf16[16,40,1536]{2,1,0:T(8,128)(2,1)}, u32[]{:S(2)}, u32[]{:S(2)}) async-start(bf16[16,40,1536]{2,1,0:T(8,128)(2,1)} %multiply_convert_fusion.2), calls=%async_computation.10 | async-start | bytes 3932160 | tf_op jit(solution)/shard_map/all_to_all | solution.py:275
  1445.7 49.5 %all-to-all-start.12 = ((bf16[4,160,1536]{2,0,1:T(4,128)(2,1)}), bf16[4,160,1536]{2,0,1:T(4,128)(2,1)}, u32[]{:S(2)}, u32[]{:S(2)}) async-start(bf16[4,160,1536]{2,0,1:T(4,128)(2,1)} %copy.795), calls=%async_computation.12 | async-start | bytes 3932160 | tf_op jit(solution)/shard_map/all_to_all | solution.py:294
  1450.2 94.9 %reduce-scatter.38.cloned.1.call-start = ((), (), s32[]{:S(2)}) async-start(), calls=%async_computation.43 | async-start | bytes 655360
  1461.5 35.6 %copy-start.310 = (s32[1024]{0:T(1024)S(1)}, s32[1024]{0:T(1024)}, u32[]{:S(2)}) copy-start(s32[1024]{0:T(1024)} %pad_clamp_fusion.7) | copy-start | bytes 12292
  1510.5 50.3 %copy-start.73 = (f32[128,1536]{1,0:T(8,128)}, f32[128,1536]{1,0:T(8,128)S(1)}, u32[]{:S(2)}) copy-start(f32[128,1536]{1,0:T(8,128)S(1)} %subtract_add_fusion.4) | copy-start | bytes 2359300
  1562.0 12.7 collective-permute-start.5
  1582.2 49.4 %copy-start.127 = (f32[4,160,1536]{2,1,0:T(8,128)S(1)}, f32[4,160,1536]{2,1,0:T(8,128)}, u32[]{:S(2)}) copy-start(f32[4,160,1536]{2,1,0:T(8,128)} %get-tuple-element.74) | copy-start | bytes 11796484
  1653.4 48.0 %all-to-all-start.16 = ((bf16[4,160,1536]{2,0,1:T(4,128)(2,1)}), bf16[4,160,1536]{2,0,1:T(4,128)(2,1)S(1)}, u32[]{:S(2)}, u32[]{:S(2)}) async-start(bf16[4,160,1536]{2,0,1:T(4,128)(2,1)} %copy.832), calls=%async_computation.16 | async-start | bytes 3932160 | tf_op jit(solution)/shard_map/all_to_all | solution.py:294
  1657.0 96.3 %reduce-scatter.40.cloned.1.call-start = ((), (), s32[]{:S(2)}) async-start(), calls=%async_computation.44 | async-start | bytes 655360
  1719.3 49.8 %copy-start.65 = (f32[128,1536]{1,0:T(8,128)}, f32[128,1536]{1,0:T(8,128)S(1)}, u32[]{:S(2)}) copy-start(f32[128,1536]{1,0:T(8,128)S(1)} %subtract_add_fusion.2) | copy-start | bytes 2359300
  1769.4 12.8 collective-permute-start.7
  1790.8 49.3 %all-to-all-start.17 = ((bf16[16,40,1536]{2,1,0:T(8,128)(2,1)}), bf16[16,40,1536]{2,1,0:T(8,128)(2,1)}, u32[]{:S(2)}, u32[]{:S(2)}) async-start(bf16[16,40,1536]{2,1,0:T(8,128)(2,1)} %multiply_convert_fusion), calls=%async_computation.17 | async-start | bytes 3932160 | tf_op jit(solution)/shard_map/all_to_all | solution.py:275
  1803.8 40.7 %copy-start.312 = (f32[128,4]{0,1:T(4,128)S(1)}, f32[128,4]{0,1:T(4,128)}, u32[]{:S(2)}) copy-start(f32[128,4]{0,1:T(4,128)} %get-tuple-element.183) | copy-start | bytes 6148
  1803.8 41.4 %copy-start.326 = (s32[512,1]{0,1:T(1,128)S(1)}, s32[512,1]{0,1:T(1,128)}, u32[]{:S(2)}) copy-start(s32[512,1]{0,1:T(1,128)} %get-tuple-element.295) | copy-start | bytes 6148
  1803.9 42.0 %copy-start.325 = (s32[512,1]{0,1:T(1,128)S(1)}, s32[512,1]{0,1:T(1,128)}, u32[]{:S(2)}) copy-start(s32[512,1]{0,1:T(1,128)} %get-tuple-element.296) | copy-start | bytes 6148
  1840.1 49.4 %all-to-all-start.19 = ((bf16[4,160,1536]{2,0,1:T(4,128)(2,1)}), bf16[4,160,1536]{2,0,1:T(4,128)(2,1)}, u32[]{:S(2)}, u32[]{:S(2)}) async-start(bf16[4,160,1536]{2,0,1:T(4,128)(2,1)} %copy.874), calls=%async_computation.19 | async-start | bytes 3932160 | tf_op jit(solution)/shard_map/all_to_all | solution.py:204
  1889.4 51.3 %all-to-all-start.18 = ((bf16[4,160,1536]{2,0,1:T(4,128)(2,1)}), bf16[4,160,1536]{2,0,1:T(4,128)(2,1)}, u32[]{:S(2)}, u32[]{:S(2)}) async-start(bf16[4,160,1536]{2,0,1:T(4,128)(2,1)} %copy.856), calls=%async_computation.18 | async-start | bytes 3932160 | tf_op jit(solution)/shard_map/all_to_all | solution.py:294
  1893.9 106.0 %reduce-scatter.42.cloned.1.call-start = ((), (), s32[]{:S(2)}) async-start(), calls=%async_computation.45 | async-start | bytes 655360
  1976.1 249.2 %reduce-scatter.44.cloned.1.call-start = ((), (), s32[]{:S(2)}) async-start(), calls=%async_computation.46 | async-start | bytes 835584
  2009.4 237.6 %reduce-scatter.32.cloned.1.call-start = ((), (), s32[]{:S(2)}) async-start(), calls=%async_computation.40 | async-start | bytes 11796480 | tf_op jit(solution)/shard_map/reduce_scatter | solution.py:393
  2040.2 266.5 %reduce-scatter.30.cloned.1.call-start = ((), (), s32[]{:S(2)}) async-start(), calls=%async_computation.39 | async-start | bytes 23592960 | tf_op jit(solution)/shard_map/reduce_scatter | solution.py:390
  2167.5 210.1 %reduce-scatter.26.cloned.1.call-start = ((), (), s32[]{:S(2)}) async-start(), calls=%async_computation.37 | async-start | bytes 3342336 | tf_op jit(solution)/shard_map/reduce_scatter | solution.py:401
  2173.8 319.3 %reduce-scatter.24.cloned.1.call-start = ((), (), s32[]{:S(2)}) async-start(), calls=%async_computation.36 | async-start | bytes 10027008 | tf_op jit(solution)/shard_map/reduce_scatter | solution.py:398
  2195.9 412.9 %reduce-scatter.28.cloned.1.call-start = ((), (), s32[]{:S(2)}) async-start(), calls=%async_computation.38 | async-start | bytes 10027008 | tf_op jit(solution)/shard_map/reduce_scatter | solution.py:404
  2224.2 19.2 collective-permute-start.8
  (360 other events, 2481.0 us)
Sparse Core Ops, SparseCore 0:
  10.9 42.8 all-gather.7
  56.6 57.2 all-gather.5
  116.7 51.9 all-gather.9
  170.7 117.7 all-gather.11
  289.9 64.2 all-gather.13
  876.5 19.9 reduce-scatter.33
  1087.8 19.2 reduce-scatter.35
  1525.7 19.4 reduce-scatter.37
  1734.4 18.8 reduce-scatter.39
  1976.2 21.1 reduce-scatter.41
  2009.5 56.0 reduce-scatter.43
  2068.1 77.4 reduce-scatter.31
  2167.6 139.0 reduce-scatter.29
  2311.4 66.1 reduce-scatter.25
  2382.7 110.2 reduce-scatter.23
  2497.6 111.1 reduce-scatter.27
where the time goes:
time: 2630 us; the launch traced here: 2620 us
  waiting for transfers between devices  874 us (33%)
  matrix products  610 us (23%)
  local copies, waits for them, and re-layouts  473 us (18%)
  blocking collectives  308 us (12%)
  other arithmetic  241 us (9%)
  starting transfers between devices  88.7 us (3%)
    all_to_all x3, blocking collectives, shards(): lax.all_to_all(outgoing, 'expert', split_axis=0, concat_axis=1, tiled=True)  151 us
    dot_general x5, matrix products, shards(): jnp.einsum('erd,erf->edf', backward_incoming, grad_both, preferred_elemen...  126 us
    all_to_all x5, waiting for transfers between devices, shards(): lax.all_to_all(grad_rows, 'expert', split_axis=1, concat_axis=0, tiled=True)  122 us
    reduce_scatter x1, waiting for transfers between devices, shards(): lax.psum_scatter(layer_total[2][None], ('expert', 'shard'), scatter_dimen...  116 us
    reduce_scatter x1, waiting for transfers between devices, shards(): lax.psum_scatter(layer_total[0][None], ('expert', 'shard'), scatter_dimen...  115 us
    all_to_all x2, blocking collectives, shards(): lax.all_to_all(slot_grad, 'expert', split_axis=0, concat_axis=1, tiled=True)  96 us
    unnamed x810, local copies, waits for them, and re-layouts  75.2 us
    all_to_all x3, waiting for transfers between devices, shards(): lax.all_to_all(slot_grad, 'expert', split_axis=0, concat_axis=1, tiled=True)  73.1 us
  transfers between devices with their start and end apart: 40, of which 28 were waited for; matrix products, arithmetic and copies ran while one was open for 32% of the time, Pallas kernels for 0%

commit v1 on v0

v1 whole, which is shorter than its diff:
```python
import functools

import jax
import jax.numpy as jnp
from jax import lax
from jax.experimental import pallas as pl
from jax.experimental.pallas import tpu as pltpu
from jax.sharding import PartitionSpec as P

D = 1536
HEADS = 12
KV_HEADS = 2
HD = 128
FF = 768
TOPK = 4
EXP_DEV = 4
MICRO = 4
GROUP = HEADS // KV_HEADS
WQ = HEADS * HD
WK = KV_HEADS * HD
SCALE = HD ** (-0.5)

epsilon = 1e-06
rope_base = 10000.0

MESH = pl.DeviceIdType.MESH
F32 = jnp.float32
BF16 = jnp.bfloat16
DMA = pltpu.SemaphoreType.DMA
VMEM_LIMIT = 60 * 2**20


class Plan:
    def __init__(self, mesh_shape, tokens):
        self.nx, self.nz, self.ns = mesh_shape
        self.tokens = tokens
        self.micro = MICRO // self.nx
        self.rows = self.micro * tokens
        self.ranks = self.nx * self.ns
        self.group = self.ranks // EXP_DEV
        self.halves = self.group // self.micro
        self.sources = self.ranks // self.halves
        self.experts = EXP_DEV * self.nz
        self.capacity = 5 * tokens * TOPK // (4 * self.experts)
        self.slots = -(-self.capacity // 16) * 16


def me():
    return lax.axis_index("section"), lax.axis_index("expert"), lax.axis_index("shard")


def remote(src, dst, send, recv, device):
    return pltpu.make_async_remote_copy(
        src_ref=src,
        dst_ref=dst,
        send_sem=send,
        recv_sem=recv,
        device_id=device,
        device_id_type=MESH,
    )


def greet_plane(plan, along=False):
    x, z, s = me()
    barrier = pltpu.get_barrier_semaphore()
    mine = x * plan.ns + s
    for step in range(1, plan.ranks):
        other = (mine + step) % plan.ranks
        pl.semaphore_signal(
            barrier, inc=1, device_id=(other // plan.ns, z, other % plan.ns), device_id_type=MESH
        )
    total = plan.ranks - 1
    if along:
        for step in range(1, plan.nz):
            pl.semaphore_signal(
                barrier, inc=1, device_id=(x, (z + step) % plan.nz, s), device_id_type=MESH
            )
        total += plan.nz - 1
    pl.semaphore_wait(barrier, total)


def nearest(place, index, count):
    left = place
    right = count - 1 - place
    short = jnp.minimum(left, right)
    odd = index % 2
    near = place + (1 - 2 * odd) * ((index + 1) // 2)
    far = jnp.where(left < right, index, count - 1 - index)
    return jnp.where(index <= 2 * short, near, far)


def moe_kernel(plan, backward, *refs):
    if backward:
        (rows_in, put, take, w_in, w_down, gate_up, out, sent_save, grad_save) = refs[:9]
        scratch = refs[9:]
    else:
        (rows_in, put, take, w_in, w_down, base, out, sent_save, gate_up, hidden) = refs[:10]
        scratch = refs[10:]
    (
        line,
        sbuf,
        xbuf,
        ybuf,
        rbuf,
        pbuf,
        qbuf,
        win_v,
        wdown_v,
        gbuf,
        zbuf,
        line_recv,
        line_right,
        line_left,
        to_send,
        to_recv,
        back_send,
        back_recv,
        sum_send,
        sum_recv,
        local_sem,
        save_sem,
    ) = scratch
    x, z, s = me()
    nz, ns = plan.nz, plan.ns
    rank = x * ns + s
    own_expert = rank // plan.group
    own_micro = (rank % plan.group) // plan.halves
    own_half = rank % plan.halves
    part = ns // plan.halves
    own_source = x * part + s // plan.halves
    slots = plan.slots
    tokens = plan.tokens
    many = plan.sources * slots

    load_in = pltpu.make_async_copy(w_in, win_v, local_sem.at[0])
    load_down = pltpu.make_async_copy(w_down, wdown_v, local_sem.at[1])
    load_in.start()
    load_down.start()
    greet_plane(plan, along=True)

    def along(block, step, own):
        src = rows_in if own else line.at[block]
        sem = line_right if step > 0 else line_left
        return remote(src, line.at[block], sem.at[block], line_recv.at[block], (x, z + step, s))

    def owner(expert, micro):
        rank_to = expert * plan.group + micro * plan.halves + s % plan.halves
        return rank_to // ns, rank_to % ns

    def dispatch_copy(block, expert, micro):
        to_x, to_s = owner(expert, micro)
        return remote(
            sbuf.at[block, micro, expert],
            xbuf.at[block, own_source],
            to_send.at[block, micro, expert],
            to_recv.at[block, own_source],
            (to_x, z, to_s),
        )

    def return_copy(block, source):
        to_x = source // part
        to_s = (source % part) * plan.halves + own_half
        return to_x, to_s, remote(
            ybuf.at[block, source],
            rbuf.at[block, own_micro, own_expert],
            back_send.at[block, source],
            back_recv.at[block, own_micro, own_expert],
            (to_x, z, to_s),
        )

    def sum_copy(block):
        return remote(
            pbuf.at[block], qbuf.at[z], sum_send.at[block], sum_recv.at[z], (x, block, s)
        )

    def wait_saved(slot):
        if backward:
            pltpu.make_async_copy(gbuf.at[slot], grad_save.at[0], save_sem.at[1, slot]).wait()
        else:
            pltpu.make_async_copy(gbuf.at[slot], gate_up.at[0], save_sem.at[1, slot]).wait()
            pltpu.make_async_copy(zbuf.at[slot], hidden.at[0], save_sem.at[2, slot]).wait()

    @pl.when(z + 1 < nz)
    def _():
        along(z, 1, True).start()

    @pl.when(z > 0)
    def _():
        along(z, -1, True).start()

    own_copy = pltpu.make_async_copy(rows_in, line.at[z], local_sem.at[2])
    own_copy.start()
    own_copy.wait()

    def stage_put(index):
        block = nearest(z, index, nz)

        @pl.when(block < z)
        def _():
            along(block, 1, False).wait_recv()

            @pl.when(z + 1 < nz)
            def _():
                along(block, 1, False).start()

        @pl.when(block > z)
        def _():
            along(block, -1, False).wait_recv()

            @pl.when(z > 0)
            def _():
                along(block, -1, False).start()

        for micro in range(plan.micro):
            laid = jnp.dot(
                put[block, micro],
                line[block, pl.ds(micro * tokens, tokens), :],
                preferred_element_type=F32,
            ).astype(BF16)
            for expert in range(EXP_DEV):
                sbuf[block, micro, expert] = laid[expert * slots : (expert + 1) * slots]
        for micro in range(plan.micro):
            for expert in range(EXP_DEV):
                to_x, to_s = owner(expert, micro)
                here = (to_x == x) & (to_s == s)

                @pl.when(here)
                def _():
                    pltpu.make_async_copy(
                        sbuf.at[block, micro, expert],
                        xbuf.at[block, own_source],
                        to_recv.at[block, own_source],
                    ).start()

                @pl.when(jnp.logical_not(here))
                def _():
                    dispatch_copy(block, expert, micro).start()

    def stage_expert(index):
        block = nearest(z, index, nz)
        slot = index % 2
        for source in range(plan.sources):
            pltpu.make_async_copy(
                xbuf.at[block, source], xbuf.at[block, source], to_recv.at[block, source]
            ).wait()

        @pl.when(index >= 2)
        def _():
            wait_saved(slot)

        if backward:
            load = pltpu.make_async_copy(gate_up.at[block], gbuf.at[slot], local_sem.at[3])
            load.start()
            load.wait()
        pltpu.make_async_copy(xbuf.at[block], sent_save.at[block], save_sem.at[0, block]).start()

        taken = xbuf[block].reshape(many, D)
        half = 256

        def middle(step, _):
            at = pl.multiple_of(step * half, half)
            if backward:
                grad_hidden = lax.dot_general(
                    taken,
                    wdown_v[pl.ds(at, half), :],
                    (((1,), (1,)), ((), ())),
                    preferred_element_type=F32,
                )
                gate = gbuf[slot, :, pl.ds(at, half)].astype(F32)
                up = gbuf[slot, :, pl.ds(FF + at, half)].astype(F32)
                sig = 1.0 / (1.0 + jnp.exp(-gate))
                gs = gate * sig
                grad_gate = grad_hidden * up * (sig + gs * (1.0 - sig))
                gbuf[slot, :, pl.ds(at, half)] = grad_gate.astype(BF16)
                gbuf[slot, :, pl.ds(FF + at, half)] = (grad_hidden * gs).astype(BF16)
            else:
                gate = jnp.dot(taken, win_v[:, pl.ds(at, half)], preferred_element_type=F32)
                up = jnp.dot(taken, win_v[:, pl.ds(FF + at, half)], preferred_element_type=F32)
                gbuf[slot, :, pl.ds(at, half)] = gate.astype(BF16)
                gbuf[slot, :, pl.ds(FF + at, half)] = up.astype(BF16)
                zbuf[slot, :, pl.ds(at, half)] = (gate / (1.0 + jnp.exp(-gate)) * up).astype(BF16)
            return 0

        lax.fori_loop(0, FF // half, middle, 0)
        if backward:
            pltpu.make_async_copy(gbuf.at[slot], grad_save.at[block], save_sem.at[1, slot]).start()
        else:
            pltpu.make_async_copy(gbuf.at[slot], gate_up.at[block], save_sem.at[1, slot]).start()
            pltpu.make_async_copy(zbuf.at[slot], hidden.at[block], save_sem.at[2, slot]).start()

        def last(step, _):
            at = pl.multiple_of(step * half, half)
            if backward:
                result = lax.dot_general(
                    gbuf[slot],
                    win_v[pl.ds(at, half), :],
                    (((1,), (1,)), ((), ())),
                    preferred_element_type=F32,
                )
            else:
                result = jnp.dot(
                    zbuf[slot], wdown_v[:, pl.ds(at, half)], preferred_element_type=F32
                )
            ybuf[block, :, :, pl.ds(at, half)] = result.astype(BF16).reshape(
                plan.sources, slots, half
            )
            return 0

        lax.fori_loop(0, D // half, last, 0)
        for source in range(plan.sources):
            to_x, to_s, copy = return_copy(block, source)
            here = (to_x == x) & (to_s == s)

            @pl.when(here)
            def _():
                pltpu.make_async_copy(
                    ybuf.at[block, source],
                    rbuf.at[block, own_micro, own_expert],
                    back_recv.at[block, own_micro, own_expert],
                ).start()

            @pl.when(jnp.logical_not(here))
            def _():
                copy.start()

    def stage_take(index):
        block = nearest(z, index, nz)
        for micro in range(plan.micro):
            for expert in range(EXP_DEV):
                pltpu.make_async_copy(
                    rbuf.at[block, micro, expert],
                    rbuf.at[block, micro, expert],
                    back_recv.at[block, micro, expert],
                ).wait()
        for micro in range(plan.micro):
            got = lax.dot_general(
                take[block, micro],
                rbuf[block, micro].reshape(EXP_DEV * slots, D),
                (((0,), (0,)), ((), ())),
                preferred_element_type=F32,
            )

            @pl.when(block == z)
            def _():
                at = pl.ds(micro * tokens, tokens)
                if backward:
                    out[at, :] = got
                else:
                    out[at, :] = base[at, :] + got

            @pl.when(block != z)
            def _():
                pbuf[block, pl.ds(micro * tokens, tokens), :] = got.astype(BF16)

        @pl.when(block != z)
        def _():
            sum_copy(block).start()

    def body(index, _):
        @pl.when(index < nz)
        def _():
            stage_put(index)

        @pl.when(index == 1)
        def _():
            load_in.wait()
            load_down.wait()

        @pl.when((index >= 1) & (index < nz + 1))
        def _():
            stage_expert(index - 1)

        @pl.when(index >= 2)
        def _():
            stage_take(index - 2)

        return 0

    lax.fori_loop(0, nz + 2, body, 0)

    def finish(block, _):
        @pl.when(block != z)
        def _():
            pltpu.make_async_copy(qbuf.at[block], qbuf.at[block], sum_recv.at[block]).wait()
            out[...] += qbuf[block].astype(F32)

        return 0

    lax.fori_loop(0, nz, finish, 0)

    def drain(block, _):
        @pl.when((block <= z) & (z + 1 < nz))
        def _():
            along(block, 1, False).wait_send()

        @pl.when((block >= z) & (z > 0))
        def _():
            along(block, -1, False).wait_send()

        for micro in range(plan.micro):
            for expert in range(EXP_DEV):
                to_x, to_s = owner(expert, micro)

                @pl.when(jnp.logical_not((to_x == x) & (to_s == s)))
                def _():
                    dispatch_copy(block, expert, micro).wait_send()

        for source in range(plan.sources):
            to_x, to_s, copy = return_copy(block, source)

            @pl.when(jnp.logical_not((to_x == x) & (to_s == s)))
            def _():
                copy.wait_send()

        @pl.when(block != z)
        def _():
            sum_copy(block).wait_send()

        pltpu.make_async_copy(xbuf.at[block], sent_save.at[block], save_sem.at[0, block]).wait()
        return 0

    lax.fori_loop(0, nz, drain, 0)
    for slot in range(2):
        wait_saved(slot)


def moe_call(plan, backward, collective_id, rows_in, put, take, w_in, w_down, last):
    nz, micro, slots, many = plan.nz, plan.micro, plan.slots, plan.sources * plan.slots
    vmem = pl.BlockSpec(memory_space=pltpu.VMEM)
    hbm = pl.BlockSpec(memory_space=pltpu.HBM)
    saved = (nz, plan.sources, slots, D)
    shape = jax.ShapeDtypeStruct
    outs = [shape((plan.rows, D), F32), shape(saved, BF16), shape((nz, many, 2 * FF), BF16)]
    if not backward:
        outs.append(shape((nz, many, FF), BF16))
    return pl.pallas_call(
        functools.partial(moe_kernel, plan, backward),
        out_shape=outs,
        in_specs=[vmem, vmem, vmem, hbm, hbm, hbm if backward else vmem],
        out_specs=[vmem] + [hbm] * (len(outs) - 1),
        scratch_shapes=[
            pltpu.VMEM((nz, plan.rows, D), BF16),
            pltpu.VMEM((nz, micro, EXP_DEV, slots, D), BF16),
            pltpu.VMEM(saved, BF16),
            pltpu.VMEM(saved, BF16),
            pltpu.VMEM((nz, micro, EXP_DEV, slots, D), BF16),
            pltpu.VMEM((nz, plan.rows, D), BF16),
            pltpu.VMEM((nz, plan.rows, D), BF16),
            pltpu.VMEM((D, 2 * FF), BF16),
            pltpu.VMEM((FF, D), BF16),
            pltpu.VMEM((2, many, 2 * FF), BF16),
            pltpu.VMEM((2, many, FF), BF16),
            DMA((nz,)),
            DMA((nz,)),
            DMA((nz,)),
            DMA((nz, micro, EXP_DEV)),
            DMA((nz, plan.sources)),
            DMA((nz, plan.sources)),
            DMA((nz, micro, EXP_DEV)),
            DMA((nz,)),
            DMA((nz,)),
            DMA((4,)),
            DMA((3, nz)),
        ],
        compiler_params=pltpu.CompilerParams(
            collective_id=collective_id, has_side_effects=True, vmem_limit_bytes=VMEM_LIMIT
        ),
    )(rows_in, put, take, w_in, w_down, last)


def spread_kernel(plan, *refs):
    ins, outs = refs[:2], refs[2:4]
    send, recv, pass_send, pass_recv, local_sem = refs[4:]
    x, z, s = me()
    nx, ns, group = plan.nx, plan.ns, plan.group
    rank = x * ns + s
    own_expert, own_part = rank // group, rank % group
    greet_plane(plan)

    def first(expert, which):
        to = expert * group + s % group
        return to, remote(
            ins[which].at[expert],
            outs[which].at[x, s],
            send.at[expert, which],
            recv.at[x, s, which],
            (to // ns, z, to % ns),
        )

    def onward(layer, source, step, which):
        to = own_expert * group + (own_part + step) % group
        return remote(
            outs[which].at[layer, source],
            outs[which].at[layer, source],
            pass_send.at[layer, source, step - 1, which],
            recv.at[layer, source, which],
            (to // ns, z, to % ns),
        )

    for which in range(2):
        for expert in range(EXP_DEV):
            to, copy = first(expert, which)

            @pl.when(to == rank)
            def _():
                pltpu.make_async_copy(
                    ins[which].at[expert], outs[which].at[x, s], recv.at[x, s, which]
                ).start()

            @pl.when(to != rank)
            def _():
                copy.start()

    def arrived(layer, source, which):
        pltpu.make_async_copy(
            outs[which].at[layer, source], outs[which].at[layer, source], recv.at[layer, source, which]
        ).wait()

    for layer in range(nx):
        for k in range(ns // group):
            source = k * group + own_part
            for which in range(2):
                arrived(layer, source, which)
                for step in range(1, group):
                    onward(layer, source, step, which).start()
    for layer in range(nx):
        for k in range(ns // group):
            for step in range(1, group):
                source = k * group + (own_part + step) % group
                for which in range(2):
                    arrived(layer, source, which)
    for which in range(2):
        for expert in range(EXP_DEV):
            to, copy = first(expert, which)

            @pl.when(to != rank)
            def _():
                copy.wait_send()

    for layer in range(nx):
        for k in range(ns // group):
            source = k * group + own_part
            for which in range(2):
                for step in range(1, group):
                    onward(layer, source, step, which).wait_send()


def spread_call(plan, collective_id, gate_up, down):
    nx, ns = plan.nx, plan.ns
    hbm = pl.BlockSpec(memory_space=pltpu.HBM)
    outs = [jax.ShapeDtypeStruct((nx, ns) + part.shape[1:], BF16) for part in (gate_up, down)]
    return pl.pallas_call(
        functools.partial(spread_kernel, plan),
        out_shape=outs,
        in_specs=[hbm, hbm],
        out_specs=[hbm, hbm],
        scratch_shapes=[
            DMA((EXP_DEV, 2)),
            DMA((nx, ns, 2)),
            DMA((nx, ns, plan.group - 1, 2)),
            DMA((1,)),
            DMA((1,)),
        ],
        compiler_params=pltpu.CompilerParams(collective_id=collective_id, has_side_effects=True),
    )(gate_up, down)


def collect_kernel(plan, layer, *refs):
    ins, outs = refs[:2], refs[2:4]
    parts, stage = refs[4:6], refs[6:8]
    swap_send, swap_recv, send, recv = refs[8:]
    x, z, s = me()
    ns, group = plan.ns, plan.group
    rank = x * ns + s
    own_expert, own_part = rank // group, rank % group
    each = ns // group
    greet_plane(plan)

    def swap(k, step, which):
        part_to = (own_part + step) % group
        to = own_expert * group + part_to
        return remote(
            ins[which].at[k * group + part_to],
            parts[which].at[step - 1, k],
            swap_send.at[step - 1, k, which],
            swap_recv.at[step - 1, k, which],
            (to // ns, z, to % ns),
        )

    def home(k, which):
        return remote(
            stage[which].at[k],
            outs[which].at[own_expert],
            send.at[k, which],
            recv.at[own_expert, which],
            (layer, z, k * group + own_part),
        )

    for k in range(each):
        for which in range(2):
            for step in range(1, group):
                swap(k, step, which).start()
    for k in range(each):
        for which in range(2):
            for step in range(1, group):
                swap(k, step, which).wait_recv()
            total = ins[which][k * group + own_part].astype(F32)
            for step in range(1, group):
                total += parts[which][step - 1, k].astype(F32)
            stage[which][k] = total.astype(BF16)
            here = (x == layer) & (s == k * group + own_part)

            @pl.when(here)
            def _():
                pltpu.make_async_copy(
                    stage[which].at[k], outs[which].at[own_expert], recv.at[own_expert, which]
                ).start()

            @pl.when(jnp.logical_not(here))
            def _():
                home(k, which).start()

    @pl.when(x == layer)
    def _():
        for which in range(2):
            for expert in range(EXP_DEV):
                pltpu.make_async_copy(
                    outs[which].at[expert], outs[which].at[expert], recv.at[expert, which]
                ).wait()

    for k in range(each):
        for which in range(2):
            for step in range(1, group):
                swap(k, step, which).wait_send()
            here = (x == layer) & (s == k * group + own_part)

            @pl.when(jnp.logical_not(here))
            def _():
                home(k, which).wait_send()


def collect_call(plan, layer, collective_id, gate_up, down):
    ns, group = plan.ns, plan.group
    each = ns // group
    vmem = pl.BlockSpec(memory_space=pltpu.VMEM)
    hbm = pl.BlockSpec(memory_space=pltpu.HBM)
    values = [part.reshape(ns, part.shape[0] // ns, D) for part in (gate_up, down)]
    return pl.pallas_call(
        functools.partial(collect_kernel, plan, layer),
        out_shape=[jax.ShapeDtypeStruct((EXP_DEV,) + part.shape[1:], BF16) for part in values],
        in_specs=[vmem, vmem],
        out_specs=[hbm, hbm],
        scratch_shapes=[pltpu.VMEM((group - 1, each) + part.shape[1:], BF16) for part in values]
        + [pltpu.VMEM((each,) + part.shape[1:], BF16) for part in values]
        + [
            DMA((group - 1, each, 2)),
            DMA((group - 1, each, 2)),
            DMA((each, 2)),
            DMA((EXP_DEV, 2)),
        ],
        compiler_params=pltpu.CompilerParams(
            collective_id=collective_id, has_side_effects=True, vmem_limit_bytes=VMEM_LIMIT
        ),
    )(*values)


def rotate(values, cosine, sine_table):
    width_half = values.shape[-1] // 2
    first_part = values[..., :width_half]
    second_part = values[..., width_half:]
    return jnp.concatenate(
        [
            first_part * cosine - second_part * sine_table,
            second_part * cosine + first_part * sine_table,
        ],
        axis=-1,
    )


def norm_forward(hidden, gain_row):
    inverse = lax.rsqrt(jnp.mean(hidden * hidden, axis=-1, keepdims=True) + epsilon)
    return (hidden * inverse * gain_row, inverse)


def norm_backward(hidden, inverse, gain_row, grad_normed):
    scaled = grad_normed * gain_row
    gain_term = jnp.sum(grad_normed * hidden * inverse, axis=0)
    row_inner = jnp.mean(scaled * hidden, axis=-1, keepdims=True)
    return (inverse * scaled - hidden * inverse * inverse * inverse * row_inner, gain_term)


def slot_tables(plan, routes, gates):
    experts, nz = plan.experts, plan.nz
    named = routes[..., None] == jnp.arange(experts, dtype=jnp.int32)
    gate = jnp.sum(jnp.where(named, gates[..., None], 0.0), axis=2)
    named = jnp.any(named, axis=2)
    earlier = jnp.tril(jnp.ones((plan.tokens, plan.tokens), BF16), -1)
    rank = jnp.einsum("ut,mte->mue", earlier, named.astype(BF16), preferred_element_type=F32)
    table = jnp.stack([jnp.where(named, rank, -1.0), gate])
    table = table.reshape(2, plan.micro, plan.tokens, nz, EXP_DEV).transpose(3, 0, 1, 4, 2)
    table = lax.all_to_all(table, "expert", split_axis=0, concat_axis=0, tiled=True)
    rank, gate = table[:, 0], table[:, 1]
    hit = rank[:, :, :, None, :] == jnp.arange(plan.slots, dtype=F32)[:, None]
    shape = (nz, plan.micro, EXP_DEV * plan.slots, plan.tokens)
    one = hit.astype(BF16).reshape(shape)
    weighted = jnp.where(hit, gate[:, :, :, None, :], 0.0).astype(BF16).reshape(shape)
    return one, weighted


def shards(
    inputs,
    segments,
    routes,
    gate_weights,
    query_weight,
    key_value_weight,
    output_weight,
    norm_gains,
    expert_gate_up,
    expert_down,
    cotangent,
):
    section = lax.axis_index("section")
    shard_index = lax.axis_index("shard")
    tokens = inputs.shape[1]
    plan = Plan((lax.axis_size("section"), lax.axis_size("expert"), lax.axis_size("shard")), tokens)
    micro, rows, layers = plan.micro, plan.rows, plan.nx
    length = tokens * plan.ns

    def mine(value):
        return lax.dynamic_slice_in_dim(value, section * micro, micro, 0)

    everywhere = ("section", "expert", "shard")
    weight_q = lax.all_gather(query_weight[0].astype(BF16), everywhere, axis=0, tiled=True)
    weight_kv = lax.all_gather(key_value_weight[0].astype(BF16), everywhere, axis=0, tiled=True)
    weight_o = lax.all_gather(output_weight[0].astype(BF16), everywhere, axis=0, tiled=True)
    weight_q, weight_kv, weight_o = (
        part.reshape((layers, D) + part.shape[1:]) for part in (weight_q, weight_kv, weight_o)
    )
    gains = lax.all_gather(norm_gains.astype(BF16), everywhere, axis=0, tiled=True)
    gains = (
        gains.reshape(layers, plan.nz * plan.ns, 2, -1)
        .transpose(0, 2, 1, 3)
        .reshape(layers, 2, D)
        .astype(F32)
    )
    wide_in, wide_down = spread_call(
        plan, 1, expert_gate_up[0].astype(BF16), expert_down[0].astype(BF16)
    )
    wide_in = wide_in.reshape(layers, D, 2 * FF)
    wide_down = wide_down.reshape(layers, FF, D)
    one, weighted = slot_tables(plan, mine(routes), mine(gate_weights))

    offset = shard_index * tokens
    position = (offset + jnp.arange(tokens, dtype=jnp.int32)).astype(F32)
    frequency = rope_base ** (-jnp.arange(HD // 2, dtype=F32) / (HD // 2))
    angles = position[:, None] * frequency[None, :]
    cosine = jnp.cos(angles)[:, None, :]
    sine_table = jnp.sin(angles)[:, None, :]
    segment_all = mine(segments)[:, 0]
    segment_own = lax.dynamic_slice_in_dim(segment_all, offset, tokens, 1)
    query_place = offset + jnp.arange(tokens, dtype=jnp.int32)
    key_place = jnp.arange(length, dtype=jnp.int32)
    allowed = (segment_own[:, :, None] == segment_all[:, None, :]) & (
        query_place[:, None] >= key_place[None, :]
    )
    allowed = jnp.tile(allowed, (1, GROUP, 1))[:, None]

    def stack_heads(values):
        return (
            values.reshape(micro, tokens, KV_HEADS, GROUP, HD)
            .transpose(0, 2, 3, 1, 4)
            .reshape(micro, KV_HEADS, GROUP * tokens, HD)
        )

    def unstack_heads(values):
        return (
            values.reshape(micro, KV_HEADS, GROUP, tokens, HD)
            .transpose(0, 3, 1, 2, 4)
            .reshape(micro, tokens, HEADS, HD)
        )

    def split_kv(all_kv):
        key_rows = all_kv[..., :WK].reshape(micro, length, KV_HEADS, HD)
        value_rows = all_kv[..., WK:].reshape(micro, length, KV_HEADS, HD)
        return key_rows, value_rows

    def score(stacked, key_rows):
        raw = jnp.einsum("mhqd,mkhd->mhqk", stacked, key_rows, preferred_element_type=F32)
        return jnp.where(allowed, raw * SCALE, -1e30)

    def attend_forward(layer, start):
        normed, inverse = norm_forward(start, gains[layer, 0])
        low = normed.astype(BF16)
        queries = jnp.dot(low, weight_q[layer], preferred_element_type=F32)
        keys_values = jnp.dot(low, weight_kv[layer], preferred_element_type=F32)
        queries_low = rotate(
            queries.reshape(micro, tokens, HEADS, HD), cosine, sine_table
        ).astype(BF16)
        key_rot = rotate(
            keys_values[:, :WK].reshape(micro, tokens, KV_HEADS, HD), cosine, sine_table
        ).reshape(rows, WK)
        local_kv = jnp.concatenate([key_rot, keys_values[:, WK:]], axis=1).astype(BF16)
        local_kv = local_kv.reshape(micro, tokens, 2 * WK)
        all_kv = jnp.stack(
            [lax.all_gather(local_kv[i], "shard", axis=0, tiled=True) for i in range(micro)]
        )
        stacked = stack_heads(queries_low)
        key_rows, value_rows = split_kv(all_kv)
        scores = score(stacked, key_rows)
        row_max = jnp.max(scores, axis=-1, keepdims=True)
        weights = jnp.exp(scores - row_max)
        row_sum = jnp.sum(weights, axis=-1, keepdims=True)
        probs = (weights / row_sum).astype(BF16)
        mixed = jnp.einsum("mhqk,mkhd->mhqd", probs, value_rows, preferred_element_type=F32)
        mixed_low = unstack_heads(mixed.astype(BF16)).reshape(rows, WQ)
        middle = start + jnp.dot(mixed_low, weight_o[layer], preferred_element_type=F32)
        return middle, (start, inverse, low, stacked, all_kv, row_max, row_sum, mixed_low)

    def attend_backward(layer, saved, grad_middle):
        start, inverse, low, stacked, all_kv, row_max, row_sum, mixed_low = saved
        branch = grad_middle.astype(BF16)
        out_term = jnp.einsum("tq,td->qd", mixed_low, branch, preferred_element_type=F32)
        grad_mixed = jnp.einsum(
            "td,qd->tq", branch, weight_o[layer], preferred_element_type=F32
        ).astype(BF16)
        grad_stacked = stack_heads(grad_mixed)
        key_rows, value_rows = split_kv(all_kv)
        scores = score(stacked, key_rows)
        probs = jnp.exp(scores - row_max) / row_sum
        grad_probs = jnp.einsum(
            "mhqd,mkhd->mhqk", grad_stacked, value_rows, preferred_element_type=F32
        )
        inner = jnp.sum(grad_probs * probs, axis=-1, keepdims=True)
        grad_raw = (probs * (grad_probs - inner) * SCALE).astype(BF16)
        grad_queries = jnp.einsum(
            "mhqk,mkhd->mhqd", grad_raw, key_rows, preferred_element_type=F32
        )
        grad_keys = jnp.einsum("mhqk,mhqd->mkhd", grad_raw, stacked, preferred_element_type=F32)
        grad_values = jnp.einsum(
            "mhqk,mhqd->mkhd", probs.astype(BF16), grad_stacked, preferred_element_type=F32
        )
        partial = jnp.concatenate(
            [grad_keys.reshape(micro, length, WK), grad_values.reshape(micro, length, WK)], axis=2
        ).astype(BF16)
        grad_kv = jnp.concatenate(
            [
                lax.psum_scatter(partial[i], "shard", scatter_dimension=0, tiled=True)
                for i in range(micro)
            ]
        ).astype(F32)
        grad_q_low = (
            rotate(unstack_heads(grad_queries), cosine, -sine_table).reshape(rows, WQ).astype(BF16)
        )
        grad_k = rotate(
            grad_kv[:, :WK].reshape(micro, tokens, KV_HEADS, HD), cosine, -sine_table
        ).reshape(rows, WK)
        grad_kv_low = jnp.concatenate([grad_k, grad_kv[:, WK:]], axis=1).astype(BF16)
        query_term = jnp.einsum("td,tq->dq", low, grad_q_low, preferred_element_type=F32)
        kv_term = jnp.einsum("td,tk->dk", low, grad_kv_low, preferred_element_type=F32)
        grad_normed = jnp.einsum(
            "tq,dq->td", grad_q_low, weight_q[layer], preferred_element_type=F32
        ) + jnp.einsum("tk,dk->td", grad_kv_low, weight_kv[layer], preferred_element_type=F32)
        grad_from, gain_term = norm_backward(start, inverse, gains[layer, 0], grad_normed)
        return grad_middle + grad_from, (query_term, kv_term, out_term, gain_term)

    hidden = mine(inputs).reshape(rows, D).astype(F32)
    kept = []
    for layer in range(layers):
        if layer > 0:
            hidden = hidden.astype(BF16).astype(F32)
        middle, saved = attend_forward(layer, hidden)
        normed, inverse = norm_forward(middle, gains[layer, 1])
        hidden, sent, gate_up, hidden_low = moe_call(
            plan,
            False,
            2 + layer,
            normed.astype(BF16),
            one,
            weighted,
            wide_in[layer],
            wide_down[layer],
            middle,
        )
        kept.append((saved, middle, inverse, sent, gate_up, hidden_low))
    output = hidden.reshape(micro, tokens, D)

    grad = mine(cotangent).reshape(rows, D)
    attention_terms = [None] * layers
    expert_terms = [None] * layers
    for layer in reversed(range(layers)):
        saved, middle, inverse, sent, gate_up, hidden_low = kept[layer]
        grad_low = grad.astype(BF16)
        grad_out = grad_low.astype(F32)
        grad_moe, grad_sent, grad_both = moe_call(
            plan,
            True,
            2 + layers + layer,
            grad_low,
            weighted,
            one,
            wide_in[layer],
            wide_down[layer],
            gate_up,
        )
        in_term = jnp.einsum(
            "rd,rf->df",
            sent.reshape(-1, D),
            grad_both.reshape(-1, 2 * FF),
            preferred_element_type=F32,
        ).astype(BF16)
        down_term = jnp.einsum(
            "rf,rd->fd",
            hidden_low.reshape(-1, FF),
            grad_sent.reshape(-1, D),
            preferred_element_type=F32,
        ).astype(BF16)
        expert_terms[layer] = collect_call(plan, layer, 2 + 2 * layers + layer, in_term, down_term)
        grad_from, gain_two = norm_backward(middle, inverse, gains[layer, 1], grad_moe)
        grad, terms = attend_backward(layer, saved, grad_out + grad_from)
        attention_terms[layer] = terms[:3] + (jnp.stack([terms[3], gain_two]),)
    input_grad = grad.reshape(micro, tokens, D)

    def scattered(parts):
        both = jnp.concatenate([part.astype(BF16) for part in parts])
        return lax.psum_scatter(both, everywhere, scatter_dimension=0, tiled=True).astype(F32)[None]

    query_grad, key_value_grad, output_weight_grad = (
        scattered([terms[i] for terms in attention_terms]) for i in range(3)
    )
    gain_parts = jnp.stack([terms[3] for terms in attention_terms])
    gain_parts = gain_parts.reshape(layers, 2, plan.nz * plan.ns, -1).transpose(0, 2, 1, 3)
    gain_grad = lax.psum_scatter(
        gain_parts.reshape((layers * plan.nz * plan.ns,) + (2, gain_parts.shape[-1])),
        everywhere,
        scatter_dimension=0,
        tiled=True,
    )
    gate_up_grad, down_grad = (
        sum(
            jnp.where(section == layer, expert_terms[layer][i], 0) for layer in range(layers)
        ).astype(F32)[None]
        for i in range(2)
    )
    return (
        output,
        input_grad,
        query_grad,
        key_value_grad,
        output_weight_grad,
        gain_grad,
        gate_up_grad,
        down_grad,
    )


def solution(mesh):
    placed = (
        P(None, ("expert", "shard"), None),
        P(None, "expert", None),
        P(None, ("expert", "shard"), None),
        P(None, ("expert", "shard"), None),
        P("section", ("expert", "shard"), None),
        P("section", ("expert", "shard"), None),
        P("section", ("expert", "shard"), None),
        P("section", None, ("expert", "shard")),
        P("section", "expert", "shard", None),
        P("section", "expert", "shard", None),
        P(None, ("expert", "shard"), None),
    )
    return jax.shard_map(
        shards,
        mesh=mesh,
        in_specs=placed,
        out_specs=(
            P("section", ("expert", "shard"), None),
            P("section", ("expert", "shard"), None),
            P("section", ("expert", "shard"), None),
            P("section", ("expert", "shard"), None),
            P("section", ("expert", "shard"), None),
            P("section", None, ("expert", "shard")),
            P("section", "expert", "shard", None),
            P("section", "expert", "shard", None),
        ),
        check_vma=False,
    )
```

time: 2630 us -> 1680 us (0.64)
  Pallas kernels: 0 us -> 951 us
  waiting for transfers between devices: 874 us -> 234 us
  matrix products: 610 us -> 185 us
  local copies, waits for them, and re-layouts: 473 us -> 69.1 us
  blocking collectives: 308 us -> 118 us
  other arithmetic: 241 us -> 86.8 us
  starting transfers between devices: 88.7 us -> 6.87 us
    pallas_call x0 -> x7, Pallas kernels: none -> 951 us  [the longest x4 653 us: moe_call(): pl.pallas_call(functools.partial(moe_kernel, plan, backward), out_shape=o...]
    dot_general x110 -> x33, matrix products: 610 us -> 172 us  [the longest x2 25.5 us: shards(): jnp.einsum('rd,rf->df', sent.reshape(-1, D), grad_both.reshape(-1, 2 * FF...]
    all_to_all x15 -> x1, waiting for transfers between devices: 300 us -> 0.01 us  [slot_tables(): lax.all_to_all(table, 'expert', split_axis=0, concat_axis=0, tiled=True)]
    all_to_all x5 -> x0, blocking collectives: 247 us -> none  [the longest x3 151 us: shards(): lax.all_to_all(outgoing, 'expert', split_axis=0, concat_axis=1, tiled=True)]
    reduce_scatter x5 -> x3, waiting for transfers between devices: 350 us -> 106 us  [scattered(): lax.psum_scatter(both, everywhere, scatter_dimension=0, tiled=True)]
    all_gather x5 -> x3, waiting for transfers between devices: 164 us -> 29.8 us  [the longest x1 29.8 us: shards(): lax.all_gather(output_weight[0].astype(BF16), everywhere, axis=0, tiled=T...]
    convert_element_type x36 -> x5, local copies, waits for them, and re-layouts: 83.7 us -> 1.46 us  [the longest x1 0.81 us: attend_backward(): rotate(unstack_heads(grad_queries), cosine, -sine_table).reshape(rows, WQ)]
    unnamed x22 -> x14, waiting for transfers between devices: 23.5 us -> 98.6 us
  transfers between devices with their start and end apart: 40 -> 11, of which waited for: 28 -> 6; matrix products, arithmetic and copies ran while one was open for 32% -> 12% of each run, Pallas kernels for 0% -> 18%
where the time goes in v1:
time: 1680 us; the launch traced here: 1670 us
  Pallas kernels  951 us (57%)
  waiting for transfers between devices  234 us (14%)
  matrix products  185 us (11%)
  blocking collectives  118 us (7%)
  other arithmetic  86.8 us (5%)
  local copies, waits for them, and re-layouts  69.1 us (4%)
    pallas_call x4, Pallas kernels, moe_call(): pl.pallas_call(functools.partial(moe_kernel, plan, backward), out_shape=o...  653 us
    pallas_call x2, Pallas kernels, collect_call(): pl.pallas_call(functools.partial(collect_kernel, plan, layer), out_shape=...  197 us
    reduce_scatter x3, waiting for transfers between devices, scattered(): lax.psum_scatter(both, everywhere, scatter_dimension=0, tiled=True)  106 us
    pallas_call x1, Pallas kernels, spread_call(): pl.pallas_call(functools.partial(spread_kernel, plan), out_shape=outs, in...  100 us
    unnamed x14, waiting for transfers between devices  98.6 us
    all_gather x1, blocking collectives, shards(): lax.all_gather(norm_gains.astype(BF16), everywhere, axis=0, tiled=True)  41.8 us
    unnamed x1, blocking collectives  39.5 us
    all_gather x4, blocking collectives, attend_forward(): lax.all_gather(local_kv[i], 'shard', axis=0, tiled=True)  36.8 us
  transfers between devices with their start and end apart: 11, of which 6 were waited for; matrix products, arithmetic and copies ran while one was open for 12% of the time, Pallas kernels for 18%

profile of v1, /device:TPU:0, one launch (start us, length us, event | category | flops | bytes accessed | tf_op | source)
XLA Modules:
  0.0 1667.0 jit_solution(6911440854098969026)
XLA Ops:
  15.0 6.3 all-to-all-start
  22.0 41.8 %all_gather.24 = bf16[32,2,96]{2,1,0:T(2,128)(2,1)S(1)} all-gather(bf16[1,2,96]{2,1,0:T(2,128)(2,1)S(1)} %convert_element_type.208), channel_id=1, replica_groups=mesh['section'=2,'expert'=4,'shard'=4] {'section','expert','shard'}, dimensions={0}, use_global_device_ids=true | all-gather | bytes 12672 | tf_op jit(solution)/shard_map/all_gather | solution.py:740
  64.0 4.1 convert_bitcast_fusion.1.refs_1_
  68.0 6.6 convert_bitcast_fusion.refs_0_
  74.7 100.3 %shard_map.170 = (bf16[2,4,384,1536]{3,2,1,0:T(8,128)(2,1)}, bf16[2,4,192,1536]{3,2,1,0:T(8,128)(2,1)}) custom-call(bf16[4,384,1536]{2,1,0:T(8,128)(2,1)} %convert_bitcast_fusion.refs_0_, bf16[4,192,1536]{2,1,0:T(8,128)(2,1)} %convert_bitcast_fusion.1.refs_1_), custom_call_target="tpu_custom_call" | custom-call | tf_op jit(solution)/shard_map/pallas_call | solution.py:552
  179.9 2.7 fusion.223
  182.6 8.4 fusion.222
  199.4 13.7 all_gather.27
  213.1 7.3 all_gather.28
  221.3 5.1 slice_bitcast_fusion.9
  226.4 6.9 copy.208
  233.3 3.3 fusion.108
  237.3 6.5 fusion.227
  243.8 4.5 fusion.79
  248.9 29.8 %all-gather.11.cloned.1.call-done = bf16[1,3072,1536]{2,1,0:T(8,128)(2,1)} async-done(((bf16[1,96,1536]{2,1,0:T(8,128)(2,1)}), bf16[1,3072,1536]{2,1,0:T(8,128)(2,1)}) %all-gather.11.cloned.1.call-update) | async-done | bytes 9437200 | tf_op jit(solution)/shard_map/all_gather | solution.py:736
  278.7 4.3 multiply_reduce_fusion.7
  284.4 155.5 %shard_map.171 = (f32[256,1536]{1,0:T(8,128)}, bf16[4,8,48,1536]{3,2,1,0:T(8,128)(2,1)}, bf16[4,384,1536]{2,1,0:T(8,128)(2,1)}, bf16[4,384,768]{2,1,0:T(8,128)(2,1)}) custom-call(bf16[256,1536]{1,0:T(8,128)(2,1)} %multiply_convert_fusion.3.refs_0_, bf16[4,2,192,128]{3,2,1,0:T(8,128)(2,1)} %fusion.111.refs_1_.refs_2_, ...), custom_call_target="tpu_custom_call" | custom-call | tf_op jit(solution)/shard_map/pallas_call | solution.py:436
  441.6 2.3 fusion.86
  444.6 5.5 fusion.17
  450.1 2.6 reshape.488
  455.3 8.6 all_gather.30
  463.9 7.3 all_gather.31
  472.1 6.5 fusion.232
  478.7 4.0 fusion.82
  483.5 4.1 multiply_reduce_fusion.6
  489.0 170.4 %shard_map.172 = (f32[256,1536]{1,0:T(8,128)}, bf16[4,8,48,1536]{3,2,1,0:T(8,128)(2,1)}, bf16[4,384,1536]{2,1,0:T(8,128)(2,1)}, bf16[4,384,768]{2,1,0:T(8,128)(2,1)}) custom-call(bf16[256,1536]{1,0:T(8,128)(2,1)} %multiply_convert_fusion.2.refs_0_, bf16[4,2,192,128]{3,2,1,0:T(8,128)(2,1)} %fusion.111.refs_1_.refs_2_, ...), custom_call_target="tpu_custom_call" | custom-call | tf_op jit(solution)/shard_map/pallas_call | solution.py:436
  659.4 171.9 %shard_map.173 = (f32[256,1536]{1,0:T(8,128)}, bf16[4,8,48,1536]{3,2,1,0:T(8,128)(2,1)}, bf16[4,384,1536]{2,1,0:T(8,128)(2,1)}) custom-call(bf16[256,1536]{1,0:T(8,128)(2,1)} %bitcast.361, bf16[4,2,192,128]{3,2,1,0:T(8,128)(2,1)} %fusion.110.refs_2_.refs_1_, bf16[4,2,192,128]{3,2,1,0:T(8,128)(2,1)} %fusion.111.refs_1_.refs_2_, bf16[1536,1536]{1,0:T(8,128)(2,1)} %bitcast.354, ...), custom_call_target="tpu_custom_call" | custom-call | tf_op jit(solution)/shard_map/pallas_call | solution.py:436
  834.1 4.3 fusion.44
  839.6 4.7 fusion.132
  844.3 4.8 fusion.90
  849.2 10.6 fusion.96
  863.4 11.7 fusion.25
  879.0 4.9 fusion.16
  883.9 16.4 reduce-scatter.22.cloned.1.call-done
  901.4 23.1 %reduce-scatter.24.cloned.1.call-done = bf16[128,512]{1,0:T(8,128)(2,1)} async-done(((bf16[512,512]{1,0:T(8,128)(2,1)}), bf16[128,512]{1,0:T(8,128)(2,1)}) %reduce-scatter.24.cloned.1.call-update) | async-done | bytes 131088
  927.6 3.6 fusion.57
  932.7 155.5 %shard_map.174 = (f32[256,1536]{1,0:T(8,128)}, bf16[4,8,48,1536]{3,2,1,0:T(8,128)(2,1)}, bf16[4,384,1536]{2,1,0:T(8,128)(2,1)}) custom-call(bf16[256,1536]{1,0:T(8,128)(2,1)} %fusion.53.refs_0_, bf16[4,2,192,128]{3,2,1,0:T(8,128)(2,1)} %fusion.110.refs_2_.refs_1_, bf16[4,2,192,128]{3,2,1,0:T(8,128)(2,1)} %fusion.111.refs_1_.refs_2_, ...), custom_call_target="tpu_custom_call" | custom-call | tf_op jit(solution)/shard_map/pallas_call | solution.py:436
  1088.2 2.6 multiply_reduce_fusion.3
  1091.3 3.7 fusion.45
  1096.3 4.7 fusion.143
  1100.9 4.8 fusion.87
  1105.8 10.6 fusion.93
  1116.4 2.1 fusion.154
  1118.6 2.0 copy.274
  1123.7 35.1 %reduce-scatter.26.cloned.1.call-done = bf16[128,512]{1,0:T(8,128)(2,1)} async-done(((bf16[512,512]{1,0:T(8,128)(2,1)}), bf16[128,512]{1,0:T(8,128)(2,1)}) %reduce-scatter.26.cloned.1.call-update) | async-done | bytes 131088
  1159.8 23.8 %reduce-scatter.28.cloned.1.call-done = bf16[128,512]{1,0:T(8,128)(2,1)} async-done(((bf16[512,512]{1,0:T(8,128)(2,1)}), bf16[128,512]{1,0:T(8,128)(2,1)}) %reduce-scatter.28.cloned.1.call-update) | async-done | bytes 131088
  1196.0 2.6 convolution_convert_fusion
  1200.0 12.2 pad_maximum_fusion.1
  1213.6 3.7 convolution_convert_fusion.2
  1217.3 12.2 fusion.31
  1234.9 12.3 pad_maximum_fusion
  1247.4 8.3 convolution_convert_fusion.6
  1255.7 12.7 convolution_convert_fusion.4
  1268.5 84.9 %shard_map.176 = (bf16[4,384,1536]{2,1,0:T(8,128)(2,1)}, bf16[4,192,1536]{2,1,0:T(8,128)(2,1)}) custom-call(bf16[4,384,1536]{2,1,0:T(8,128)(2,1)} %bitcast.369, bf16[4,192,1536]{2,1,0:T(8,128)(2,1)} %bitcast.385), custom_call_target="tpu_custom_call" | custom-call | tf_op jit(solution)/shard_map/pallas_call | solution.py:648
  1353.6 8.6 convolution_convert_fusion.7
  1362.2 12.7 convolution_convert_fusion.5
  1375.0 112.3 %shard_map.175 = (bf16[4,384,1536]{2,1,0:T(8,128)(2,1)}, bf16[4,192,1536]{2,1,0:T(8,128)(2,1)}) custom-call(bf16[4,384,1536]{2,1,0:T(8,128)(2,1)} %bitcast.370, bf16[4,192,1536]{2,1,0:T(8,128)(2,1)} %bitcast.386), custom_call_target="tpu_custom_call" | custom-call | tf_op jit(solution)/shard_map/pallas_call | solution.py:648
  1487.3 4.0 fusion.8
  1491.4 2.8 bitcast_convert_fusion.1
  1496.9 5.0 bitcast_convert_fusion
  1501.9 2.0 fusion.70
  1504.0 39.5 %all-reduce = f32[32,2,96]{2,1,0:T(2,128)S(1)} all-reduce(f32[32,2,96]{2,1,0:T(2,128)S(1)} %bitcast.419), channel_id=12, replica_groups=mesh['section'=2,'expert'=4,'shard'=4] {'section','expert','shard'}, use_global_device_ids=true, to_apply=%region_27.28.clone | all-reduce | flops 6144 | bytes 49152
  1544.1 3.5 fusion.64
  1551.2 105.8 %reduce-scatter.16.cloned.1.call-done = bf16[96,1536]{1,0:T(8,128)(2,1)} async-done(((bf16[3072,1536]{1,0:T(8,128)(2,1)}), bf16[96,1536]{1,0:T(8,128)(2,1)}) %reduce-scatter.16.cloned.1.call-update) | async-done | bytes 294928 | tf_op jit(solution)/shard_map/reduce_scatter | solution.py:926
  (301 shorter events, 86.4 us)
Async XLA Ops:
  7.2 168.5 %copy-start = (bf16[4,128,1536]{2,1,0:T(8,128)(2,1)S(1)}, bf16[4,128,1536]{2,1,0:T(8,128)(2,1)}, u32[]{:S(2)}) copy-start(bf16[4,128,1536]{2,1,0:T(8,128)(2,1)} %param.21) | copy-start | bytes 4718596
  7.2 56.7 %copy-start.61 = (s32[4,1,512]{2,1,0:T(1,128)S(1)}, s32[4,1,512]{2,1,0:T(1,128)}, u32[]{:S(2)}) copy-start(s32[4,1,512]{2,1,0:T(1,128)} %param.12) | copy-start | bytes 24580
  7.2 189.1 %all-gather.9.cloned.1.call-start = ((), (), s32[]{:S(2)}) async-start(), calls=%async_computation.12 | async-start | bytes 3244032 | tf_op jit(solution)/shard_map/all_gather | solution.py:735
  9.0 212.4 %all-gather.7.cloned.1.call-start = ((), (), s32[]{:S(2)}) async-start(), calls=%async_computation.11 | async-start | bytes 9732096 | tf_op jit(solution)/shard_map/all_gather | solution.py:734
  10.8 267.9 %all-gather.11.cloned.1.call-start = ((), (), s32[]{:S(2)}) async-start(), calls=%async_computation.13 | async-start | bytes 9732096 | tf_op jit(solution)/shard_map/all_gather | solution.py:736
  15.0 178.0 %all-to-all-start = ((f32[4,2,2,4,128]{4,3,2,1,0:T(4,128)}), f32[4,2,2,4,128]{4,3,2,1,0:T(4,128)}, u32[]{:S(2)}, u32[]{:S(2)}) async-start(f32[4,2,2,4,128]{4,3,2,1,0:T(4,128)} %copy.216), calls=%async_computation | async-start | bytes 65536 | tf_op jit(solution)/shard_map/all_to_all | solution.py:701
  21.3 879.1 %reduce-scatter.22.cloned.1.call-start = ((), (), s32[]{:S(2)}) async-start(), calls=%async_computation.14 | async-start | bytes 655360
  74.7 100.3 %copy-start.12 = (bf16[4,128,1536]{2,1,0:T(8,128)(2,1)S(1)}, bf16[4,128,1536]{2,1,0:T(8,128)(2,1)}, u32[]{:S(2)}) copy-start(bf16[4,128,1536]{2,1,0:T(8,128)(2,1)} %param.11) | copy-start | bytes 4718596
  175.4 4.0 copy-start.51
  175.4 4.0 copy-start.58
  176.7 3.2 copy-start.23
  179.4 53.9 %copy-start.18 = (bf16[2,128,1536]{2,1,0:T(8,128)(2,1)}, bf16[2,128,1536]{2,1,0:T(8,128)(2,1)S(1)}, u32[]{:S(2)}) copy-start(bf16[2,128,1536]{2,1,0:T(8,128)(2,1)S(1)} %fusion.67) | copy-start | bytes 2359300
  191.0 5.4 copy-start.34
  192.9 44.4 %copy-start.37 = (pred[2,768,512]{1,2,0:T(8,128)(4,1)}, pred[2,768,512]{1,2,0:T(8,128)(4,1)S(1)}, u32[]{:S(2)}) copy-start(pred[2,768,512]{1,2,0:T(8,128)(4,1)S(1)} %copy.206) | copy-start | bytes 2359300
  221.3 22.5 %copy-start.29 = (bf16[2,64,2,8,128]{4,3,2,1,0:T(8,128)(2,1)}, bf16[2,64,2,8,128]{4,3,2,1,0:T(8,128)(2,1)S(1)}, u32[]{:S(2)}) copy-start(bf16[2,64,2,8,128]{4,3,2,1,0:T(8,128)(2,1)S(1)} %get-tuple-element.83) | copy-start | bytes 1572868
  237.3 6.5 copy-start.35
  243.8 862.0 %copy-start.63 = (f32[2,2,768]{2,1,0:T(2,128)}, f32[2,2,768]{2,1,0:T(2,128)S(1)}, u32[]{:S(2)}) copy-start(f32[2,2,768]{2,1,0:T(2,128)S(1)} %get-tuple-element.105) | copy-start | bytes 36868
  248.9 34.1 %copy-start.20 = (bf16[2,2,6,128,128]{3,0,4,2,1:T(2,128)(2,1)}, bf16[2,2,6,128,128]{3,0,4,2,1:T(2,128)(2,1)S(1)}, u32[]{:S(2)}) copy-start(bf16[2,2,6,128,128]{3,0,4,2,1:T(2,128)(2,1)S(1)} %copy.215) | copy-start | bytes 2359300
  441.5 42.0 %copy-start.8 = (bf16[256,1536]{1,0:T(8,128)(2,1)}, bf16[256,1536]{1,0:T(8,128)(2,1)S(1)}, u32[]{:S(2)}) copy-start(bf16[256,1536]{1,0:T(8,128)(2,1)S(1)} %get-tuple-element.61) | copy-start | bytes 2359300
  441.6 680.2 %copy-start.56 = (f32[256]{0:T(256)}, f32[256]{0:T(256)S(1)}, u32[]{:S(2)}) copy-start(f32[256]{0:T(256)S(1)} %add_rsqrt_fusion.1) | copy-start | bytes 3076
  443.9 6.2 copy-start.33
  454.3 17.8 %copy-start.38 = (pred[2,768,512]{1,2,0:T(8,128)(4,1)S(1)}, pred[2,768,512]{1,2,0:T(8,128)(4,1)}, u32[]{:S(2)}) copy-start(pred[2,768,512]{1,2,0:T(8,128)(4,1)} %copy-done.37) | copy-start | bytes 2359300
  472.1 6.5 copy-start.30
  483.5 4.1 copy-start.22
  659.4 172.0 %copy-start.5 = (f32[256,1536]{1,0:T(8,128)S(1)}, f32[256,1536]{1,0:T(8,128)}, u32[]{:S(2)}) copy-start(f32[256,1536]{1,0:T(8,128)} %copy-done.4) | copy-start | bytes 4718596
  834.1 97.1 %copy-start.6 = (f32[256,1536]{1,0:T(8,128)}, f32[256,1536]{1,0:T(8,128)S(1)}, u32[]{:S(2)}) copy-start(f32[256,1536]{1,0:T(8,128)S(1)} %subtract_add_fusion.1) | copy-start | bytes 4718596
  844.3 4.8 copy-start.39
  859.7 3.6 copy-start.50
  862.1 62.4 %reduce-scatter.24.cloned.1.call-start = ((), (), s32[]{:S(2)}) async-start(), calls=%async_computation.15 | async-start | bytes 655360
  862.3 64.5 %copy-start.40 = (f32[128,64]{1,0:T(8,128)}, f32[128,64]{1,0:T(8,128)S(1)}, u32[]{:S(2)}) copy-start(f32[128,64]{1,0:T(8,128)S(1)} %copy.238) | copy-start | bytes 98308
  863.3 295.5 %reduce-scatter.26.cloned.1.call-start = ((), (), s32[]{:S(2)}) async-start(), calls=%async_computation.16 | async-start | bytes 655360
  883.9 43.6 %copy-start.9 = (bf16[256,1536]{1,0:T(8,128)(2,1)S(1)}, bf16[256,1536]{1,0:T(8,128)(2,1)}, u32[]{:S(2)}) copy-start(bf16[256,1536]{1,0:T(8,128)(2,1)} %copy-done.8) | copy-start | bytes 2359300
  901.4 24.8 %copy-start.45 = (bf16[128,512]{0,1:T(8,128)(2,1)}, bf16[128,512]{0,1:T(8,128)(2,1)S(1)}, u32[]{:S(2)}) copy-start(bf16[128,512]{0,1:T(8,128)(2,1)S(1)} %copy.271) | copy-start | bytes 393220
  927.6 3.6 copy-start.53
  932.7 155.5 %copy-start.3 = (f32[256,1536]{1,0:T(8,128)S(1)}, f32[256,1536]{1,0:T(8,128)}, u32[]{:S(2)}) copy-start(f32[256,1536]{1,0:T(8,128)} %copy-done.2) | copy-start | bytes 4718596
  1088.2 2.6 copy-start.15
  1100.9 4.8 copy-start.36
  1116.4 5.4 copy-start.10
  1116.4 5.4 copy-start.46
  1116.4 5.4 copy-start.48
  1116.4 5.4 copy-start.54
  1120.7 63.0 %reduce-scatter.28.cloned.1.call-start = ((), (), s32[]{:S(2)}) async-start(), calls=%async_computation.17 | async-start | bytes 655360
  1121.7 425.9 %reduce-scatter.18.cloned.1.call-start = ((), (), s32[]{:S(2)}) async-start(), calls=%async_computation.9 | async-start | bytes 3244032 | tf_op jit(solution)/shard_map/reduce_scatter | solution.py:926
  1159.8 24.9 %copy-start.41 = (bf16[128,512]{0,1:T(8,128)(2,1)}, bf16[128,512]{0,1:T(8,128)(2,1)S(1)}, u32[]{:S(2)}) copy-start(bf16[128,512]{0,1:T(8,128)(2,1)S(1)} %copy.275) | copy-start | bytes 393220
  1185.5 7.1 copy-start.32
  1194.6 354.7 %reduce-scatter.20.cloned.1.call-start = ((), (), s32[]{:S(2)}) async-start(), calls=%async_computation.10 | async-start | bytes 9732096 | tf_op jit(solution)/shard_map/reduce_scatter | solution.py:926
  1196.0 2.6 copy-start.21
  1212.2 5.1 copy-start.64
  1212.2 444.8 %reduce-scatter.16.cloned.1.call-start = ((), (), s32[]{:S(2)}) async-start(), calls=%async_computation.8 | async-start | bytes 9732096 | tf_op jit(solution)/shard_map/reduce_scatter | solution.py:926
  1268.4 84.9 %copy-start.55 = (f32[1536]{0:T(1024)S(1)}, f32[1536]{0:T(1024)}, u32[]{:S(2)}) copy-start(f32[1536]{0:T(1024)} %get-tuple-element.50) | copy-start | bytes 18436
  1268.5 85.0 %copy-start.60 = (f32[1536]{0:T(1024)S(1)}, f32[1536]{0:T(1024)}, u32[]{:S(2)}) copy-start(f32[1536]{0:T(1024)} %get-tuple-element.54) | copy-start | bytes 18436
  1487.3 4.1 copy-start.27
  1487.3 4.1 copy-start.28
  1491.3 3.9 slice-start.2
  1491.3 4.0 slice-start.3
  1491.4 5.5 copy-start.24
  1496.8 5.0 copy-start.13
  1496.8 5.0 copy-start.42
  1496.8 5.0 copy-start.44
  1496.9 5.0 copy-start.52
  1496.9 5.0 copy-start.59
  1496.9 5.0 copy-start.62
  1544.1 115.9 %copy-start.1 = (bf16[4,128,1536]{2,1,0:T(8,128)(2,1)S(1)}, bf16[4,128,1536]{2,1,0:T(8,128)(2,1)}, u32[]{:S(2)}) copy-start(bf16[4,128,1536]{2,1,0:T(8,128)(2,1)} %param.21) | copy-start | bytes 4718596
  1547.6 111.2 %copy-start.31 = (f32[256,1536]{1,0:T(8,128)S(1)}, f32[256,1536]{1,0:T(8,128)}, u32[]{:S(2)}) copy-start(f32[256,1536]{1,0:T(8,128)} %get-tuple-element.31) | copy-start | bytes 4718596
  (17 other events, 26.5 us)
Sparse Core Ops, SparseCore 0:
  11.5 61.7 all-gather.8
  76.7 114.0 all-gather.6
  194.3 84.3 all-gather.10
  862.2 38.0 reduce-scatter.21
  902.9 21.6 reduce-scatter.23
  1120.8 37.9 reduce-scatter.25
  1162.0 21.6 reduce-scatter.27
  1194.7 101.4 reduce-scatter.17
  1302.1 213.2 reduce-scatter.19
  1522.2 134.7 reduce-scatter.15

commit v2 on v1

v2 whole, which is shorter than its diff:
```python
import functools

import jax
import jax.numpy as jnp
from jax import lax
from jax.experimental import pallas as pl
from jax.experimental.pallas import tpu as pltpu
from jax.sharding import PartitionSpec as P

D = 1536
HEADS = 12
KV_HEADS = 2
HD = 128
FF = 768
TOPK = 4
EXP_DEV = 4
MICRO = 4
GROUP = HEADS // KV_HEADS
WQ = HEADS * HD
WK = KV_HEADS * HD
SCALE = HD ** (-0.5)

epsilon = 1e-06
rope_base = 10000.0

MESH = pl.DeviceIdType.MESH
F32 = jnp.float32
BF16 = jnp.bfloat16
DMA = pltpu.SemaphoreType.DMA
VMEM_LIMIT = 60 * 2**20


class Plan:
    def __init__(self, mesh_shape, tokens):
        self.nx, self.nz, self.ns = mesh_shape
        self.tokens = tokens
        self.micro = MICRO // self.nx
        self.rows = self.micro * tokens
        self.ranks = self.nx * self.ns
        self.group = self.ranks // EXP_DEV
        self.halves = self.group // 2
        self.sources = self.ranks // self.halves
        self.experts = EXP_DEV * self.nz
        self.capacity = 5 * tokens * TOPK // (4 * self.experts)
        self.slots = -(-self.micro * self.capacity // 16) * 16
        self.blocks = self.nz // 2
        self.many = self.sources * self.slots


def me():
    return lax.axis_index("section"), lax.axis_index("expert"), lax.axis_index("shard")


def remote(src, dst, send, recv, device):
    return pltpu.make_async_remote_copy(
        src_ref=src,
        dst_ref=dst,
        send_sem=send,
        recv_sem=recv,
        device_id=device,
        device_id_type=MESH,
    )


def landed(ref, sem):
    pltpu.make_async_copy(ref, ref, sem).wait()


def greet_plane(plan, along=False):
    x, z, s = me()
    barrier = pltpu.get_barrier_semaphore()
    mine = x * plan.ns + s
    for step in range(1, plan.ranks):
        other = (mine + step) % plan.ranks
        pl.semaphore_signal(
            barrier, inc=1, device_id=(other // plan.ns, z, other % plan.ns), device_id_type=MESH
        )
    total = plan.ranks - 1
    if along:
        for step in range(1, plan.nz):
            pl.semaphore_signal(
                barrier, inc=1, device_id=(x, (z + step) % plan.nz, s), device_id_type=MESH
            )
        total += plan.nz - 1
    pl.semaphore_wait(barrier, total)


def nearest(place, index, count):
    left = place
    right = count - 1 - place
    short = jnp.minimum(left, right)
    odd = index % 2
    near = place + (1 - 2 * odd) * ((index + 1) // 2)
    far = jnp.where(left < right, index, count - 1 - index)
    return jnp.where(index <= 2 * short, near, far)


HALF = D // 2
TILE = 256


def moe_kernel(plan, backward, *refs):
    if backward:
        (rows_in, put, take, w_in, w_down, gate_up, out, sent_save, grad_save) = refs[:9]
        scratch = refs[9:]
    else:
        (rows_in, put, take, w_in, w_down, base, out, sent_save, gate_up, hidden) = refs[:10]
        scratch = refs[10:]
    (
        line,
        sbuf,
        xbuf,
        ybuf,
        rbuf,
        pbuf,
        qbuf,
        win_v,
        wdown_v,
        gbuf,
        zbuf,
        line_recv,
        line_right,
        line_left,
        to_send,
        to_recv,
        back_send,
        back_recv,
        sum_send,
        sum_recv,
        local_sem,
        save_sem,
    ) = scratch
    x, z, s = me()
    nz, ns, slots, many = plan.nz, plan.ns, plan.slots, plan.many
    rank = x * ns + s
    own_expert = rank // plan.group
    own_turn = (rank % plan.group) // plan.halves
    own_half = rank % plan.halves
    part = ns // plan.halves
    own_source = x * part + s // plan.halves
    chunk = plan.tokens

    load_in = pltpu.make_async_copy(w_in, win_v, local_sem.at[0])
    load_down = pltpu.make_async_copy(w_down, wdown_v, local_sem.at[1])
    load_in.start()
    load_down.start()
    if backward:
        load_gate = pltpu.make_async_copy(gate_up, gbuf, local_sem.at[3])
        load_gate.start()
    greet_plane(plan, along=True)

    def along(block, piece, step, own):
        at = pl.ds(piece * chunk, chunk)
        src = rows_in.at[at] if own else line.at[block, at]
        sem = line_right if step > 0 else line_left
        return remote(
            src,
            line.at[block, at],
            sem.at[block, piece],
            line_recv.at[block, piece],
            (x, z + step, s),
        )

    def owner(block, expert):
        rank_to = expert * plan.group + (block % 2) * plan.halves + s % plan.halves
        return rank_to // ns, rank_to % ns

    def dispatch_copy(block, expert):
        to_x, to_s = owner(block, expert)
        here = (to_x == x) & (to_s == s)
        return here, remote(
            sbuf.at[block, expert],
            xbuf.at[block // 2, own_source],
            to_send.at[block, expert],
            to_recv.at[block // 2, own_source],
            (to_x, z, to_s),
        )

    def return_copy(block, half, source):
        to_x = source // part
        to_s = (source % part) * plan.halves + own_half
        here = (to_x == x) & (to_s == s)
        return here, remote(
            ybuf.at[block // 2, half, source],
            rbuf.at[block, half, own_expert],
            back_send.at[block // 2, half, source],
            back_recv.at[block, half, own_expert],
            (to_x, z, to_s),
        )

    def sum_copy(block, half):
        rightward = (block > z).astype(jnp.int32)
        to = z - 1 + 2 * rightward
        into = jnp.where((rightward == 1) & (block == to), nz, block)
        return remote(
            pbuf.at[block, half],
            qbuf.at[into, half],
            sum_send.at[block, half],
            sum_recv.at[into, half],
            (x, to, s),
        )

    for piece in range(plan.micro):

        @pl.when(z + 1 < nz)
        def _():
            along(z, piece, 1, True).start()

        @pl.when(z > 0)
        def _():
            along(z, piece, -1, True).start()

    own_copy = pltpu.make_async_copy(rows_in, line.at[z], local_sem.at[2])
    own_copy.start()
    own_copy.wait()

    def stage_put(index):
        block = nearest(z, index, nz)
        for piece in range(plan.micro):

            @pl.when(block < z)
            def _():
                along(block, piece, 1, False).wait_recv()

                @pl.when(z + 1 < nz)
                def _():
                    along(block, piece, 1, False).start()

            @pl.when(block > z)
            def _():
                along(block, piece, -1, False).wait_recv()

                @pl.when(z > 0)
                def _():
                    along(block, piece, -1, False).start()

        def lay(step, _):
            at = pl.ds(pl.multiple_of(step * TILE, TILE), TILE)
            laid = jnp.dot(put[block], line[block, :, at], preferred_element_type=F32)
            sbuf[block, :, :, at] = laid.astype(BF16).reshape(EXP_DEV, slots, TILE)
            return 0

        lax.fori_loop(0, D // TILE, lay, 0)
        for expert in range(EXP_DEV):
            here, copy = dispatch_copy(block, expert)

            @pl.when(here)
            def _():
                pltpu.make_async_copy(
                    sbuf.at[block, expert],
                    xbuf.at[block // 2, own_source],
                    to_recv.at[block // 2, own_source],
                ).start()

            @pl.when(jnp.logical_not(here))
            def _():
                copy.start()

    def stage_expert(index):
        block = nearest(z, index, nz)
        pair = block // 2
        for source in range(plan.sources):
            landed(xbuf.at[pair, source], to_recv.at[pair, source])
        pltpu.make_async_copy(xbuf.at[pair], sent_save.at[pair], save_sem.at[0, pair]).start()
        taken = xbuf[pair].reshape(many, D)

        def middle(step, _):
            at = pl.multiple_of(step * TILE, TILE)
            if backward:
                grad_hidden = lax.dot_general(
                    taken,
                    wdown_v[pl.ds(at, TILE), :],
                    (((1,), (1,)), ((), ())),
                    preferred_element_type=F32,
                )
                gate = gbuf[pair, :, pl.ds(at, TILE)].astype(F32)
                up = gbuf[pair, :, pl.ds(FF + at, TILE)].astype(F32)
                sig = 1.0 / (1.0 + jnp.exp(-gate))
                gs = gate * sig
                grad_gate = grad_hidden * up * (sig + gs * (1.0 - sig))
                gbuf[pair, :, pl.ds(at, TILE)] = grad_gate.astype(BF16)
                gbuf[pair, :, pl.ds(FF + at, TILE)] = (grad_hidden * gs).astype(BF16)
            else:
                gate = jnp.dot(taken, win_v[:, pl.ds(at, TILE)], preferred_element_type=F32)
                up = jnp.dot(taken, win_v[:, pl.ds(FF + at, TILE)], preferred_element_type=F32)
                gbuf[pair, :, pl.ds(at, TILE)] = gate.astype(BF16)
                gbuf[pair, :, pl.ds(FF + at, TILE)] = up.astype(BF16)
                zbuf[pair, :, pl.ds(at, TILE)] = (gate / (1.0 + jnp.exp(-gate)) * up).astype(BF16)
            return 0

        lax.fori_loop(0, FF // TILE, middle, 0)
        if backward:
            pltpu.make_async_copy(gbuf.at[pair], grad_save.at[pair], save_sem.at[1, pair]).start()
        else:
            pltpu.make_async_copy(gbuf.at[pair], gate_up.at[pair], save_sem.at[1, pair]).start()
            pltpu.make_async_copy(zbuf.at[pair], hidden.at[pair], save_sem.at[2, pair]).start()

        def last(step, _):
            half = step // (HALF // TILE)
            at = pl.multiple_of(step * TILE, TILE)
            inside = pl.multiple_of((step % (HALF // TILE)) * TILE, TILE)
            if backward:
                result = lax.dot_general(
                    gbuf[pair],
                    win_v[pl.ds(at, TILE), :],
                    (((1,), (1,)), ((), ())),
                    preferred_element_type=F32,
                )
            else:
                result = jnp.dot(
                    zbuf[pair], wdown_v[:, pl.ds(at, TILE)], preferred_element_type=F32
                )
            ybuf[pair, half, :, :, pl.ds(inside, TILE)] = result.astype(BF16).reshape(
                plan.sources, slots, TILE
            )

            @pl.when(step % (HALF // TILE) == HALF // TILE - 1)
            def _():
                for source in range(plan.sources):
                    here, copy = return_copy(block, half, source)

                    @pl.when(here)
                    def _():
                        pltpu.make_async_copy(
                            ybuf.at[pair, half, source],
                            rbuf.at[block, half, own_expert],
                            back_recv.at[block, half, own_expert],
                        ).start()

                    @pl.when(jnp.logical_not(here))
                    def _():
                        copy.start()

            return 0

        lax.fori_loop(0, D // TILE, last, 0)

    def stage_take(index):
        block = nearest(z, index, nz)
        origin = ((block < z) & (z == nz - 1)) | ((block > z) & (z == 0))
        for half in range(2):
            for expert in range(EXP_DEV):
                landed(rbuf.at[block, half, expert], back_recv.at[block, half, expert])
            got = lax.dot_general(
                take[block],
                rbuf[block, half].reshape(EXP_DEV * slots, HALF),
                (((0,), (0,)), ((), ())),
                preferred_element_type=F32,
            )

            @pl.when(block == z)
            def _():
                at = pl.ds(half * HALF, HALF)
                if backward:
                    out[:, at] = got
                else:
                    out[:, at] = base[:, at] + got

            @pl.when(block != z)
            def _():
                pbuf[block, half] = got.astype(BF16)

            @pl.when(origin)
            def _():
                sum_copy(block, half).start()

    def relay(turn):
        lower = z < nz // 2
        first = jnp.where(lower, nz - 1 - z, z)
        early = turn < first
        ahead = jnp.where(early, turn + 1, turn - first + 1)
        rightward = lower == early
        block = jnp.where(rightward, z + ahead, z - ahead)

        @pl.when((z > 0) & (z < nz - 1))
        def _():
            for half in range(2):
                landed(qbuf.at[block, half], sum_recv.at[block, half])
                pbuf[block, half] = (
                    pbuf[block, half].astype(F32) + qbuf[block, half].astype(F32)
                ).astype(BF16)
                sum_copy(block, half).start()

    def body(index, _):
        @pl.when(index < nz)
        def _():
            stage_put(index)

        @pl.when(index == 1)
        def _():
            load_in.wait()
            load_down.wait()
            if backward:
                load_gate.wait()

        before = nearest(z, jnp.clip(index - 1, 0, nz - 1), nz)

        @pl.when((index >= 1) & (index < nz + 1) & (before % 2 == own_turn))
        def _():
            stage_expert(index - 1)

        @pl.when(index == nz + 1)
        def _():
            relay(0)

        @pl.when(index >= 2)
        def _():
            stage_take(index - 2)

        return 0

    lax.fori_loop(0, nz + 2, body, 0)

    def onward(turn, _):
        relay(turn)
        return 0

    lax.fori_loop(1, nz - 1, onward, 0)
    for half in range(2):
        at = pl.ds(half * HALF, HALF)

        @pl.when(z + 1 < nz)
        def _():
            landed(qbuf.at[z, half], sum_recv.at[z, half])
            out[:, at] += qbuf[z, half].astype(F32)

        @pl.when(z > 0)
        def _():
            landed(qbuf.at[nz, half], sum_recv.at[nz, half])
            out[:, at] += qbuf[nz, half].astype(F32)

    def drain(block, _):
        for piece in range(plan.micro):

            @pl.when((block <= z) & (z + 1 < nz))
            def _():
                along(block, piece, 1, False).wait_send()

            @pl.when((block >= z) & (z > 0))
            def _():
                along(block, piece, -1, False).wait_send()

        for expert in range(EXP_DEV):
            here, copy = dispatch_copy(block, expert)

            @pl.when(jnp.logical_not(here))
            def _():
                copy.wait_send()

        @pl.when(block % 2 == own_turn)
        def _():
            for half in range(2):
                for source in range(plan.sources):
                    here, copy = return_copy(block, half, source)

                    @pl.when(jnp.logical_not(here))
                    def _():
                        copy.wait_send()

        @pl.when(block != z)
        def _():
            for half in range(2):
                sum_copy(block, half).wait_send()

        return 0

    lax.fori_loop(0, nz, drain, 0)
    for pair in range(plan.blocks):
        pltpu.make_async_copy(xbuf.at[pair], sent_save.at[pair], save_sem.at[0, pair]).wait()
        if backward:
            pltpu.make_async_copy(gbuf.at[pair], grad_save.at[pair], save_sem.at[1, pair]).wait()
        else:
            pltpu.make_async_copy(gbuf.at[pair], gate_up.at[pair], save_sem.at[1, pair]).wait()
            pltpu.make_async_copy(zbuf.at[pair], hidden.at[pair], save_sem.at[2, pair]).wait()


def moe_call(plan, backward, collective_id, rows_in, put, take, w_in, w_down, last):
    nz, blocks, slots, many, sources = plan.nz, plan.blocks, plan.slots, plan.many, plan.sources
    vmem = pl.BlockSpec(memory_space=pltpu.VMEM)
    hbm = pl.BlockSpec(memory_space=pltpu.HBM)
    saved = (blocks, sources, slots, D)
    shape = jax.ShapeDtypeStruct
    outs = [shape((plan.rows, D), F32), shape(saved, BF16), shape((blocks, many, 2 * FF), BF16)]
    if not backward:
        outs.append(shape((blocks, many, FF), BF16))
    return pl.pallas_call(
        functools.partial(moe_kernel, plan, backward),
        out_shape=outs,
        in_specs=[vmem, vmem, vmem, hbm, hbm, hbm if backward else vmem],
        out_specs=[vmem] + [hbm] * (len(outs) - 1),
        scratch_shapes=[
            pltpu.VMEM((nz, plan.rows, D), BF16),
            pltpu.VMEM((nz, EXP_DEV, slots, D), BF16),
            pltpu.VMEM(saved, BF16),
            pltpu.VMEM((blocks, 2, sources, slots, HALF), BF16),
            pltpu.VMEM((nz, 2, EXP_DEV, slots, HALF), BF16),
            pltpu.VMEM((nz, 2, plan.rows, HALF), BF16),
            pltpu.VMEM((nz + 1, 2, plan.rows, HALF), BF16),
            pltpu.VMEM((D, 2 * FF), BF16),
            pltpu.VMEM((FF, D), BF16),
            pltpu.VMEM((blocks, many, 2 * FF), BF16),
            pltpu.VMEM((blocks, many, FF), BF16),
            DMA((nz, plan.micro)),
            DMA((nz, plan.micro)),
            DMA((nz, plan.micro)),
            DMA((nz, EXP_DEV)),
            DMA((blocks, sources)),
            DMA((blocks, 2, sources)),
            DMA((nz, 2, EXP_DEV)),
            DMA((nz, 2)),
            DMA((nz + 1, 2)),
            DMA((4,)),
            DMA((3, blocks)),
        ],
        compiler_params=pltpu.CompilerParams(
            collective_id=collective_id, has_side_effects=True, vmem_limit_bytes=VMEM_LIMIT
        ),
        cost_estimate=pl.CostEstimate(
            flops=100_000_000_000, bytes_accessed=30_000_000, transcendentals=0
        ),
    )(rows_in, put, take, w_in, w_down, last)


def expert_spread(plan, ins, outs, send, recv, pass_send, pass_recv):
    x, z, s = me()
    nx, ns, group = plan.nx, plan.ns, plan.group
    rank = x * ns + s
    own_expert, own_part = rank // group, rank % group
    own = [(layer, k) for layer in range(nx) for k in range(ns // group)]

    def first(expert, which):
        to = expert * group + s % group
        return to == rank, remote(
            ins[which].at[expert],
            outs[which].at[x, s],
            send.at[expert, which],
            recv.at[x, s, which],
            (to // ns, z, to % ns),
        )

    def onward(layer, source, step, which):
        to = own_expert * group + (own_part + step) % group
        return remote(
            outs[which].at[layer, source],
            outs[which].at[layer, source],
            pass_send.at[layer, source, step - 1, which],
            pass_recv.at[layer, source, which],
            (to // ns, z, to % ns),
        )

    def start():
        for which in range(2):
            for expert in range(EXP_DEV):
                here, copy = first(expert, which)

                @pl.when(here)
                def _():
                    pltpu.make_async_copy(
                        ins[which].at[expert], outs[which].at[x, s], recv.at[x, s, which]
                    ).start()

                @pl.when(jnp.logical_not(here))
                def _():
                    copy.start()

    def pass_on():
        for layer, k in own:
            source = k * group + own_part
            for which in range(2):
                landed(outs[which].at[layer, source], recv.at[layer, source, which])
                for step in range(1, group):
                    onward(layer, source, step, which).start()

    def finish():
        for layer, k in own:
            for step in range(1, group):
                source = k * group + (own_part + step) % group
                for which in range(2):
                    landed(outs[which].at[layer, source], pass_recv.at[layer, source, which])
        for which in range(2):
            for expert in range(EXP_DEV):
                here, copy = first(expert, which)

                @pl.when(jnp.logical_not(here))
                def _():
                    copy.wait_send()

        for layer, k in own:
            source = k * group + own_part
            for which in range(2):
                for step in range(1, group):
                    onward(layer, source, step, which).wait_send()

    return start, pass_on, finish


def spread_scratch(plan):
    nx, ns, group = plan.nx, plan.ns, plan.group
    return [
        DMA((EXP_DEV, 2)),
        DMA((nx, ns, 2)),
        DMA((nx, ns, group - 1, 2)),
        DMA((nx, ns, 2)),
    ]


def spread_kernel(plan, *refs):
    greet_plane(plan)
    start, pass_on, finish = expert_spread(plan, refs[:2], refs[2:4], *refs[4:])
    start()
    pass_on()
    finish()


def spread_call(plan, collective_id, gate_up, down):
    hbm = pl.BlockSpec(memory_space=pltpu.HBM)
    outs = [
        jax.ShapeDtypeStruct((plan.nx, plan.ns) + part.shape[1:], BF16) for part in (gate_up, down)
    ]
    return pl.pallas_call(
        functools.partial(spread_kernel, plan),
        out_shape=outs,
        in_specs=[hbm, hbm],
        out_specs=[hbm, hbm],
        scratch_shapes=spread_scratch(plan),
        compiler_params=pltpu.CompilerParams(collective_id=collective_id, has_side_effects=True),
    )(gate_up, down)


def gather_kernel(plan, *refs):
    ins, wide_ins = refs[:2], refs[2:4]
    outs, wide_outs = refs[4:6], refs[6:8]
    line_recv, right, left, copy_sem, plane_recv, to_core, to_x, to_y, spare = refs[8:17]
    x, z, s = me()
    nz = plan.nz
    greet_plane(plan, along=True)
    start, pass_on, finish = expert_spread(plan, wide_ins, wide_outs, *refs[17:])
    size = ins[0].shape[0] // 2
    pieces = [(half, which) for which in range(2) for half in range(2)]
    core = (x, z, s + 1 - 2 * (s % 2))
    across_x = (1 - x, z, s)
    across_y = (x, z, (s + 2) % 4)

    def spot(layer, block, shard, half, which):
        return outs[which].at[layer, block, shard, pl.ds(half * size, size)]

    def along(block, step, half, which, own):
        place = spot(x, block, s, half, which)
        src = ins[which].at[pl.ds(half * size, size)] if own else place
        sem = right if step > 0 else left
        return remote(
            src, place, sem.at[block, half, which], line_recv.at[block, half, which], (x, z + step, s)
        )

    def passed(layer, block, shard, half, which, sem, to):
        place = spot(layer, block, shard, half, which)
        return remote(
            place,
            place,
            sem.at[layer, block, shard // 2, half, which],
            plane_recv.at[layer, block, shard, half, which],
            to,
        )

    def arrived(layer, block, shard, half, which):
        landed(
            spot(layer, block, shard, half, which), plane_recv.at[layer, block, shard, half, which]
        )

    for half, which in pieces:

        @pl.when(z + 1 < nz)
        def _():
            along(z, 1, half, which, True).start()

        @pl.when(z > 0)
        def _():
            along(z, -1, half, which, True).start()

        pltpu.make_async_copy(
            ins[which].at[pl.ds(half * size, size)],
            spot(x, z, s, half, which),
            copy_sem.at[half, which],
        ).start()
    for half, which in pieces:
        pltpu.make_async_copy(
            ins[which].at[pl.ds(half * size, size)],
            spot(x, z, s, half, which),
            copy_sem.at[half, which],
        ).wait()
    start()

    def column(index):
        block = nearest(z, index, nz)
        for half, which in pieces:

            @pl.when(block < z)
            def _():
                along(block, 1, half, which, False).wait_recv()

                @pl.when(z + 1 < nz)
                def _():
                    along(block, 1, half, which, False).start()

            @pl.when(block > z)
            def _():
                along(block, -1, half, which, False).wait_recv()

                @pl.when(z > 0)
                def _():
                    along(block, -1, half, which, False).start()

            passed(x, block, s, half, which, to_x, across_x).start()
            passed(x, block, s, half, which, to_y, across_y).start()
            passed(x, block, s, half, which, to_core, core).start()

    def neighbours(index):
        block = nearest(z, index, nz)
        over = (s + 2) % 4
        for half, which in pieces:
            arrived(1 - x, block, s, half, which)
            if half == 0:
                passed(1 - x, block, s, half, which, to_y, across_y).start()
            passed(1 - x, block, s, half, which, to_core, core).start()
            arrived(x, block, over, half, which)
            if half == 1:
                passed(x, block, over, half, which, to_x, across_x).start()
            passed(x, block, over, half, which, to_core, core).start()

    def opposite(index):
        block = nearest(z, index, nz)
        over = (s + 2) % 4
        for half, which in pieces:
            arrived(1 - x, block, over, half, which)
            passed(1 - x, block, over, half, which, to_core, core).start()

    def body(index, _):
        @pl.when(index < nz)
        def _():
            column(index)

        @pl.when((index >= 1) & (index < nz + 1))
        def _():
            neighbours(index - 1)

        @pl.when(index >= 2)
        def _():
            opposite(index - 2)

        return 0

    lax.fori_loop(0, nz + 2, body, 0)
    pass_on()

    def drain(block, _):
        other = s + 1 - 2 * (s % 2)
        over = (s + 2) % 4
        for half, which in pieces:
            for layer in range(2):
                for row in range(2):
                    arrived(layer, block, row * 2 + other % 2, half, which)
                    passed(layer, block, row * 2 + s % 2, half, which, to_core, core).wait_send()

            @pl.when((block <= z) & (z + 1 < nz))
            def _():
                along(block, 1, half, which, False).wait_send()

            @pl.when((block >= z) & (z > 0))
            def _():
                along(block, -1, half, which, False).wait_send()

            passed(x, block, s, half, which, to_x, across_x).wait_send()
            passed(x, block, s, half, which, to_y, across_y).wait_send()
            if half == 0:
                passed(1 - x, block, s, half, which, to_y, across_y).wait_send()
            else:
                passed(x, block, over, half, which, to_x, across_x).wait_send()
        return 0

    lax.fori_loop(0, nz, drain, 0)
    finish()


def gather_call(plan, collective_id, attention, experts):
    hbm = pl.BlockSpec(memory_space=pltpu.HBM)
    nx, nz, ns = plan.nx, plan.nz, plan.ns
    outs = [jax.ShapeDtypeStruct((nx, nz, ns) + part.shape, BF16) for part in attention]
    outs += [jax.ShapeDtypeStruct((nx, ns) + part.shape[1:], BF16) for part in experts]
    return pl.pallas_call(
        functools.partial(gather_kernel, plan),
        out_shape=outs,
        in_specs=[hbm] * 4,
        out_specs=[hbm] * 4,
        scratch_shapes=[
            DMA((nz, 2, 2)),
            DMA((nz, 2, 2)),
            DMA((nz, 2, 2)),
            DMA((2, 2)),
            DMA((nx, nz, ns, 2, 2)),
            DMA((nx, nz, 2, 2, 2)),
            DMA((nx, nz, 2, 2, 2)),
            DMA((nx, nz, 2, 2, 2)),
            DMA((1,)),
        ]
        + spread_scratch(plan),
        compiler_params=pltpu.CompilerParams(collective_id=collective_id, has_side_effects=True),
    )(*attention, *experts)


def expert_collect(plan, ins, outs, parts, stage, load, swap_send, swap_recv, send, recv):
    x, z, s = me()
    ns, group = plan.ns, plan.group
    rank = x * ns + s
    own_expert, own_part = rank // group, rank % group
    order = [(k, kind) for kind in range(len(ins)) for k in range(ns // group)]

    def swap(k, step, kind):
        part_to = (own_part + step) % group
        to = own_expert * group + part_to
        return remote(
            ins[kind].at[k * group + part_to],
            parts[kind].at[step - 1, k],
            swap_send.at[step - 1, k, kind],
            swap_recv.at[step - 1, k, kind],
            (to // ns, z, to % ns),
        )

    def own(k, kind):
        return pltpu.make_async_copy(
            ins[kind].at[k * group + own_part], stage[kind].at[k], load.at[k, kind]
        )

    def home(k, kind):
        layer, which = kind // 2, kind % 2
        here = (x == layer) & (s == k * group + own_part)
        return here, remote(
            stage[kind].at[k],
            outs[which].at[own_expert],
            send.at[k, kind],
            recv.at[own_expert, which],
            (layer, z, k * group + own_part),
        )

    def start():
        for k, kind in order:
            own(k, kind).start()
            for step in range(1, group):
                swap(k, step, kind).start()

    def add(place):
        k, kind = order[place]
        own(k, kind).wait()
        for step in range(1, group):
            swap(k, step, kind).wait_recv()
        total = stage[kind][k].astype(F32)
        for step in range(1, group):
            total += parts[kind][step - 1, k].astype(F32)
        stage[kind][k] = total.astype(BF16)
        here, copy = home(k, kind)

        @pl.when(here)
        def _():
            which = kind % 2
            pltpu.make_async_copy(
                stage[kind].at[k], outs[which].at[own_expert], recv.at[own_expert, which]
            ).start()

        @pl.when(jnp.logical_not(here))
        def _():
            copy.start()

    def finish():
        for which in range(2):
            for expert in range(EXP_DEV):
                landed(outs[which].at[expert], recv.at[expert, which])
        for k, kind in order:
            for step in range(1, group):
                swap(k, step, kind).wait_send()
            here, copy = home(k, kind)

            @pl.when(jnp.logical_not(here))
            def _():
                copy.wait_send()

    return len(order), start, add, finish


def collect_scratch(plan, values):
    group, each, kinds = plan.group, plan.ns // plan.group, len(values)
    return (
        [pltpu.VMEM((group - 1, each) + part.shape[1:], BF16) for part in values]
        + [pltpu.VMEM((each,) + part.shape[1:], BF16) for part in values]
        + [
            DMA((each, kinds)),
            DMA((group - 1, each, kinds)),
            DMA((group - 1, each, kinds)),
            DMA((each, kinds)),
            DMA((EXP_DEV, 2)),
        ]
    )


def collect_kernel(plan, *refs):
    kinds = 2 * plan.nx
    ins, outs = refs[:kinds], refs[kinds : kinds + 2]
    parts, stage = refs[kinds + 2 : 2 * kinds + 2], refs[2 * kinds + 2 : 3 * kinds + 2]
    greet_plane(plan)
    count, start, add, finish = expert_collect(
        plan, ins, outs, parts, stage, *refs[3 * kinds + 2 :]
    )
    start()
    for place in range(count):
        add(place)
    finish()


def collect_call(plan, collective_id, terms):
    ns = plan.ns
    hbm = pl.BlockSpec(memory_space=pltpu.HBM)
    values = [part.reshape(ns, part.shape[0] // ns, D) for layer in terms for part in layer]
    return pl.pallas_call(
        functools.partial(collect_kernel, plan),
        out_shape=[jax.ShapeDtypeStruct((EXP_DEV,) + part.shape[1:], BF16) for part in values[:2]],
        in_specs=[hbm] * len(values),
        out_specs=[hbm, hbm],
        scratch_shapes=collect_scratch(plan, values),
        compiler_params=pltpu.CompilerParams(
            collective_id=collective_id, has_side_effects=True, vmem_limit_bytes=VMEM_LIMIT
        ),
    )(*values)


def reduce_kernel(plan, *refs):
    grads, wide_ins = (refs[0:2], refs[2:4]), refs[4:8]
    outs, wide_outs = refs[8:10], refs[10:12]
    scratch = refs[12:]
    mine, given, x_one, y_one, y_two, x_two, chain = (scratch[2 * i : 2 * i + 2] for i in range(7))
    (
        load_sem,
        core_send,
        core_recv,
        x_one_send,
        x_one_recv,
        y_one_send,
        y_one_recv,
        x_two_send,
        x_two_recv,
        y_two_send,
        y_two_recv,
        chain_send,
        chain_recv,
    ) = scratch[14:27]
    parts, stage = scratch[27:31], scratch[31:35]
    x, z, s = me()
    nz = plan.nz
    row, side = s // 2, s % 2
    core = (x, z, s + 1 - 2 * side)
    across_x = (1 - x, z, s)
    across_y = (x, z, (s + 2) % 4)
    size = grads[0][0].shape[2] // 2
    greet_plane(plan, along=True)
    count, start, add, finish = expert_collect(plan, wide_ins, wide_outs, parts, stage, *scratch[35:])
    both = range(2)
    low, high = pl.ds(0, size), pl.ds(size, size)

    def load(layer, block, to_row, which):
        return pltpu.make_async_copy(
            grads[layer][which].at[block, to_row * 2 + side],
            mine[which].at[layer, block, to_row],
            load_sem.at[layer, block, to_row, which],
        )

    def give(layer, block, to_row, which):
        return remote(
            grads[layer][which].at[block, to_row * 2 + 1 - side],
            given[which].at[layer, block, to_row],
            core_send.at[layer, block, to_row, which],
            core_recv.at[layer, block, to_row, which],
            core,
        )

    def send_x_one(block, to_row, which):
        return remote(
            mine[which].at[1 - x, block, to_row, low],
            x_one[which].at[block, to_row],
            x_one_send.at[block, to_row, which],
            x_one_recv.at[block, to_row, which],
            across_x,
        )

    def send_y_one(layer, block, which):
        return remote(
            mine[which].at[layer, block, 1 - row, high],
            y_one[which].at[layer, block],
            y_one_send.at[layer, block, which],
            y_one_recv.at[layer, block, which],
            across_y,
        )

    def send_y_two(block, which):
        return remote(
            mine[which].at[x, block, 1 - row, low],
            y_two[which].at[block],
            y_two_send.at[block, which],
            y_two_recv.at[block, which],
            across_y,
        )

    def send_x_two(block, which):
        return remote(
            mine[which].at[1 - x, block, row, high],
            x_two[which].at[block],
            x_two_send.at[block, which],
            x_two_recv.at[block, which],
            across_x,
        )

    def send_chain(block, which):
        rightward = (block > z).astype(jnp.int32)
        to = z - 1 + 2 * rightward
        into = jnp.where((rightward == 1) & (block == to), nz, block)
        return remote(
            mine[which].at[x, block, row],
            chain[which].at[into],
            chain_send.at[block, which],
            chain_recv.at[into, which],
            (x, to, s),
        )

    def gain(target, at, other):
        target[at] = (target[at].astype(F32) + other.astype(F32)).astype(BF16)

    def begin(index, _):
        block = nearest(z, nz - 1 - index, nz)
        for which in both:
            for layer in both:
                for to_row in both:
                    load(layer, block, to_row, which).start()
                    give(layer, block, to_row, which).start()
        return 0

    def stage_core(index):
        block = nearest(z, nz - 1 - index, nz)
        for which in both:
            for layer in both:
                for to_row in both:
                    load(layer, block, to_row, which).wait()
                    give(layer, block, to_row, which).wait_recv()
                    gain(mine[which], (layer, block, to_row), given[which][layer, block, to_row])
            for to_row in both:
                send_x_one(block, to_row, which).start()
            for layer in both:
                send_y_one(layer, block, which).start()

    def stage_first(index):
        block = nearest(z, nz - 1 - index, nz)
        for which in both:
            for to_row in both:
                send_x_one(block, to_row, which).wait_recv()
                gain(mine[which], (x, block, to_row, low), x_one[which][block, to_row])
            send_y_two(block, which).start()
            for layer in both:
                send_y_one(layer, block, which).wait_recv()
                gain(mine[which], (layer, block, row, high), y_one[which][layer, block])
            send_x_two(block, which).start()

    def stage_second(index):
        block = nearest(z, nz - 1 - index, nz)
        origin = ((block < z) & (z == nz - 1)) | ((block > z) & (z == 0))
        for which in both:
            send_y_two(block, which).wait_recv()
            gain(mine[which], (x, block, row, low), y_two[which][block])
            send_x_two(block, which).wait_recv()
            gain(mine[which], (x, block, row, high), x_two[which][block])

            @pl.when(origin)
            def _():
                send_chain(block, which).start()

    start()
    lax.fori_loop(0, nz, begin, 0)
    each = -(-count // nz)

    for index in range(nz + 2):
        if index < nz:
            stage_core(index)
            for place in range(index * each, min(count, (index + 1) * each)):
                add(place)
        if 1 <= index < nz + 1:
            stage_first(index - 1)
        if index >= 2:
            stage_second(index - 2)

    def relay(turn, _):
        lower = z < nz // 2
        first = jnp.where(lower, nz - 1 - z, z)
        early = turn < first
        ahead = jnp.where(early, first - turn, nz - 1 - turn)
        rightward = lower == early
        block = jnp.where(rightward, z + ahead, z - ahead)

        @pl.when((z > 0) & (z < nz - 1))
        def _():
            for which in both:
                landed(chain[which].at[block], chain_recv.at[block, which])
                gain(mine[which], (x, block, row), chain[which][block])
                send_chain(block, which).start()

        return 0

    lax.fori_loop(0, nz - 1, relay, 0)
    for which in both:
        outs[which][...] = mine[which][x, z, row].astype(F32)

        @pl.when(z + 1 < nz)
        def _():
            landed(chain[which].at[z], chain_recv.at[z, which])
            outs[which][...] += chain[which][z].astype(F32)

        @pl.when(z > 0)
        def _():
            landed(chain[which].at[nz], chain_recv.at[nz, which])
            outs[which][...] += chain[which][nz].astype(F32)

    def drain(block, _):
        for which in both:
            for layer in both:
                for to_row in both:
                    give(layer, block, to_row, which).wait_send()
                send_y_one(layer, block, which).wait_send()
            for to_row in both:
                send_x_one(block, to_row, which).wait_send()
            send_y_two(block, which).wait_send()
            send_x_two(block, which).wait_send()

            @pl.when(block != z)
            def _():
                send_chain(block, which).wait_send()

        return 0

    lax.fori_loop(0, nz, drain, 0)
    finish()


def reduce_call(plan, collective_id, attention, terms):
    nx, nz, ns = plan.nx, plan.nz, plan.ns
    hbm = pl.BlockSpec(memory_space=pltpu.HBM)
    vmem = pl.BlockSpec(memory_space=pltpu.VMEM)
    grads = [part.reshape(nz, ns, -1, part.shape[1]) for layer in attention for part in layer]
    values = [part.reshape(ns, part.shape[0] // ns, D) for layer in terms for part in layer]
    sizes = [part.shape[2:] for part in grads[:2]]
    halves = [(rows // 2, width) for rows, width in sizes]
    return pl.pallas_call(
        functools.partial(reduce_kernel, plan),
        out_shape=[jax.ShapeDtypeStruct(size, F32) for size in sizes]
        + [jax.ShapeDtypeStruct((EXP_DEV,) + part.shape[1:], BF16) for part in values[:2]],
        in_specs=[hbm] * 8,
        out_specs=[vmem, vmem, hbm, hbm],
        scratch_shapes=[pltpu.VMEM((nx, nz, 2) + size, BF16) for size in sizes]
        + [pltpu.VMEM((nx, nz, 2) + size, BF16) for size in sizes]
        + [pltpu.VMEM((nz, 2) + size, BF16) for size in halves]
        + [pltpu.VMEM((nx, nz) + size, BF16) for size in halves]
        + [pltpu.VMEM((nz,) + size, BF16) for size in halves]
        + [pltpu.VMEM((nz,) + size, BF16) for size in halves]
        + [pltpu.VMEM((nz + 1,) + size, BF16) for size in sizes]
        + [
            DMA((nx, nz, 2, 2)),
            DMA((nx, nz, 2, 2)),
            DMA((nx, nz, 2, 2)),
            DMA((nz, 2, 2)),
            DMA((nz, 2, 2)),
            DMA((nx, nz, 2)),
            DMA((nx, nz, 2)),
            DMA((nz, 2)),
            DMA((nz, 2)),
            DMA((nz, 2)),
            DMA((nz, 2)),
            DMA((nz, 2)),
            DMA((nz + 1, 2)),
        ]
        + collect_scratch(plan, values),
        compiler_params=pltpu.CompilerParams(
            collective_id=collective_id, has_side_effects=True, vmem_limit_bytes=VMEM_LIMIT
        ),
    )(*grads, *values)


def rotate(values, cosine, sine_table):
    width_half = values.shape[-1] // 2
    first_part = values[..., :width_half]
    second_part = values[..., width_half:]
    return jnp.concatenate(
        [
            first_part * cosine - second_part * sine_table,
            second_part * cosine + first_part * sine_table,
        ],
        axis=-1,
    )


def norm_forward(hidden, gain_row):
    inverse = lax.rsqrt(jnp.mean(hidden * hidden, axis=-1, keepdims=True) + epsilon)
    return (hidden * inverse * gain_row, inverse)


def norm_backward(hidden, inverse, gain_row, grad_normed):
    scaled = grad_normed * gain_row
    gain_term = jnp.sum(grad_normed * hidden * inverse, axis=0)
    row_inner = jnp.mean(scaled * hidden, axis=-1, keepdims=True)
    return (inverse * scaled - hidden * inverse * inverse * inverse * row_inner, gain_term)


def slot_tables(plan, routes, gates):
    experts, nz = plan.experts, plan.nz
    named = routes[..., None] == jnp.arange(experts, dtype=jnp.int32)
    gate = jnp.sum(jnp.where(named, gates[..., None], 0.0), axis=2)
    named = jnp.any(named, axis=2)
    earlier = jnp.tril(jnp.ones((plan.tokens, plan.tokens), BF16), -1)
    rank = jnp.einsum("ut,mte->mue", earlier, named.astype(BF16), preferred_element_type=F32)
    table = jnp.stack([jnp.where(named, rank, -1.0), gate])
    table = table.reshape(2, plan.micro, plan.tokens, nz, EXP_DEV).transpose(3, 0, 1, 4, 2)
    table = lax.all_to_all(table, "expert", split_axis=0, concat_axis=0, tiled=True)
    rank, gate = table[:, 0], table[:, 1]
    first = jnp.arange(plan.micro, dtype=F32)[:, None, None] * plan.capacity
    place = jnp.where(rank >= 0, rank + first, -1.0).transpose(0, 2, 1, 3)
    hit = place[:, :, None] == jnp.arange(plan.slots, dtype=F32)[:, None, None]
    shape = (nz, EXP_DEV * plan.slots, plan.rows)
    one = hit.astype(BF16).reshape(shape)
    weighted = jnp.where(hit, gate.transpose(0, 2, 1, 3)[:, :, None], 0.0)
    weighted = weighted.astype(BF16).reshape(shape)
    return one, weighted


def shards(
    inputs,
    segments,
    routes,
    gate_weights,
    query_weight,
    key_value_weight,
    output_weight,
    norm_gains,
    expert_gate_up,
    expert_down,
    cotangent,
):
    section = lax.axis_index("section")
    shard_index = lax.axis_index("shard")
    tokens = inputs.shape[1]
    plan = Plan((lax.axis_size("section"), lax.axis_size("expert"), lax.axis_size("shard")), tokens)
    micro, rows, layers = plan.micro, plan.rows, plan.nx
    length = tokens * plan.ns

    def mine(value):
        return lax.dynamic_slice_in_dim(value, section * micro, micro, 0)

    paired = plan.nx == 2 and plan.ns == 4 and query_weight.shape[1] % 32 == 0
    gain_columns = jnp.pad(norm_gains[0].T, ((0, 0), (0, 126)))
    attention_weights = (
        jnp.concatenate([query_weight[0], key_value_weight[0], gain_columns], axis=1).astype(BF16),
        output_weight[0].astype(BF16),
    )
    expert_weights = (expert_gate_up[0].astype(BF16), expert_down[0].astype(BF16))
    if paired:
        weight_in, weight_o, wide_in, wide_down = gather_call(
            plan, 1, attention_weights, expert_weights
        )
    else:
        weight_in, weight_o = (
            lax.all_gather(part, ("section", "expert", "shard"), axis=0, tiled=True)
            for part in attention_weights
        )
        wide_in, wide_down = spread_call(plan, 1, *expert_weights)
    weight_in = weight_in.reshape(layers, D, -1)
    weight_o = weight_o.reshape(layers, WQ, D)
    gains = weight_in[:, :, WQ + 2 * WK : WQ + 2 * WK + 2].transpose(0, 2, 1).astype(F32)
    wide_in = wide_in.reshape(layers, D, 2 * FF)
    wide_down = wide_down.reshape(layers, FF, D)
    one, weighted = slot_tables(plan, mine(routes), mine(gate_weights))

    offset = shard_index * tokens
    position = (offset + jnp.arange(tokens, dtype=jnp.int32)).astype(F32)
    frequency = rope_base ** (-jnp.arange(HD // 2, dtype=F32) / (HD // 2))
    angles = position[:, None] * frequency[None, :]
    cosine = jnp.cos(angles)[:, None, :]
    sine_table = jnp.sin(angles)[:, None, :]
    segment_all = mine(segments)[:, 0]
    segment_own = lax.dynamic_slice_in_dim(segment_all, offset, tokens, 1)
    query_place = offset + jnp.arange(tokens, dtype=jnp.int32)
    key_place = jnp.arange(length, dtype=jnp.int32)
    allowed = (segment_own[:, :, None] == segment_all[:, None, :]) & (
        query_place[:, None] >= key_place[None, :]
    )
    allowed = jnp.tile(allowed, (1, GROUP, 1))[:, None]

    def stack_heads(values):
        return (
            values.reshape(micro, tokens, KV_HEADS, GROUP, HD)
            .transpose(0, 2, 3, 1, 4)
            .reshape(micro, KV_HEADS, GROUP * tokens, HD)
        )

    def unstack_heads(values):
        return (
            values.reshape(micro, KV_HEADS, GROUP, tokens, HD)
            .transpose(0, 3, 1, 2, 4)
            .reshape(micro, tokens, HEADS, HD)
        )

    def split_kv(all_kv):
        key_rows = all_kv[..., :WK].reshape(micro, length, KV_HEADS, HD)
        value_rows = all_kv[..., WK:].reshape(micro, length, KV_HEADS, HD)
        return key_rows, value_rows

    def score(stacked, key_rows):
        raw = jnp.einsum("mhqd,mkhd->mhqk", stacked, key_rows, preferred_element_type=F32)
        return jnp.where(allowed, raw * SCALE, -1e30)

    def attend_forward(layer, start):
        normed, inverse = norm_forward(start, gains[layer, 0])
        low = normed.astype(BF16)
        projected = jnp.dot(low, weight_in[layer], preferred_element_type=F32)
        queries, keys_values = projected[:, :WQ], projected[:, WQ : WQ + 2 * WK]
        queries_low = rotate(
            queries.reshape(micro, tokens, HEADS, HD), cosine, sine_table
        ).astype(BF16)
        key_rot = rotate(
            keys_values[:, :WK].reshape(micro, tokens, KV_HEADS, HD), cosine, sine_table
        ).reshape(rows, WK)
        local_kv = jnp.concatenate([key_rot, keys_values[:, WK:]], axis=1).astype(BF16)
        local_kv = local_kv.reshape(micro, tokens, 2 * WK)
        all_kv = jnp.stack(
            [lax.all_gather(local_kv[i], "shard", axis=0, tiled=True) for i in range(micro)]
        )
        stacked = stack_heads(queries_low)
        key_rows, value_rows = split_kv(all_kv)
        scores = score(stacked, key_rows)
        row_max = jnp.max(scores, axis=-1, keepdims=True)
        weights = jnp.exp(scores - row_max)
        row_sum = jnp.sum(weights, axis=-1, keepdims=True)
        probs = (weights / row_sum).astype(BF16)
        mixed = jnp.einsum("mhqk,mkhd->mhqd", probs, value_rows, preferred_element_type=F32)
        mixed_low = unstack_heads(mixed.astype(BF16)).reshape(rows, WQ)
        middle = start + jnp.dot(mixed_low, weight_o[layer], preferred_element_type=F32)
        return middle, (start, inverse, low, stacked, all_kv, row_max, row_sum, mixed_low)

    def attend_backward(layer, saved, grad_middle):
        start, inverse, low, stacked, all_kv, row_max, row_sum, mixed_low = saved
        branch = grad_middle.astype(BF16)
        out_term = jnp.einsum("tq,td->qd", mixed_low, branch, preferred_element_type=F32)
        out_term = out_term.astype(BF16)
        grad_mixed = jnp.einsum(
            "td,qd->tq", branch, weight_o[layer], preferred_element_type=F32
        ).astype(BF16)
        grad_stacked = stack_heads(grad_mixed)
        key_rows, value_rows = split_kv(all_kv)
        scores = score(stacked, key_rows)
        probs = jnp.exp(scores - row_max) / row_sum
        grad_probs = jnp.einsum(
            "mhqd,mkhd->mhqk", grad_stacked, value_rows, preferred_element_type=F32
        )
        inner = jnp.sum(grad_probs * probs, axis=-1, keepdims=True)
        grad_raw = (probs * (grad_probs - inner) * SCALE).astype(BF16)
        grad_queries = jnp.einsum(
            "mhqk,mkhd->mhqd", grad_raw, key_rows, preferred_element_type=F32
        )
        grad_keys = jnp.einsum("mhqk,mhqd->mkhd", grad_raw, stacked, preferred_element_type=F32)
        grad_values = jnp.einsum(
            "mhqk,mhqd->mkhd", probs.astype(BF16), grad_stacked, preferred_element_type=F32
        )
        partial = jnp.concatenate(
            [grad_keys.reshape(micro, length, WK), grad_values.reshape(micro, length, WK)], axis=2
        ).astype(BF16)
        grad_kv = jnp.concatenate(
            [
                lax.psum_scatter(partial[i], "shard", scatter_dimension=0, tiled=True)
                for i in range(micro)
            ]
        ).astype(F32)
        grad_q_low = (
            rotate(unstack_heads(grad_queries), cosine, -sine_table).reshape(rows, WQ).astype(BF16)
        )
        grad_k = rotate(
            grad_kv[:, :WK].reshape(micro, tokens, KV_HEADS, HD), cosine, -sine_table
        ).reshape(rows, WK)
        grad_kv_low = jnp.concatenate([grad_k, grad_kv[:, WK:]], axis=1).astype(BF16)
        both = jnp.concatenate([grad_q_low, grad_kv_low], axis=1)
        in_term = jnp.einsum("td,tq->dq", low, both, preferred_element_type=F32).astype(BF16)
        grad_normed = jnp.einsum(
            "tq,dq->td", both, weight_in[layer, :, : WQ + 2 * WK], preferred_element_type=F32
        )
        grad_from, gain_term = norm_backward(start, inverse, gains[layer, 0], grad_normed)
        return grad_middle + grad_from, (in_term, out_term, gain_term)

    def gathered(in_term, out_term, gain_term):
        columns = jnp.pad(gain_term.T, ((0, 0), (0, 126))).astype(BF16)
        return jnp.concatenate([in_term, columns], axis=1), out_term

    hidden = mine(inputs).reshape(rows, D).astype(F32)
    kept = []
    for layer in range(layers):
        if layer > 0:
            hidden = hidden.astype(BF16).astype(F32)
        middle, saved = attend_forward(layer, hidden)
        normed, inverse = norm_forward(middle, gains[layer, 1])
        hidden, sent, gate_up, hidden_low = moe_call(
            plan,
            False,
            2 + layer,
            normed.astype(BF16),
            one,
            weighted,
            wide_in[layer],
            wide_down[layer],
            middle,
        )
        kept.append((saved, middle, inverse, sent, gate_up, hidden_low))
    output = hidden.reshape(micro, tokens, D)

    grad = mine(cotangent).reshape(rows, D)
    attention_terms = [None] * layers
    expert_terms = [None] * layers
    for layer in reversed(range(layers)):
        saved, middle, inverse, sent, gate_up, hidden_low = kept[layer]
        grad_low = grad.astype(BF16)
        grad_out = grad_low.astype(F32)
        grad_moe, grad_sent, grad_both = moe_call(
            plan,
            True,
            2 + layers + layer,
            grad_low,
            weighted,
            one,
            wide_in[layer],
            wide_down[layer],
            gate_up,
        )
        in_term = jnp.einsum(
            "rd,rf->df",
            sent.reshape(-1, D),
            grad_both.reshape(-1, 2 * FF),
            preferred_element_type=F32,
        ).astype(BF16)
        down_term = jnp.einsum(
            "rf,rd->fd",
            hidden_low.reshape(-1, FF),
            grad_sent.reshape(-1, D),
            preferred_element_type=F32,
        ).astype(BF16)
        expert_terms[layer] = (in_term, down_term)
        grad_from, gain_two = norm_backward(middle, inverse, gains[layer, 1], grad_moe)
        grad, terms = attend_backward(layer, saved, grad_out + grad_from)
        attention_terms[layer] = gathered(
            terms[0], terms[1], jnp.stack([terms[2], gain_two])
        )
    input_grad = grad.reshape(micro, tokens, D)

    if paired:
        in_grad, output_weight_grad, gate_up_grad, down_grad = reduce_call(
            plan, 2 + 2 * layers, attention_terms, expert_terms
        )
    else:
        gate_up_grad, down_grad = collect_call(plan, 2 + 2 * layers, expert_terms)
        in_grad, output_weight_grad = (
            lax.psum_scatter(
                jnp.concatenate([terms[i] for terms in attention_terms]),
                ("section", "expert", "shard"),
                scatter_dimension=0,
                tiled=True,
            )
            for i in range(2)
        )
    query_grad, key_value_grad, gain_grad, output_weight_grad, gate_up_grad, down_grad = (
        part.astype(F32)[None]
        for part in (
            in_grad[:, :WQ],
            in_grad[:, WQ : WQ + 2 * WK],
            in_grad[:, WQ + 2 * WK : WQ + 2 * WK + 2].T,
            output_weight_grad,
            gate_up_grad,
            down_grad,
        )
    )
    return (
        output,
        input_grad,
        query_grad,
        key_value_grad,
        output_weight_grad,
        gain_grad,
        gate_up_grad,
        down_grad,
    )


def solution(mesh):
    placed = (
        P(None, ("expert", "shard"), None),
        P(None, "expert", None),
        P(None, ("expert", "shard"), None),
        P(None, ("expert", "shard"), None),
        P("section", ("expert", "shard"), None),
        P("section", ("expert", "shard"), None),
        P("section", ("expert", "shard"), None),
        P("section", None, ("expert", "shard")),
        P("section", "expert", "shard", None),
        P("section", "expert", "shard", None),
        P(None, ("expert", "shard"), None),
    )
    return jax.shard_map(
        shards,
        mesh=mesh,
        in_specs=placed,
        out_specs=(
            P("section", ("expert", "shard"), None),
            P("section", ("expert", "shard"), None),
            P("section", ("expert", "shard"), None),
            P("section", ("expert", "shard"), None),
            P("section", ("expert", "shard"), None),
            P("section", None, ("expert", "shard")),
            P("section", "expert", "shard", None),
            P("section", "expert", "shard", None),
        ),
        check_vma=False,
    )
```

time: 1680 us -> 1460 us (0.87)
  waiting for transfers between devices: 234 us -> 30.2 us
  blocking collectives: 118 us -> 30.2 us
  Pallas kernels: 951 us -> 1030 us
  local copies, waits for them, and re-layouts: 69.1 us -> 92.6 us
  matrix products: 185 us -> 163 us
    pallas_call x3 -> x2, Pallas kernels: 297 us -> 428 us  [the longest x1 217 us: reduce_call(): pl.pallas_call(functools.partial(reduce_kernel, plan), out_shape=[jax.Sha...]
    reduce_scatter x3 -> x0, waiting for transfers between devices: 106 us -> none  [scattered(): lax.psum_scatter(both, everywhere, scatter_dimension=0, tiled=True)]
    unnamed x14 -> x8, waiting for transfers between devices: 98.6 us -> 30.2 us
    pallas_call x4, Pallas kernels: 653 us -> 605 us  [moe_call(): pl.pallas_call(functools.partial(moe_kernel, plan, backward), out_shape=o...]
    all_gather x1 -> x0, blocking collectives: 41.8 us -> none  [shards(): lax.all_gather(norm_gains.astype(BF16), everywhere, axis=0, tiled=True)]
    unnamed x1 -> x0, blocking collectives: 39.5 us -> none
    all_gather x3 -> x0, waiting for transfers between devices: 29.8 us -> none  [the longest x1 29.8 us: shards(): lax.all_gather(output_weight[0].astype(BF16), everywhere, axis=0, tiled=T...]
    slice x1 -> x6, local copies, waits for them, and re-layouts: 0.12 us -> 20.4 us  [the longest x1 10.6 us: attend_forward(): projected = jnp.dot(low, weight_in[layer], preferred_element_type=F32)]
  transfers between devices with their start and end apart: 11 -> 5, of which waited for: 6 -> 2; matrix products, arithmetic and copies ran while one was open for 12% -> 10% of each run, Pallas kernels for 18% -> 15%
where the time goes in v2:
time: 1460 us; the launch traced here: 1440 us
  Pallas kernels  1030 us (71%)
  matrix products  163 us (11%)
  local copies, waits for them, and re-layouts  92.6 us (6%)
  other arithmetic  73 us (5%)
  blocking collectives  30.2 us (2%)
  waiting for transfers between devices  30.2 us (2%)
  between operations  15.6 us (1%)
    pallas_call x4, Pallas kernels, moe_call(): pl.pallas_call(functools.partial(moe_kernel, plan, backward), out_shape=o...  605 us
    pallas_call x1, Pallas kernels, reduce_call(): pl.pallas_call(functools.partial(reduce_kernel, plan), out_shape=[jax.Sha...  217 us
    pallas_call x1, Pallas kernels, gather_call(): pl.pallas_call(functools.partial(gather_kernel, plan), out_shape=outs, in...  211 us
    unnamed x214, local copies, waits for them, and re-layouts  30.8 us
    unnamed x8, waiting for transfers between devices  30.2 us
    all_gather x4, blocking collectives, attend_forward(): lax.all_gather(local_kv[i], 'shard', axis=0, tiled=True)  30.2 us
  transfers between devices with their start and end apart: 5, of which 2 were waited for; matrix products, arithmetic and copies ran while one was open for 10% of the time, Pallas kernels for 15%

profile of v2, /device:TPU:0, one launch (start us, length us, event | category | flops | bytes accessed | tf_op | source)
XLA Modules:
  0.0 1444.9 jit_solution(17430213683499854382)
XLA Ops:
  9.5 6.3 all-to-all-start
  17.9 6.5 convert_bitcast_fusion.refs_2_
  24.5 1.7 convert_bitcast_fusion.1.refs_3_
  27.9 211.2 %shard_map.170 = (bf16[2,4,4,96,2176]{4,3,2,1,0:T(8,128)(2,1)}, bf16[2,4,4,96,1536]{4,3,2,1,0:T(8,128)(2,1)}, bf16[2,4,384,1536]{3,2,1,0:T(8,128)(2,1)}, bf16[2,4,192,1536]{3,2,1,0:T(8,128)(2,1)}) custom-call(bf16[96,2176]{1,0:T(8,128)(2,1)} %fusion.151.refs_0_, bf16[96,1536]{1,0:T(8,128)(2,1)} %convert_bitcast_fusion.2.refs_1_, ...), custom_call_target="tpu_custom_call" | custom-call | tf_op jit(solution)/shard_map/pallas_call | solution.py:789
  239.1 10.6 fusion.203
  252.5 4.9 fusion.221
  259.1 7.8 all_gather.12
  266.9 7.7 all_gather.13
  278.9 2.0 copy.232
  281.1 6.8 fusion.211
  288.0 5.1 fusion.77
  293.0 2.3 copy.244
  295.3 2.5 dynamic-slice_convert_fusion
  297.9 8.5 fusion.205
  306.4 4.0 multiply_reduce_fusion.7
  310.4 8.7 fusion.204
  319.1 2.4 fusion.206
  327.9 153.4 %shard_map.171 = (f32[256,1536]{1,0:T(8,128)}, bf16[2,8,80,1536]{3,2,1,0:T(8,128)(2,1)}, bf16[2,640,1536]{2,1,0:T(8,128)(2,1)}, bf16[2,640,768]{2,1,0:T(8,128)(2,1)}) custom-call(bf16[256,1536]{1,0:T(8,128)(2,1)} %multiply_convert_fusion.3.refs_0_, bf16[4,320,256]{2,1,0:T(8,128)(2,1)} %convert_element_type.182.refs_1_.refs_2_, ...), custom_call_target="tpu_custom_call" | custom-call | flops 99999997952 | bytes 30000000 | tf_op jit(solution)/shard_map/pallas_call | solution.py:486
  483.8 5.0 fusion.167
  494.3 7.2 all_gather.14
  501.5 7.5 all_gather.15
  509.9 6.4 fusion.216
  516.3 4.1 fusion.80
  521.1 4.1 multiply_reduce_fusion.6
  526.6 150.6 %shard_map.172 = (f32[256,1536]{1,0:T(8,128)}, bf16[2,8,80,1536]{3,2,1,0:T(8,128)(2,1)}, bf16[2,640,1536]{2,1,0:T(8,128)(2,1)}, bf16[2,640,768]{2,1,0:T(8,128)(2,1)}) custom-call(bf16[256,1536]{1,0:T(8,128)(2,1)} %multiply_convert_fusion.2.refs_0_, bf16[4,320,256]{2,1,0:T(8,128)(2,1)} %convert_element_type.182.refs_1_.refs_2_, ...), custom_call_target="tpu_custom_call" | custom-call | flops 99999997952 | bytes 30000000 | tf_op jit(solution)/shard_map/pallas_call | solution.py:486
  677.3 151.7 %shard_map.173 = (f32[256,1536]{1,0:T(8,128)}, bf16[2,8,80,1536]{3,2,1,0:T(8,128)(2,1)}, bf16[2,640,1536]{2,1,0:T(8,128)(2,1)}) custom-call(bf16[256,1536]{1,0:T(8,128)(2,1)} %bitcast.359, bf16[4,320,256]{2,1,0:T(8,128)(2,1)} %get-tuple-element.106.refs_2_.refs_1_, bf16[4,320,256]{2,1,0:T(8,128)(2,1)} %convert_element_type.182.refs_1_.refs_2_, ...), custom_call_target="tpu_custom_call" | custom-call | flops 99999997952 | bytes 30000000 | tf_op jit(solution)/shard_map/pallas_call | solution.py:486
  829.1 2.0 multiply_reduce_fusion.2
  831.7 1.7 copy-done.17
  836.1 4.6 fusion.121
  840.7 4.9 fusion.86
  845.5 10.4 fusion.92
  856.0 2.1 fusion.116
  859.1 10.9 convolution_convert_fusion.2
  870.0 9.8 fusion.22
  879.8 2.2 fusion.208
  882.0 2.5 copy.312
  885.9 2.3 subtract_convert_fusion.1
  892.1 3.5 convolution_convert_fusion.4
  895.6 4.6 convolution_convert_fusion.6
  901.4 11.4 reduce-scatter.15.cloned.1.call-done
  915.2 5.3 fusion.55
  920.5 4.6 convolution_convert_fusion
  926.6 148.9 %shard_map.174 = (f32[256,1536]{1,0:T(8,128)}, bf16[2,8,80,1536]{3,2,1,0:T(8,128)(2,1)}, bf16[2,640,1536]{2,1,0:T(8,128)(2,1)}) custom-call(bf16[256,1536]{1,0:T(8,128)(2,1)} %fusion.51.refs_0_, bf16[4,320,256]{2,1,0:T(8,128)(2,1)} %get-tuple-element.106.refs_2_.refs_1_, bf16[4,320,256]{2,1,0:T(8,128)(2,1)} %convert_element_type.182.refs_1_.refs_2_, ...), custom_call_target="tpu_custom_call" | custom-call | flops 99999997952 | bytes 30000000 | tf_op jit(solution)/shard_map/pallas_call | solution.py:486
  1075.6 2.0 multiply_reduce_fusion.3
  1078.8 3.6 convolution_convert_fusion.5
  1085.0 4.7 fusion.132
  1089.7 4.8 fusion.83
  1094.5 9.7 fusion.28
  1104.2 11.6 fusion.89
  1115.8 2.2 fusion.207
  1118.1 2.5 copy.316
  1125.5 10.9 convolution_convert_fusion.3
  1138.0 4.6 convolution_convert_fusion.7
  1144.9 6.6 fusion.7
  1152.7 18.7 %reduce-scatter.19.cloned.1.call-done = bf16[128,512]{1,0:T(8,128)(2,1)} async-done(((bf16[512,512]{1,0:T(8,128)(2,1)}), bf16[128,512]{1,0:T(8,128)(2,1)}) %reduce-scatter.19.cloned.1.call-update) | async-done | bytes 131088
  1176.7 1.7 copy.319
  1180.3 7.0 fusion.68
  1187.4 4.5 convolution_convert_fusion.1
  1193.4 6.6 fusion.6
  1200.0 217.3 %shard_map.175 = (f32[96,2176]{1,0:T(8,128)}, f32[96,1536]{1,0:T(8,128)}, bf16[4,384,1536]{2,1,0:T(8,128)(2,1)}, bf16[4,192,1536]{2,1,0:T(8,128)(2,1)}) custom-call(bf16[4,4,96,2176]{3,2,1,0:T(8,128)(2,1)} %bitcast.327, bf16[4,4,96,1536]{3,2,1,0:T(8,128)(2,1)} %bitcast.325, bf16[4,4,96,2176]{3,2,1,0:T(8,128)(2,1)} %bitcast.326, ...), custom_call_target="tpu_custom_call" | custom-call | tf_op jit(solution)/shard_map/pallas_call | solution.py:1154
  1417.3 1.9 slice_bitcast_fusion.4
  1421.6 7.6 bitcast_convert_fusion
  1429.2 2.8 bitcast_convert_fusion.1
  1432.7 3.2 fusion.61
  (344 shorter events, 74.0 us)
Async XLA Ops:
  7.2 271.1 %copy-start = (s32[4,1,512]{2,1,0:T(1,128)S(1)}, s32[4,1,512]{2,1,0:T(1,128)}, u32[]{:S(2)}) copy-start(s32[4,1,512]{2,1,0:T(1,128)} %param.12) | copy-start | bytes 24580
  9.5 314.0 %all-to-all-start = ((f32[4,2,2,4,128]{4,3,2,1,0:T(4,128)}), f32[4,2,2,4,128]{4,3,2,1,0:T(4,128)S(1)}, u32[]{:S(2)}, u32[]{:S(2)}) async-start(f32[4,2,2,4,128]{4,3,2,1,0:T(4,128)} %copy.245), calls=%async_computation | async-start | bytes 65536 | tf_op jit(solution)/shard_map/all_to_all | solution.py:1223
  15.8 884.5 %reduce-scatter.13.cloned.1.call-start = ((), (), s32[]{:S(2)}) async-start(), calls=%async_computation.5 | async-start | bytes 655360
  15.8 8.7 slice-start
  17.9 6.5 slice-start.1
  252.2 5.2 copy-start.65
  252.2 69.3 %copy-start.61 = (f32[1536]{0:T(1024)}, f32[1536]{0:T(1024)S(1)}, u32[]{:S(2)}) copy-start(f32[1536]{0:T(1024)S(1)} %get-tuple-element.102) | copy-start | bytes 18436
  252.2 230.7 %copy-start.67 = (f32[1536]{0:T(1024)}, f32[1536]{0:T(1024)S(1)}, u32[]{:S(2)}) copy-start(f32[1536]{0:T(1024)S(1)} %get-tuple-element.101) | copy-start | bytes 18436
  258.0 64.7 %copy-start.52 = (f32[128,64]{0,1:T(8,128)}, f32[128,64]{0,1:T(8,128)S(1)}, u32[]{:S(2)}) copy-start(f32[128,64]{0,1:T(8,128)S(1)} %get-tuple-element.155) | copy-start | bytes 98308
  258.0 233.5 %copy-start.37 = (f32[128,64]{0,1:T(8,128)}, f32[128,64]{0,1:T(8,128)S(1)}, u32[]{:S(2)}) copy-start(f32[128,64]{0,1:T(8,128)S(1)} %get-tuple-element.157) | copy-start | bytes 98308
  258.1 8.8 copy-start.32
  258.2 8.7 copy-start.47
  281.1 6.9 copy-start.59
  281.1 6.8 copy-start.29
  288.0 5.1 copy-start.83
  288.0 7.3 copy-start.9
  295.3 11.0 copy-start.13
  306.4 12.7 slice-start.2
  310.3 11.1 copy-start.2
  310.4 11.1 copy-start.70
  310.4 8.7 slice-start.3
  482.9 5.9 copy-start.74
  493.3 16.6 %copy-start.41 = (bf16[2,2,6,128,128]{4,3,2,1,0:T(8,128)(2,1)}, bf16[2,2,6,128,128]{4,3,2,1,0:T(8,128)(2,1)S(1)}, u32[]{:S(2)}) copy-start(bf16[2,2,6,128,128]{4,3,2,1,0:T(8,128)(2,1)S(1)} %copy.251) | copy-start | bytes 2359300
  493.9 16.0 %copy-start.40 = (pred[2,768,512]{1,2,0:T(8,128)(4,1)S(1)}, pred[2,768,512]{1,2,0:T(8,128)(4,1)}, u32[]{:S(2)}) copy-start(pred[2,768,512]{1,2,0:T(8,128)(4,1)} %copy.232) | copy-start | bytes 2359300
  509.9 6.4 copy-start.30
  516.3 4.8 copy-start.23
  521.1 4.1 copy-start.15
  521.1 4.2 copy-start.63
  677.3 151.8 %copy-start.5 = (f32[256,1536]{1,0:T(8,128)S(1)}, f32[256,1536]{1,0:T(8,128)}, u32[]{:S(2)}) copy-start(f32[256,1536]{1,0:T(8,128)} %copy-done.4) | copy-start | bytes 4718596
  677.3 151.8 %copy-start.64 = (f32[1536]{0:T(1024)S(1)}, f32[1536]{0:T(1024)}, u32[]{:S(2)}) copy-start(f32[1536]{0:T(1024)} %get-tuple-element.100) | copy-start | bytes 18436
  677.3 151.8 %copy-start.73 = (f32[256]{0:T(256)S(1)}, f32[256]{0:T(256)}, u32[]{:S(2)}) copy-start(f32[256]{0:T(256)} %copy-done.72) | copy-start | bytes 3076
  836.0 4.6 copy-start.86
  840.7 4.9 copy-start.42
  859.1 53.7 %reduce-scatter.15.cloned.1.call-start = ((), (), s32[]{:S(2)}) async-start(), calls=%async_computation.6 | async-start | bytes 655360
  885.9 4.3 copy-start.28
  891.8 259.7 %reduce-scatter.17.cloned.1.call-start = ((), (), s32[]{:S(2)}) async-start(), calls=%async_computation.7 | async-start | bytes 655360
  900.3 14.1 copy-start.34
  900.3 14.1 copy-start.45
  900.3 14.9 %copy-start.24 = (bf16[256,1536]{1,0:T(8,128)(2,1)S(1)}, bf16[256,1536]{1,0:T(8,128)(2,1)}, u32[]{:S(2)}) copy-start(bf16[256,1536]{1,0:T(8,128)(2,1)} %copy-done.22) | copy-start | bytes 2359300
  900.3 14.9 %copy-start.68 = (f32[1536]{0:T(1024)S(1)}, f32[1536]{0:T(1024)}, u32[]{:S(2)}) copy-start(f32[1536]{0:T(1024)} %copy-done.67) | copy-start | bytes 18436
  900.3 14.9 %copy-start.75 = (f32[256]{0:T(256)S(1)}, f32[256]{0:T(256)}, u32[]{:S(2)}) copy-start(f32[256]{0:T(256)} %copy-done.74) | copy-start | bytes 3076
  915.2 5.3 copy-start.43
  926.6 149.0 %copy-start.3 = (f32[256,1536]{1,0:T(8,128)S(1)}, f32[256,1536]{1,0:T(8,128)}, u32[]{:S(2)}) copy-start(f32[256,1536]{1,0:T(8,128)} %copy-done.2) | copy-start | bytes 4718596
  926.6 149.0 %copy-start.62 = (f32[1536]{0:T(1024)S(1)}, f32[1536]{0:T(1024)}, u32[]{:S(2)}) copy-start(f32[1536]{0:T(1024)} %copy-done.61) | copy-start | bytes 18436
  926.6 149.0 %copy-start.71 = (f32[256]{0:T(256)S(1)}, f32[256]{0:T(256)}, u32[]{:S(2)}) copy-start(f32[256]{0:T(256)} %copy-done.70) | copy-start | bytes 3076
  1077.6 4.7 slice-start.4
  1085.0 4.8 copy-start.84
  1124.2 47.2 %reduce-scatter.19.cloned.1.call-start = ((), (), s32[]{:S(2)}) async-start(), calls=%async_computation.8 | async-start | bytes 655360
  1125.5 11.0 copy-start.69
  1125.5 11.0 copy-start.19
  1125.5 11.0 copy-start.20
  1125.5 11.0 copy-start.39
  1125.5 11.0 copy-start.54
  1125.5 11.8 copy-start.80
  1151.5 27.0 %copy-start.35 = (f32[128,64]{1,0:T(8,128)S(1)}, f32[128,64]{1,0:T(8,128)}, u32[]{:S(2)}) copy-start(f32[128,64]{1,0:T(8,128)} %copy-done.32) | copy-start | bytes 98308
  1151.5 27.0 %copy-start.46 = (f32[128,64]{1,0:T(8,128)S(1)}, f32[128,64]{1,0:T(8,128)}, u32[]{:S(2)}) copy-start(f32[128,64]{1,0:T(8,128)} %copy.269) | copy-start | bytes 98308
  1151.5 28.8 %copy-start.10 = (bf16[4,128,1536]{2,1,0:T(8,128)(2,1)S(1)}, bf16[4,128,1536]{2,1,0:T(8,128)(2,1)}, u32[]{:S(2)}) copy-start(bf16[4,128,1536]{2,1,0:T(8,128)(2,1)} %param.11) | copy-start | bytes 4718596
  1151.5 28.8 %copy-start.66 = (f32[1536]{0:T(1024)S(1)}, f32[1536]{0:T(1024)}, u32[]{:S(2)}) copy-start(f32[1536]{0:T(1024)} %copy-done.65) | copy-start | bytes 18436
  1152.7 19.8 %copy-start.55 = (bf16[128,512]{0,1:T(8,128)(2,1)}, bf16[128,512]{0,1:T(8,128)(2,1)S(1)}, u32[]{:S(2)}) copy-start(bf16[128,512]{0,1:T(8,128)(2,1)S(1)} %copy.307) | copy-start | bytes 393220
  1180.3 7.1 copy-start.44
  1180.3 7.1 copy-start.56
  1180.3 7.1 copy-start.58
  1421.6 7.6 copy-start.25
  1432.7 5.5 copy-start.1
  (35 other events, 82.4 us)
Sparse Core Ops, SparseCore 0:
  859.2 20.7 reduce-scatter.12
  892.0 20.7 reduce-scatter.14
  1124.4 22.2 reduce-scatter.16
  1149.8 21.6 reduce-scatter.18

commit v3 on v2

v3 whole, which is shorter than its diff:
```python
import functools

import jax
import jax.numpy as jnp
from jax import lax
from jax.experimental import pallas as pl
from jax.experimental.pallas import tpu as pltpu
from jax.sharding import PartitionSpec as P

D = 1536
HEADS = 12
KV_HEADS = 2
HD = 128
FF = 768
TOPK = 4
EXP_DEV = 4
MICRO = 4
GROUP = HEADS // KV_HEADS
PAD = 128
WQ = HEADS * HD
WK = KV_HEADS * HD
PROJ = WQ + 2 * WK
WIN = PROJ + PAD
SCALE = HD ** (-0.5)

epsilon = 1e-06
rope_base = 10000.0

MESH = pl.DeviceIdType.MESH
F32 = jnp.float32
BF16 = jnp.bfloat16
DMA = pltpu.SemaphoreType.DMA
VMEM_LIMIT = 60 * 2**20


class Plan:
    def __init__(self, mesh_shape, tokens):
        self.nx, self.nz, self.ns = mesh_shape
        self.tokens = tokens
        self.micro = MICRO // self.nx
        self.rows = self.micro * tokens
        self.ranks = self.nx * self.ns
        self.group = self.ranks // EXP_DEV
        self.halves = self.group // 2
        self.sources = self.ranks // self.halves
        self.experts = EXP_DEV * self.nz
        self.capacity = 5 * tokens * TOPK // (4 * self.experts)
        self.slots = -(-self.micro * self.capacity // 16) * 16
        self.blocks = self.nz // 2
        self.many = self.sources * self.slots


def me():
    return lax.axis_index("section"), lax.axis_index("expert"), lax.axis_index("shard")


def remote(src, dst, send, recv, device):
    return pltpu.make_async_remote_copy(
        src_ref=src,
        dst_ref=dst,
        send_sem=send,
        recv_sem=recv,
        device_id=device,
        device_id_type=MESH,
    )


def landed(ref, sem):
    pltpu.make_async_copy(ref, ref, sem).wait()


def greet_plane(plan, along=False):
    x, z, s = me()
    barrier = pltpu.get_barrier_semaphore()
    mine = x * plan.ns + s
    for step in range(1, plan.ranks):
        other = (mine + step) % plan.ranks
        pl.semaphore_signal(
            barrier, inc=1, device_id=(other // plan.ns, z, other % plan.ns), device_id_type=MESH
        )
    total = plan.ranks - 1
    if along:
        for step in range(1, plan.nz):
            pl.semaphore_signal(
                barrier, inc=1, device_id=(x, (z + step) % plan.nz, s), device_id_type=MESH
            )
        total += plan.nz - 1
    pl.semaphore_wait(barrier, total)


def nearest(place, index, count):
    left = place
    right = count - 1 - place
    short = jnp.minimum(left, right)
    odd = index % 2
    near = place + (1 - 2 * odd) * ((index + 1) // 2)
    far = jnp.where(left < right, index, count - 1 - index)
    return jnp.where(index <= 2 * short, near, far)


TILE = 256
CUTS = 3
CUT = D // CUTS


def moe_kernel(plan, layer, backward, *refs):
    if backward:
        (rows_in, put, take, w_in, w_down, gate_up, out, sent_save, grad_save) = refs[:9]
        scratch = refs[9:]
    else:
        (rows_in, put, take, w_in, w_down, base, out, sent_save, gate_up, hidden) = refs[:10]
        scratch = refs[10:]
    (
        line,
        sbuf,
        xbuf,
        ybuf,
        rbuf,
        pbuf,
        qbuf,
        win_v,
        wdown_v,
        gbuf,
        zbuf,
        line_recv,
        line_right,
        line_left,
        to_send,
        to_recv,
        back_send,
        back_recv,
        sum_send,
        sum_recv,
        local_sem,
        save_sem,
    ) = scratch
    x, z, s = me()
    nz, ns, slots, many = plan.nz, plan.ns, plan.slots, plan.many
    rank = x * ns + s
    own_expert = rank // plan.group
    own_turn = (rank % plan.group) // plan.halves
    own_half = rank % plan.halves
    part = ns // plan.halves
    own_source = x * part + s // plan.halves
    chunk = plan.tokens

    load_in = pltpu.make_async_copy(w_in.at[layer], win_v, local_sem.at[0])
    load_down = pltpu.make_async_copy(w_down.at[layer], wdown_v, local_sem.at[1])
    load_in.start()
    load_down.start()
    if backward:
        load_gate = pltpu.make_async_copy(gate_up, gbuf, local_sem.at[3])
        load_gate.start()
    greet_plane(plan, along=True)

    def along(block, piece, step, own):
        at = pl.ds(piece * chunk, chunk)
        src = rows_in.at[at] if own else line.at[block, at]
        sem = line_right if step > 0 else line_left
        return remote(
            src,
            line.at[block, at],
            sem.at[block, piece],
            line_recv.at[block, piece],
            (x, z + step, s),
        )

    def owner(block, expert):
        rank_to = expert * plan.group + (block % 2) * plan.halves + s % plan.halves
        return rank_to // ns, rank_to % ns

    def dispatch_copy(block, expert):
        to_x, to_s = owner(block, expert)
        here = (to_x == x) & (to_s == s)
        return here, remote(
            sbuf.at[block, expert],
            xbuf.at[block // 2, own_source],
            to_send.at[block, expert],
            to_recv.at[block // 2, own_source],
            (to_x, z, to_s),
        )

    def return_copy(block, half, source):
        to_x = source // part
        to_s = (source % part) * plan.halves + own_half
        here = (to_x == x) & (to_s == s)
        return here, remote(
            ybuf.at[block // 2, half, source],
            rbuf.at[block, half, own_expert],
            back_send.at[block // 2, half, source],
            back_recv.at[block, half, own_expert],
            (to_x, z, to_s),
        )

    def sum_copy(block, half):
        rightward = (block > z).astype(jnp.int32)
        to = z - 1 + 2 * rightward
        into = jnp.where((rightward == 1) & (block == to), nz, block)
        return remote(
            pbuf.at[block, half],
            qbuf.at[into, half],
            sum_send.at[block, half],
            sum_recv.at[into, half],
            (x, to, s),
        )

    for piece in range(plan.micro):

        @pl.when(z + 1 < nz)
        def _():
            along(z, piece, 1, True).start()

        @pl.when(z > 0)
        def _():
            along(z, piece, -1, True).start()

    own_copy = pltpu.make_async_copy(rows_in, line.at[z], local_sem.at[2])
    own_copy.start()
    own_copy.wait()

    def stage_put(index):
        block = nearest(z, index, nz)
        for piece in range(plan.micro):

            @pl.when(block < z)
            def _():
                along(block, piece, 1, False).wait_recv()

                @pl.when(z + 1 < nz)
                def _():
                    along(block, piece, 1, False).start()

            @pl.when(block > z)
            def _():
                along(block, piece, -1, False).wait_recv()

                @pl.when(z > 0)
                def _():
                    along(block, piece, -1, False).start()

        def lay(step, _):
            at = pl.ds(pl.multiple_of(step * TILE, TILE), TILE)
            laid = jnp.dot(put[block], line[block, :, at], preferred_element_type=F32)
            sbuf[block, :, :, at] = laid.astype(BF16).reshape(EXP_DEV, slots, TILE)
            return 0

        lax.fori_loop(0, D // TILE, lay, 0)
        for expert in range(EXP_DEV):
            here, copy = dispatch_copy(block, expert)

            @pl.when(here)
            def _():
                pltpu.make_async_copy(
                    sbuf.at[block, expert],
                    xbuf.at[block // 2, own_source],
                    to_recv.at[block // 2, own_source],
                ).start()

            @pl.when(jnp.logical_not(here))
            def _():
                copy.start()

    def stage_expert(index):
        block = nearest(z, index, nz)
        pair = block // 2
        for source in range(plan.sources):
            landed(xbuf.at[pair, source], to_recv.at[pair, source])
        pltpu.make_async_copy(xbuf.at[pair], sent_save.at[pair], save_sem.at[0, pair]).start()
        taken = xbuf[pair].reshape(many, D)

        def middle(step, _):
            at = pl.multiple_of(step * TILE, TILE)
            if backward:
                grad_hidden = lax.dot_general(
                    taken,
                    wdown_v[pl.ds(at, TILE), :],
                    (((1,), (1,)), ((), ())),
                    preferred_element_type=F32,
                )
                gate = gbuf[pair, :, pl.ds(at, TILE)].astype(F32)
                up = gbuf[pair, :, pl.ds(FF + at, TILE)].astype(F32)
                sig = 1.0 / (1.0 + jnp.exp(-gate))
                gs = gate * sig
                grad_gate = grad_hidden * up * (sig + gs * (1.0 - sig))
                gbuf[pair, :, pl.ds(at, TILE)] = grad_gate.astype(BF16)
                gbuf[pair, :, pl.ds(FF + at, TILE)] = (grad_hidden * gs).astype(BF16)
            else:
                gate = jnp.dot(taken, win_v[:, pl.ds(at, TILE)], preferred_element_type=F32)
                up = jnp.dot(taken, win_v[:, pl.ds(FF + at, TILE)], preferred_element_type=F32)
                gbuf[pair, :, pl.ds(at, TILE)] = gate.astype(BF16)
                gbuf[pair, :, pl.ds(FF + at, TILE)] = up.astype(BF16)
                zbuf[pair, :, pl.ds(at, TILE)] = (gate / (1.0 + jnp.exp(-gate)) * up).astype(BF16)
            return 0

        lax.fori_loop(0, FF // TILE, middle, 0)
        if backward:
            pltpu.make_async_copy(gbuf.at[pair], grad_save.at[pair], save_sem.at[1, pair]).start()
        else:
            pltpu.make_async_copy(gbuf.at[pair], gate_up.at[pair], save_sem.at[1, pair]).start()
            pltpu.make_async_copy(zbuf.at[pair], hidden.at[pair], save_sem.at[2, pair]).start()

        def last(step, _):
            half = step // (CUT // TILE)
            at = pl.multiple_of(step * TILE, TILE)
            inside = pl.multiple_of((step % (CUT // TILE)) * TILE, TILE)
            if backward:
                result = lax.dot_general(
                    gbuf[pair],
                    win_v[pl.ds(at, TILE), :],
                    (((1,), (1,)), ((), ())),
                    preferred_element_type=F32,
                )
            else:
                result = jnp.dot(
                    zbuf[pair], wdown_v[:, pl.ds(at, TILE)], preferred_element_type=F32
                )
            ybuf[pair, half, :, :, pl.ds(inside, TILE)] = result.astype(BF16).reshape(
                plan.sources, slots, TILE
            )

            return 0

        lax.fori_loop(0, D // TILE, last, 0)

    def give_back(index):
        block = nearest(z, index, nz)
        pair = block // 2
        for half in range(CUTS):
            for source in range(plan.sources):
                here, copy = return_copy(block, half, source)

                @pl.when(here)
                def _():
                    pltpu.make_async_copy(
                        ybuf.at[pair, half, source],
                        rbuf.at[block, half, own_expert],
                        back_recv.at[block, half, own_expert],
                    ).start()

                @pl.when(jnp.logical_not(here))
                def _():
                    copy.start()

    def stage_take(index):
        block = nearest(z, index, nz)
        origin = ((block < z) & (z == nz - 1)) | ((block > z) & (z == 0))
        for half in range(CUTS):
            for expert in range(EXP_DEV):
                landed(rbuf.at[block, half, expert], back_recv.at[block, half, expert])
            got = lax.dot_general(
                take[block],
                rbuf[block, half].reshape(EXP_DEV * slots, CUT),
                (((0,), (0,)), ((), ())),
                preferred_element_type=F32,
            )

            @pl.when(block == z)
            def _():
                at = pl.ds(half * CUT, CUT)
                if backward:
                    out[:, at] = got
                else:
                    out[:, at] = base[:, at] + got

            @pl.when(block != z)
            def _():
                pbuf[block, half] = got.astype(BF16)

            @pl.when(origin)
            def _():
                sum_copy(block, half).start()

    def relay(turn):
        lower = z < nz // 2
        first = jnp.where(lower, nz - 1 - z, z)
        early = turn < first
        ahead = jnp.where(early, first - turn, nz - 1 - turn)
        rightward = lower == early
        block = jnp.where(rightward, z + ahead, z - ahead)

        @pl.when((z > 0) & (z < nz - 1))
        def _():
            for half in range(CUTS):
                landed(qbuf.at[block, half], sum_recv.at[block, half])
                pbuf[block, half] = (
                    pbuf[block, half].astype(F32) + qbuf[block, half].astype(F32)
                ).astype(BF16)
                sum_copy(block, half).start()

    def own_turn_do(index, act):
        @pl.when(nearest(z, index, nz) % 2 == own_turn)
        def _():
            act(index)

    final = nz - 1
    stage_put(0)
    load_in.wait()
    load_down.wait()
    if backward:
        load_gate.wait()
    for index in range(1, nz):
        stage_put(index)
        own_turn_do(index - 1, stage_expert)
        if 1 < index < final:
            own_turn_do(index - 1, give_back)
    for index in range(1, nz - 2):
        stage_take(index)
    own_turn_do(final, stage_expert)
    own_turn_do(final, give_back)
    stage_take(final)
    own_turn_do(final - 1, give_back)
    own_turn_do(0, give_back)
    relay(0)
    stage_take(final - 1)
    stage_take(0)
    for turn in (2, 1) if nz == 4 else range(1, nz - 1):
        relay(turn)
    for half in range(CUTS):
        at = pl.ds(half * CUT, CUT)

        @pl.when(z + 1 < nz)
        def _():
            landed(qbuf.at[z, half], sum_recv.at[z, half])
            out[:, at] += qbuf[z, half].astype(F32)

        @pl.when(z > 0)
        def _():
            landed(qbuf.at[nz, half], sum_recv.at[nz, half])
            out[:, at] += qbuf[nz, half].astype(F32)

    def drain(block, _):
        for piece in range(plan.micro):

            @pl.when((block <= z) & (z + 1 < nz))
            def _():
                along(block, piece, 1, False).wait_send()

            @pl.when((block >= z) & (z > 0))
            def _():
                along(block, piece, -1, False).wait_send()

        for expert in range(EXP_DEV):
            here, copy = dispatch_copy(block, expert)

            @pl.when(jnp.logical_not(here))
            def _():
                copy.wait_send()

        @pl.when(block % 2 == own_turn)
        def _():
            for half in range(CUTS):
                for source in range(plan.sources):
                    here, copy = return_copy(block, half, source)

                    @pl.when(jnp.logical_not(here))
                    def _():
                        copy.wait_send()

        @pl.when(block != z)
        def _():
            for half in range(CUTS):
                sum_copy(block, half).wait_send()

        return 0

    lax.fori_loop(0, nz, drain, 0)
    for pair in range(plan.blocks):
        pltpu.make_async_copy(xbuf.at[pair], sent_save.at[pair], save_sem.at[0, pair]).wait()
        if backward:
            pltpu.make_async_copy(gbuf.at[pair], grad_save.at[pair], save_sem.at[1, pair]).wait()
        else:
            pltpu.make_async_copy(gbuf.at[pair], gate_up.at[pair], save_sem.at[1, pair]).wait()
            pltpu.make_async_copy(zbuf.at[pair], hidden.at[pair], save_sem.at[2, pair]).wait()


def moe_call(plan, layer, backward, collective_id, rows_in, put, take, w_in, w_down, last):
    nz, blocks, slots, many, sources = plan.nz, plan.blocks, plan.slots, plan.many, plan.sources
    vmem = pl.BlockSpec(memory_space=pltpu.VMEM)
    hbm = pl.BlockSpec(memory_space=pltpu.HBM)
    saved = (blocks, sources, slots, D)
    shape = jax.ShapeDtypeStruct
    outs = [shape((plan.rows, D), F32), shape(saved, BF16), shape((blocks, many, 2 * FF), BF16)]
    if not backward:
        outs.append(shape((blocks, many, FF), BF16))
    return pl.pallas_call(
        functools.partial(moe_kernel, plan, layer, backward),
        out_shape=outs,
        in_specs=[vmem, vmem, vmem, hbm, hbm, hbm if backward else vmem],
        out_specs=[vmem] + [hbm] * (len(outs) - 1),
        scratch_shapes=[
            pltpu.VMEM((nz, plan.rows, D), BF16),
            pltpu.VMEM((nz, EXP_DEV, slots, D), BF16),
            pltpu.VMEM(saved, BF16),
            pltpu.VMEM((blocks, CUTS, sources, slots, CUT), BF16),
            pltpu.VMEM((nz, CUTS, EXP_DEV, slots, CUT), BF16),
            pltpu.VMEM((nz, CUTS, plan.rows, CUT), BF16),
            pltpu.VMEM((nz + 1, CUTS, plan.rows, CUT), BF16),
            pltpu.VMEM((D, 2 * FF), BF16),
            pltpu.VMEM((FF, D), BF16),
            pltpu.VMEM((blocks, many, 2 * FF), BF16),
            pltpu.VMEM((blocks, many, FF), BF16),
            DMA((nz, plan.micro)),
            DMA((nz, plan.micro)),
            DMA((nz, plan.micro)),
            DMA((nz, EXP_DEV)),
            DMA((blocks, sources)),
            DMA((blocks, CUTS, sources)),
            DMA((nz, CUTS, EXP_DEV)),
            DMA((nz, CUTS)),
            DMA((nz + 1, CUTS)),
            DMA((4,)),
            DMA((3, blocks)),
        ],
        compiler_params=pltpu.CompilerParams(
            collective_id=collective_id, has_side_effects=True, vmem_limit_bytes=VMEM_LIMIT
        ),
        cost_estimate=pl.CostEstimate(
            flops=100_000_000_000, bytes_accessed=30_000_000, transcendentals=0
        ),
    )(rows_in, put, take, w_in, w_down, last)


def expert_spread(plan, ins, outs, send, recv, pass_send, pass_recv):
    x, z, s = me()
    nx, ns, group = plan.nx, plan.ns, plan.group
    rank = x * ns + s
    own_expert, own_part = rank // group, rank % group
    own = [(layer, k) for layer in range(nx) for k in range(ns // group)]

    def first(expert, which):
        to = expert * group + s % group
        return to == rank, remote(
            ins[which].at[expert],
            outs[which].at[x, s],
            send.at[expert, which],
            recv.at[x, s, which],
            (to // ns, z, to % ns),
        )

    def onward(layer, source, step, which):
        to = own_expert * group + (own_part + step) % group
        return remote(
            outs[which].at[layer, source],
            outs[which].at[layer, source],
            pass_send.at[layer, source, step - 1, which],
            pass_recv.at[layer, source, which],
            (to // ns, z, to % ns),
        )

    def start():
        for which in range(2):
            for expert in range(EXP_DEV):
                here, copy = first(expert, which)

                @pl.when(here)
                def _():
                    pltpu.make_async_copy(
                        ins[which].at[expert], outs[which].at[x, s], recv.at[x, s, which]
                    ).start()

                @pl.when(jnp.logical_not(here))
                def _():
                    copy.start()

    def pass_on():
        for layer, k in own:
            source = k * group + own_part
            for which in range(2):
                landed(outs[which].at[layer, source], recv.at[layer, source, which])
                for step in range(1, group):
                    onward(layer, source, step, which).start()

    def finish():
        for layer, k in own:
            for step in range(1, group):
                source = k * group + (own_part + step) % group
                for which in range(2):
                    landed(outs[which].at[layer, source], pass_recv.at[layer, source, which])
        for which in range(2):
            for expert in range(EXP_DEV):
                here, copy = first(expert, which)

                @pl.when(jnp.logical_not(here))
                def _():
                    copy.wait_send()

        for layer, k in own:
            source = k * group + own_part
            for which in range(2):
                for step in range(1, group):
                    onward(layer, source, step, which).wait_send()

    return start, pass_on, finish


def spread_scratch(plan):
    nx, ns, group = plan.nx, plan.ns, plan.group
    return [
        DMA((EXP_DEV, 2)),
        DMA((nx, ns, 2)),
        DMA((nx, ns, group - 1, 2)),
        DMA((nx, ns, 2)),
    ]


def spread_kernel(plan, *refs):
    greet_plane(plan)
    start, pass_on, finish = expert_spread(plan, refs[:2], refs[2:4], *refs[4:])
    start()
    pass_on()
    finish()


def spread_call(plan, collective_id, gate_up, down):
    hbm = pl.BlockSpec(memory_space=pltpu.HBM)
    vmem = pl.BlockSpec(memory_space=pltpu.VMEM)
    outs = [
        jax.ShapeDtypeStruct((plan.nx, plan.ns) + part.shape[1:], BF16) for part in (gate_up, down)
    ]
    return pl.pallas_call(
        functools.partial(spread_kernel, plan),
        out_shape=outs,
        in_specs=[vmem, vmem],
        out_specs=[hbm, hbm],
        scratch_shapes=spread_scratch(plan),
        compiler_params=pltpu.CompilerParams(
            collective_id=collective_id, has_side_effects=True, vmem_limit_bytes=VMEM_LIMIT
        ),
    )(gate_up, down)


def gather_kernel(plan, *refs):
    piece, wide_ins, out, wide_outs = refs[0], refs[1:3], refs[3], refs[4:6]
    line_recv, right, left, copy_sem, plane_recv, to_core, to_x, to_y = refs[6:14]
    x, z, s = me()
    nz = plan.nz
    over = (s + 2) % 4
    greet_plane(plan, along=True)
    start, pass_on, finish = expert_spread(plan, wide_ins, wide_outs, *refs[14:])
    size = piece.shape[0] // 2
    whole = pl.ds(0, 2 * size)
    parts = (pl.ds(0, size), pl.ds(size, size))
    core = (x, z, s + 1 - 2 * (s % 2))
    across_x = (1 - x, z, s)
    across_y = (x, z, over)

    def along(block, step, own):
        place = out.at[x, block, s]
        sem = right if step > 0 else left
        return remote(
            piece if own else place, place, sem.at[block], line_recv.at[block], (x, z + step, s)
        )

    def passed(layer, block, shard, rows, kind, sem, to, own=False):
        place = out.at[layer, block, shard, rows]
        return remote(
            piece if own else place,
            place,
            sem.at[layer, block, shard // 2],
            plane_recv.at[layer, block, shard, kind],
            to,
        )

    def arrived(layer, block, shard, rows, kind):
        landed(out.at[layer, block, shard, rows], plane_recv.at[layer, block, shard, kind])

    @pl.when(z + 1 < nz)
    def _():
        along(z, 1, True).start()

    @pl.when(z > 0)
    def _():
        along(z, -1, True).start()

    own = pltpu.make_async_copy(piece, out.at[x, z, s], copy_sem.at[0])
    own.start()
    start()

    def column_copies(block, own=False):
        ways = ((to_x, across_x), (to_y, across_y), (to_core, core))
        return [passed(x, block, s, whole, 0, sem, to, own) for sem, to in ways]

    def column(index):
        block = nearest(z, index, nz)

        @pl.when(block < z)
        def _():
            along(block, 1, False).wait_recv()

            @pl.when(z + 1 < nz)
            def _():
                along(block, 1, False).start()

        @pl.when(block > z)
        def _():
            along(block, -1, False).wait_recv()

            @pl.when(z > 0)
            def _():
                along(block, -1, False).start()

        @pl.when(block == z)
        def _():
            for copy in column_copies(block, True):
                copy.start()

        @pl.when(block != z)
        def _():
            for copy in column_copies(block):
                copy.start()

    def neighbour_copies(block):
        return [
            passed(1 - x, block, s, parts[0], 1, to_y, across_y),
            passed(1 - x, block, s, whole, 0, to_core, core),
            passed(x, block, over, parts[1], 2, to_x, across_x),
            passed(x, block, over, whole, 0, to_core, core),
        ]

    def neighbours(index):
        block = nearest(z, index, nz)
        copies = neighbour_copies(block)
        arrived(1 - x, block, s, whole, 0)
        copies[0].start()
        copies[1].start()
        arrived(x, block, over, whole, 0)
        copies[2].start()
        copies[3].start()

    def opposite(index):
        block = nearest(z, index, nz)
        arrived(1 - x, block, over, parts[0], 1)
        arrived(1 - x, block, over, parts[1], 2)
        passed(1 - x, block, over, whole, 0, to_core, core).start()

    def each(act):
        def body(index, _):
            act(index)
            return 0

        lax.fori_loop(0, nz, body, 0)

    each(column)
    each(neighbours)
    each(opposite)
    own.wait()
    pass_on()

    def drain(block, _):
        other = s + 1 - 2 * (s % 2)
        for layer in range(2):
            for row in range(2):
                arrived(layer, block, row * 2 + other % 2, whole, 0)

        @pl.when((block <= z) & (z + 1 < nz))
        def _():
            along(block, 1, False).wait_send()

        @pl.when((block >= z) & (z > 0))
        def _():
            along(block, -1, False).wait_send()

        for copy in column_copies(block) + neighbour_copies(block):
            copy.wait_send()
        passed(1 - x, block, over, whole, 0, to_core, core).wait_send()
        return 0

    lax.fori_loop(0, nz, drain, 0)
    finish()


def gather_call(plan, collective_id, attention, experts):
    hbm = pl.BlockSpec(memory_space=pltpu.HBM)
    vmem = pl.BlockSpec(memory_space=pltpu.VMEM)
    nx, nz, ns = plan.nx, plan.nz, plan.ns
    outs = [jax.ShapeDtypeStruct((nx, nz, ns) + attention.shape, BF16)]
    outs += [jax.ShapeDtypeStruct((nx, ns) + part.shape[1:], BF16) for part in experts]
    return pl.pallas_call(
        functools.partial(gather_kernel, plan),
        out_shape=outs,
        in_specs=[vmem] * 3,
        out_specs=[hbm] * 3,
        scratch_shapes=[
            DMA((nz,)),
            DMA((nz,)),
            DMA((nz,)),
            DMA((1,)),
            DMA((nx, nz, ns, 3)),
            DMA((nx, nz, 2)),
            DMA((nx, nz, 2)),
            DMA((nx, nz, 2)),
        ]
        + spread_scratch(plan),
        compiler_params=pltpu.CompilerParams(
            collective_id=collective_id, has_side_effects=True, vmem_limit_bytes=VMEM_LIMIT
        ),
    )(attention, *experts)


def expert_collect(plan, ins, outs, parts, stage, load, swap_send, swap_recv, send, recv):
    x, z, s = me()
    ns, group = plan.ns, plan.group
    rank = x * ns + s
    own_expert, own_part = rank // group, rank % group
    order = [(k, kind) for kind in range(len(ins)) for k in range(ns // group)]

    def swap(k, step, kind):
        part_to = (own_part + step) % group
        to = own_expert * group + part_to
        return remote(
            ins[kind].at[k * group + part_to],
            parts[kind].at[step - 1, k],
            swap_send.at[step - 1, k, kind],
            swap_recv.at[step - 1, k, kind],
            (to // ns, z, to % ns),
        )

    def own(k, kind):
        return pltpu.make_async_copy(
            ins[kind].at[k * group + own_part], stage[kind].at[k], load.at[k, kind]
        )

    def home(k, kind):
        layer, which = kind // 2, kind % 2
        here = (x == layer) & (s == k * group + own_part)
        return here, remote(
            stage[kind].at[k],
            outs[which].at[own_expert],
            send.at[k, kind],
            recv.at[own_expert, which],
            (layer, z, k * group + own_part),
        )

    def start():
        for k, kind in order:
            own(k, kind).start()
            for step in range(1, group):
                swap(k, step, kind).start()

    def add(place):
        k, kind = order[place]
        own(k, kind).wait()
        for step in range(1, group):
            swap(k, step, kind).wait_recv()
        total = stage[kind][k].astype(F32)
        for step in range(1, group):
            total += parts[kind][step - 1, k].astype(F32)
        stage[kind][k] = total.astype(BF16)
        here, copy = home(k, kind)

        @pl.when(here)
        def _():
            which = kind % 2
            pltpu.make_async_copy(
                stage[kind].at[k], outs[which].at[own_expert], recv.at[own_expert, which]
            ).start()

        @pl.when(jnp.logical_not(here))
        def _():
            copy.start()

    def finish():
        for which in range(2):
            for expert in range(EXP_DEV):
                landed(outs[which].at[expert], recv.at[expert, which])
        for k, kind in order:
            for step in range(1, group):
                swap(k, step, kind).wait_send()
            here, copy = home(k, kind)

            @pl.when(jnp.logical_not(here))
            def _():
                copy.wait_send()

    return len(order), start, add, finish


def collect_scratch(plan, values):
    group, each, kinds = plan.group, plan.ns // plan.group, len(values)
    return (
        [pltpu.VMEM((group - 1, each) + part.shape[1:], BF16) for part in values]
        + [pltpu.VMEM((each,) + part.shape[1:], BF16) for part in values]
        + [
            DMA((each, kinds)),
            DMA((group - 1, each, kinds)),
            DMA((group - 1, each, kinds)),
            DMA((each, kinds)),
            DMA((EXP_DEV, 2)),
        ]
    )


def collect_kernel(plan, *refs):
    kinds = 2 * plan.nx
    ins, outs = refs[:kinds], refs[kinds : kinds + 2]
    parts, stage = refs[kinds + 2 : 2 * kinds + 2], refs[2 * kinds + 2 : 3 * kinds + 2]
    greet_plane(plan)
    count, start, add, finish = expert_collect(
        plan, ins, outs, parts, stage, *refs[3 * kinds + 2 :]
    )
    start()
    for place in range(count):
        add(place)
    finish()


def collect_call(plan, collective_id, terms):
    ns = plan.ns
    hbm = pl.BlockSpec(memory_space=pltpu.HBM)
    values = [part.reshape(ns, part.shape[0] // ns, D) for layer in terms for part in layer]
    return pl.pallas_call(
        functools.partial(collect_kernel, plan),
        out_shape=[jax.ShapeDtypeStruct((EXP_DEV,) + part.shape[1:], BF16) for part in values[:2]],
        in_specs=[hbm] * len(values),
        out_specs=[hbm, hbm],
        scratch_shapes=collect_scratch(plan, values),
        compiler_params=pltpu.CompilerParams(
            collective_id=collective_id, has_side_effects=True, vmem_limit_bytes=VMEM_LIMIT
        ),
    )(*values)


ADDS = (0, 0, 0, 0, 8, 8, 8)
DEPTH = 1


def reduce_kernel(plan, *refs):
    grads, wide_ins, out, wide_outs = refs[0:2], refs[2:6], refs[6], refs[7:9]
    scratch = refs[9:]
    mine, given, x_one, y_one, y_two, x_two, chain = scratch[:7]
    (
        load_sem,
        core_send,
        core_recv,
        x_one_send,
        x_one_recv,
        y_one_send,
        y_one_recv,
        x_two_send,
        x_two_recv,
        y_two_send,
        y_two_recv,
        chain_send,
        chain_recv,
    ) = scratch[7:20]
    parts, stage = scratch[20:24], scratch[24:28]
    x, z, s = me()
    nz = plan.nz
    row, side = s // 2, s % 2
    core = (x, z, s + 1 - 2 * side)
    across_x = (1 - x, z, s)
    across_y = (x, z, (s + 2) % 4)
    size = grads[0].shape[2] // 2
    greet_plane(plan, along=True)
    count, start, add, finish = expert_collect(plan, wide_ins, wide_outs, parts, stage, *scratch[28:])
    both = range(2)
    low, high = pl.ds(0, size), pl.ds(size, size)

    def load(layer, block, to_row):
        return pltpu.make_async_copy(
            grads[layer].at[block, to_row * 2 + side],
            mine.at[layer, block, to_row],
            load_sem.at[layer, block, to_row],
        )

    def give(layer, block, to_row):
        return remote(
            grads[layer].at[block, to_row * 2 + 1 - side],
            given.at[layer, block, to_row],
            core_send.at[layer, block, to_row],
            core_recv.at[layer, block, to_row],
            core,
        )

    def send_x_one(block, to_row):
        return remote(
            mine.at[1 - x, block, to_row, low],
            x_one.at[block, to_row],
            x_one_send.at[block, to_row],
            x_one_recv.at[block, to_row],
            across_x,
        )

    def send_y_one(layer, block):
        return remote(
            mine.at[layer, block, 1 - row, high],
            y_one.at[layer, block],
            y_one_send.at[layer, block],
            y_one_recv.at[layer, block],
            across_y,
        )

    def send_y_two(block):
        return remote(
            mine.at[x, block, 1 - row, low],
            y_two.at[block],
            y_two_send.at[block],
            y_two_recv.at[block],
            across_y,
        )

    def send_x_two(block):
        return remote(
            mine.at[1 - x, block, row, high],
            x_two.at[block],
            x_two_send.at[block],
            x_two_recv.at[block],
            across_x,
        )

    def send_chain(block):
        rightward = (block > z).astype(jnp.int32)
        to = z - 1 + 2 * rightward
        into = jnp.where((rightward == 1) & (block == to), nz, block)
        return remote(
            mine.at[x, block, row],
            chain.at[into],
            chain_send.at[block],
            chain_recv.at[into],
            (x, to, s),
        )

    def gain(target, at, other):
        target[at] = (target[at].astype(F32) + other.astype(F32)).astype(BF16)

    def begin(index):
        block = nearest(z, nz - 1 - index, nz)
        for layer in both:
            for to_row in both:
                load(layer, block, to_row).start()
                give(layer, block, to_row).start()

    def stage_core(index):
        block = nearest(z, nz - 1 - index, nz)
        for layer in both:
            for to_row in both:
                load(layer, block, to_row).wait()
                give(layer, block, to_row).wait_recv()
                gain(mine, (layer, block, to_row), given[layer, block, to_row])
        for to_row in both:
            send_x_one(block, to_row).start()
        for layer in both:
            send_y_one(layer, block).start()

    def stage_first(index):
        block = nearest(z, nz - 1 - index, nz)
        for to_row in both:
            send_x_one(block, to_row).wait_recv()
            gain(mine, (x, block, to_row, low), x_one[block, to_row])
        send_y_two(block).start()
        for layer in both:
            send_y_one(layer, block).wait_recv()
            gain(mine, (layer, block, row, high), y_one[layer, block])
        send_x_two(block).start()

    def stage_second(index):
        block = nearest(z, nz - 1 - index, nz)
        origin = ((block < z) & (z == nz - 1)) | ((block > z) & (z == 0))
        send_y_two(block).wait_recv()
        gain(mine, (x, block, row, low), y_two[block])
        send_x_two(block).wait_recv()
        gain(mine, (x, block, row, high), x_two[block])

        @pl.when(origin)
        def _():
            send_chain(block).start()

    begin(0)
    begin(1)
    adds = 0
    for index in range(nz + 3):
        if index < nz:
            stage_core(index)
        if index + 2 < nz:
            begin(index + 2)
        if index == 0:
            start()
        if DEPTH <= index < nz + DEPTH:
            stage_first(index - DEPTH)
        if DEPTH + 1 <= index < nz + DEPTH + 1:
            stage_second(index - DEPTH - 1)
        while adds < count and adds < ADDS[index]:
            add(adds)
            adds += 1
    while adds < count:
        add(adds)
        adds += 1

    def relay(turn, _):
        lower = z < nz // 2
        first = jnp.where(lower, nz - 1 - z, z)
        early = turn < first
        ahead = jnp.where(early, first - turn, nz - 1 - turn)
        rightward = lower == early
        block = jnp.where(rightward, z + ahead, z - ahead)

        @pl.when((z > 0) & (z < nz - 1))
        def _():
            landed(chain.at[block], chain_recv.at[block])
            gain(mine, (x, block, row), chain[block])
            send_chain(block).start()

        return 0

    lax.fori_loop(0, nz - 1, relay, 0)
    out[...] = mine[x, z, row].astype(F32)

    @pl.when(z + 1 < nz)
    def _():
        landed(chain.at[z], chain_recv.at[z])
        out[...] += chain[z].astype(F32)

    @pl.when(z > 0)
    def _():
        landed(chain.at[nz], chain_recv.at[nz])
        out[...] += chain[nz].astype(F32)

    def drain(block, _):
        for layer in both:
            for to_row in both:
                give(layer, block, to_row).wait_send()
            send_y_one(layer, block).wait_send()
        for to_row in both:
            send_x_one(block, to_row).wait_send()
        send_y_two(block).wait_send()
        send_x_two(block).wait_send()

        @pl.when(block != z)
        def _():
            send_chain(block).wait_send()

        return 0

    lax.fori_loop(0, nz, drain, 0)
    finish()


def reduce_call(plan, collective_id, attention, terms):
    nx, nz, ns = plan.nx, plan.nz, plan.ns
    hbm = pl.BlockSpec(memory_space=pltpu.HBM)
    vmem = pl.BlockSpec(memory_space=pltpu.VMEM)
    grads = [part.reshape(nz, ns, -1, part.shape[1]) for part in attention]
    values = [part.reshape(ns, part.shape[0] // ns, D) for layer in terms for part in layer]
    size = grads[0].shape[2:]
    half = (size[0] // 2, size[1])
    return pl.pallas_call(
        functools.partial(reduce_kernel, plan),
        out_shape=[jax.ShapeDtypeStruct(size, F32)]
        + [jax.ShapeDtypeStruct((EXP_DEV,) + part.shape[1:], BF16) for part in values[:2]],
        in_specs=[hbm] * 6,
        out_specs=[vmem, hbm, hbm],
        scratch_shapes=[
            pltpu.VMEM((nx, nz, 2) + size, BF16),
            pltpu.VMEM((nx, nz, 2) + size, BF16),
            pltpu.VMEM((nz, 2) + half, BF16),
            pltpu.VMEM((nx, nz) + half, BF16),
            pltpu.VMEM((nz,) + half, BF16),
            pltpu.VMEM((nz,) + half, BF16),
            pltpu.VMEM((nz + 1,) + size, BF16),
            DMA((nx, nz, 2)),
            DMA((nx, nz, 2)),
            DMA((nx, nz, 2)),
            DMA((nz, 2)),
            DMA((nz, 2)),
            DMA((nx, nz)),
            DMA((nx, nz)),
            DMA((nz,)),
            DMA((nz,)),
            DMA((nz,)),
            DMA((nz,)),
            DMA((nz,)),
            DMA((nz + 1,)),
        ]
        + collect_scratch(plan, values),
        compiler_params=pltpu.CompilerParams(
            collective_id=collective_id, has_side_effects=True, vmem_limit_bytes=VMEM_LIMIT
        ),
    )(*grads, *values)


NARROW = (((1,), (1,)), ((), ()))
ACROSS = (((0,), (0,)), ((), ()))


def greet_shards(plan):
    x, z, s = me()
    barrier = pltpu.get_barrier_semaphore()
    for step in range(1, plan.ns):
        pl.semaphore_signal(
            barrier, inc=1, device_id=(x, z, (s + step) % plan.ns), device_id_type=MESH
        )
    pl.semaphore_wait(barrier, plan.ns - 1)


def turned(value, cosine, sine):
    return value * cosine + pltpu.roll(value, HD // 2, 1) * sine


def weights_of(queries, keys, allowed):
    raw = lax.dot_general(queries, keys, NARROW, preferred_element_type=F32)
    raw = jnp.where(allowed, raw * SCALE, -1e30)
    raw = jnp.exp(raw - jnp.max(raw, axis=1, keepdims=True))
    return raw / jnp.sum(raw, axis=1, keepdims=True)


def attend_kernel(plan, layer, *refs):
    (start, gains, cosine, sine, mask, weights) = refs[:6]
    (middle, normed, low, queries, kv, mixed) = refs[6:12]
    (win_v, wout_v, load_sem, send, recv) = refs[12:]
    x, z, s = me()
    tokens, rows, micro, ns = plan.tokens, plan.rows, plan.micro, plan.ns
    length = ns * tokens
    load_in = pltpu.make_async_copy(weights.at[layer, :, pl.ds(0, WIN)], win_v, load_sem.at[0])
    load_out = pltpu.make_async_copy(weights.at[layer, :, pl.ds(WIN, D)], wout_v, load_sem.at[1])
    load_in.start()
    load_out.start()
    greet_shards(plan)

    hidden = start[...].astype(F32)
    inverse = lax.rsqrt(jnp.mean(hidden * hidden, axis=1, keepdims=True) + epsilon)
    low[...] = (hidden * inverse * gains[0:1, :]).astype(BF16)
    load_in.wait()
    own = jnp.dot(low[...], win_v[:, WQ : WQ + 2 * WK], preferred_element_type=F32)
    for head in range(KV_HEADS):
        at = slice(head * HD, (head + 1) * HD)
        key = turned(own[:, at], cosine[...], sine[...]).astype(BF16)
        value = own[:, WK + head * HD : WK + (head + 1) * HD].astype(BF16)
        for m in range(micro):
            block = slice(m * tokens, (m + 1) * tokens)
            kv[s, m, :, at] = key[block]
            kv[s, m, :, WK + head * HD : WK + (head + 1) * HD] = value[block]

    def share(step, m):
        return remote(
            kv.at[s, m],
            kv.at[s, m],
            send.at[step - 1, m],
            recv.at[s, m],
            (x, z, (s + step) % ns),
        )

    for m in range(micro):
        for step in range(1, ns):
            share(step, m).start()

    def project(step, _):
        at = pl.multiple_of(step * 4 * HD, 4 * HD)
        part = jnp.dot(low[...], win_v[:, pl.ds(at, 4 * HD)], preferred_element_type=F32)
        for head in range(4):
            here = part[:, head * HD : (head + 1) * HD]
            queries[:, pl.ds(at + head * HD, HD)] = turned(here, cosine[...], sine[...]).astype(
                BF16
            )
        return 0

    lax.fori_loop(0, HEADS // 4, project, 0)

    def group(turn, _):
        m, pair = turn // KV_HEADS, turn % KV_HEADS

        @pl.when(pair == 0)
        def _():
            for step in range(1, ns):
                landed(kv.at[(s + step) % ns, m], recv.at[(s + step) % ns, m])

        span = pl.ds(pl.multiple_of(m * tokens, tokens), tokens)
        keys = kv[:, m, :, pl.ds(pl.multiple_of(pair * HD, HD), HD)].reshape(length, HD)
        values = kv[:, m, :, pl.ds(pl.multiple_of(WK + pair * HD, HD), HD)].reshape(length, HD)
        allowed = mask[m] > 0
        for i in range(GROUP):
            at = pl.ds(pl.multiple_of((pair * GROUP + i) * HD, HD), HD)
            probs = weights_of(queries[span, at], keys, allowed).astype(BF16)
            mixed[span, at] = jnp.dot(probs, values, preferred_element_type=F32).astype(BF16)
        return 0

    lax.fori_loop(0, micro * KV_HEADS, group, 0)
    load_out.wait()

    def back(step, _):
        at = pl.ds(pl.multiple_of(step * 512, 512), 512)
        middle[:, at] = start[:, at].astype(F32) + jnp.dot(
            mixed[...], wout_v[:, at], preferred_element_type=F32
        )
        return 0

    lax.fori_loop(0, D // 512, back, 0)
    after = middle[...]
    inverse = lax.rsqrt(jnp.mean(after * after, axis=1, keepdims=True) + epsilon)
    normed[...] = (after * inverse * gains[1:2, :]).astype(BF16)
    for m in range(micro):
        for step in range(1, ns):
            share(step, m).wait_send()


def attend_call(plan, layer, collective_id, start, gains, tables, weights):
    rows, ns, micro = plan.rows, plan.ns, plan.micro
    vmem = pl.BlockSpec(memory_space=pltpu.VMEM)
    hbm = pl.BlockSpec(memory_space=pltpu.HBM)
    shape = jax.ShapeDtypeStruct
    return pl.pallas_call(
        functools.partial(attend_kernel, plan, layer),
        out_shape=[
            shape((rows, D), F32),
            shape((rows, D), BF16),
            shape((rows, D), BF16),
            shape((rows, WQ), BF16),
            shape((ns, micro, plan.tokens, 2 * WK), BF16),
            shape((rows, WQ), BF16),
        ],
        in_specs=[vmem] * 5 + [hbm],
        out_specs=[vmem] * 6,
        scratch_shapes=[
            pltpu.VMEM((D, WIN), BF16),
            pltpu.VMEM((WQ, D), BF16),
            DMA((2,)),
            DMA((ns - 1, micro)),
            DMA((ns, micro)),
        ],
        compiler_params=pltpu.CompilerParams(
            collective_id=collective_id, has_side_effects=True, vmem_limit_bytes=VMEM_LIMIT
        ),
    )(start, gains, *tables, weights)


def return_kernel(plan, layer, *refs):
    (grad_out, grad_moe, middle, start, low, queries, kv, mixed) = refs[:8]
    (gains, cosine, sine, mask, weights) = refs[8:13]
    (grad_in, terms) = refs[13:15]
    (win_v, wout_v, branch, grad_mixed, both, part, got, in_v, out_v) = refs[15:24]
    (load_sem, save_in, save_out, send, recv) = refs[24:]
    x, z, s = me()
    tokens, rows, micro, ns = plan.tokens, plan.rows, plan.micro, plan.ns
    length = ns * tokens
    load_in = pltpu.make_async_copy(weights.at[layer, :, pl.ds(0, WIN)], win_v, load_sem.at[0])
    load_out = pltpu.make_async_copy(weights.at[layer, :, pl.ds(WIN, D)], wout_v, load_sem.at[1])
    load_out.start()
    load_in.start()
    greet_shards(plan)

    after = middle[...]
    inverse = lax.rsqrt(jnp.mean(after * after, axis=1, keepdims=True) + epsilon)
    scaled = grad_moe[...] * gains[1:2, :]
    inner = jnp.mean(scaled * after, axis=1, keepdims=True)
    total = grad_out[...].astype(F32) + inverse * scaled - after * (
        inverse * inverse * inverse * inner
    )
    grad_in[...] = total
    branch[...] = total.astype(BF16)
    gain_two = jnp.sum(grad_moe[...] * after * inverse, axis=0, keepdims=True)
    load_out.wait()

    def mix(step, _):
        at = pl.ds(pl.multiple_of(step * 512, 512), 512)
        grad_mixed[:, at] = lax.dot_general(
            branch[...], wout_v[at, :], NARROW, preferred_element_type=F32
        ).astype(BF16)
        return 0

    lax.fori_loop(0, WQ // 512, mix, 0)

    def share(step, m):
        to = (s + step) % ns
        return remote(
            part.at[to, m],
            got.at[s, m],
            send.at[step - 1, m],
            recv.at[s, m],
            (x, z, to),
        )

    def group(turn, _):
        m, pair = turn // KV_HEADS, turn % KV_HEADS
        span = pl.ds(pl.multiple_of(m * tokens, tokens), tokens)
        key_at = pl.ds(pl.multiple_of(pair * HD, HD), HD)
        value_at = pl.ds(pl.multiple_of(WK + pair * HD, HD), HD)
        keys = kv[:, m, :, key_at].reshape(length, HD)
        values = kv[:, m, :, value_at].reshape(length, HD)
        allowed = mask[m] > 0
        grad_keys = jnp.zeros((length, HD), F32)
        grad_values = jnp.zeros((length, HD), F32)
        for i in range(GROUP):
            at = pl.ds(pl.multiple_of((pair * GROUP + i) * HD, HD), HD)
            mine, given = queries[span, at], grad_mixed[span, at]
            probs = weights_of(mine, keys, allowed)
            grad_probs = lax.dot_general(given, values, NARROW, preferred_element_type=F32)
            inside = jnp.sum(grad_probs * probs, axis=1, keepdims=True)
            raw = (probs * (grad_probs - inside) * SCALE).astype(BF16)
            grad_query = jnp.dot(raw, keys, preferred_element_type=F32)
            both[span, at] = turned(grad_query, cosine[span], -sine[span]).astype(BF16)
            grad_keys += lax.dot_general(raw, mine, ACROSS, preferred_element_type=F32)
            grad_values += lax.dot_general(
                probs.astype(BF16), given, ACROSS, preferred_element_type=F32
            )
        part[:, m, :, key_at] = grad_keys.astype(BF16).reshape(ns, tokens, HD)
        part[:, m, :, value_at] = grad_values.astype(BF16).reshape(ns, tokens, HD)

        @pl.when(pair == KV_HEADS - 1)
        def _():
            for step in range(1, ns):
                share(step, m).start()

        return 0

    lax.fori_loop(0, micro * KV_HEADS, group, 0)

    def out_copy(step):
        at = pl.ds(step * 256, 256)
        return pltpu.make_async_copy(out_v.at[at], terms.at[at, pl.ds(WIN, D)], save_out.at[step])

    def in_copy(step):
        at = pl.ds(step * 256, 256)
        return pltpu.make_async_copy(in_v.at[at], terms.at[at, pl.ds(0, WIN)], save_in.at[step])

    def out_tile(step, _):
        at = pl.ds(pl.multiple_of(step * 256, 256), 256)
        out_v[at, :] = lax.dot_general(
            mixed[:, at], branch[...], ACROSS, preferred_element_type=F32
        ).astype(BF16)
        out_copy(step).start()
        return 0

    lax.fori_loop(0, WQ // 256, out_tile, 0)
    load_in.wait()
    for m in range(micro):
        for step in range(1, ns):
            landed(got.at[(s + step) % ns, m], recv.at[(s + step) % ns, m])
        span = slice(m * tokens, (m + 1) * tokens)
        total = part[s, m].astype(F32)
        for step in range(1, ns):
            total += got[(s + step) % ns, m].astype(F32)
        for head in range(KV_HEADS):
            at = slice(head * HD, (head + 1) * HD)
            both[span, WQ + head * HD : WQ + (head + 1) * HD] = turned(
                total[:, at], cosine[span], -sine[span]
            ).astype(BF16)
        both[span, WQ + WK :] = total[:, WK:].astype(BF16)

    def in_tile(step, _):
        at = pl.ds(pl.multiple_of(step * 256, 256), 256)
        in_v[at, : WQ + 2 * WK] = lax.dot_general(
            low[:, at], both[...], ACROSS, preferred_element_type=F32
        ).astype(BF16)
        return 0

    lax.fori_loop(0, D // 256, in_tile, 0)
    grad_normed = []
    for step in range(D // 512):
        at = slice(step * 512, (step + 1) * 512)
        grad_normed.append(
            lax.dot_general(
                both[...], win_v[at, : WQ + 2 * WK], NARROW, preferred_element_type=F32
            )
        )
    grad_normed = jnp.concatenate(grad_normed, axis=1)
    hidden = start[...].astype(F32)
    inverse = lax.rsqrt(jnp.mean(hidden * hidden, axis=1, keepdims=True) + epsilon)
    scaled = grad_normed * gains[0:1, :]
    inner = jnp.mean(scaled * hidden, axis=1, keepdims=True)
    grad_in[...] += inverse * scaled - hidden * (inverse * inverse * inverse * inner)
    gain_one = jnp.sum(grad_normed * hidden * inverse, axis=0, keepdims=True)
    place = lax.broadcasted_iota(jnp.int32, (128, D), 0)
    rows_of = jnp.where(place == 0, gain_one, jnp.where(place == 1, gain_two, 0.0))
    in_v[:, WQ + 2 * WK :] = rows_of.T.astype(BF16)
    for step in range(D // 256):
        in_copy(step).start()
    for step in range(D // 256):
        in_copy(step).wait()
        out_copy(step).wait()
    for m in range(micro):
        for step in range(1, ns):
            share(step, m).wait_send()


def return_call(plan, layer, collective_id, grads, saved, gains, tables, weights):
    rows, ns, micro, tokens = plan.rows, plan.ns, plan.micro, plan.tokens
    vmem = pl.BlockSpec(memory_space=pltpu.VMEM)
    hbm = pl.BlockSpec(memory_space=pltpu.HBM)
    shape = jax.ShapeDtypeStruct
    exchange = (ns, micro, tokens, 2 * WK)
    return pl.pallas_call(
        functools.partial(return_kernel, plan, layer),
        out_shape=[
            shape((rows, D), F32),
            shape((D, WIN + D), BF16),
        ],
        in_specs=[vmem] * 12 + [hbm],
        out_specs=[vmem, hbm],
        scratch_shapes=[
            pltpu.VMEM((D, WIN), BF16),
            pltpu.VMEM((WQ, D), BF16),
            pltpu.VMEM((rows, D), BF16),
            pltpu.VMEM((rows, WQ), BF16),
            pltpu.VMEM((rows, WQ + 2 * WK), BF16),
            pltpu.VMEM(exchange, BF16),
            pltpu.VMEM(exchange, BF16),
            pltpu.VMEM((D, WIN), BF16),
            pltpu.VMEM((WQ, D), BF16),
            DMA((2,)),
            DMA((D // 256,)),
            DMA((WQ // 256,)),
            DMA((ns - 1, micro)),
            DMA((ns, micro)),
        ],
        compiler_params=pltpu.CompilerParams(
            collective_id=collective_id, has_side_effects=True, vmem_limit_bytes=VMEM_LIMIT
        ),
    )(*grads, *saved, gains, *tables, weights)


def slot_tables(plan, routes, gates):
    experts, nz = plan.experts, plan.nz
    named = routes[..., None] == jnp.arange(experts, dtype=jnp.int32)
    gate = jnp.sum(jnp.where(named, gates[..., None], 0.0), axis=2)
    named = jnp.any(named, axis=2)
    earlier = jnp.tril(jnp.ones((plan.tokens, plan.tokens), BF16), -1)
    rank = jnp.einsum("ut,mte->mue", earlier, named.astype(BF16), preferred_element_type=F32)
    table = jnp.stack([jnp.where(named, rank, -1.0), gate])
    table = table.reshape(2, plan.micro, plan.tokens, nz, EXP_DEV).transpose(3, 0, 1, 4, 2)
    table = lax.all_to_all(table, "expert", split_axis=0, concat_axis=0, tiled=True)
    rank, gate = table[:, 0], table[:, 1]
    first = jnp.arange(plan.micro, dtype=F32)[:, None, None] * plan.capacity
    place = jnp.where(rank >= 0, rank + first, -1.0).transpose(0, 2, 1, 3)
    hit = place[:, :, None] == jnp.arange(plan.slots, dtype=F32)[:, None, None]
    shape = (nz, EXP_DEV * plan.slots, plan.rows)
    one = hit.astype(BF16).reshape(shape)
    weighted = jnp.where(hit, gate.transpose(0, 2, 1, 3)[:, :, None], 0.0)
    weighted = weighted.astype(BF16).reshape(shape)
    return one, weighted


def shards(
    inputs,
    segments,
    routes,
    gate_weights,
    query_weight,
    key_value_weight,
    output_weight,
    norm_gains,
    expert_gate_up,
    expert_down,
    cotangent,
):
    section = lax.axis_index("section")
    shard_index = lax.axis_index("shard")
    tokens = inputs.shape[1]
    plan = Plan((lax.axis_size("section"), lax.axis_size("expert"), lax.axis_size("shard")), tokens)
    micro, rows, layers = plan.micro, plan.rows, plan.nx
    length = tokens * plan.ns

    def mine(value):
        return lax.dynamic_slice_in_dim(value, section * micro, micro, 0)

    paired = plan.nx == 2 and plan.ns == 4 and query_weight.shape[1] % 32 == 0
    gain_columns = jnp.pad(norm_gains[0].T, ((0, 0), (0, PAD - 2)))
    attention_weights = jnp.concatenate(
        [query_weight[0], key_value_weight[0], gain_columns, output_weight[0]], axis=1
    ).astype(BF16)
    expert_weights = (expert_gate_up[0].astype(BF16), expert_down[0].astype(BF16))
    if paired:
        weights, wide_in, wide_down = gather_call(plan, 1, attention_weights, expert_weights)
    else:
        weights = lax.all_gather(
            attention_weights, ("section", "expert", "shard"), axis=0, tiled=True
        )
        wide_in, wide_down = spread_call(plan, 1, *expert_weights)
    weights = weights.reshape(layers, D, WIN + D)
    gains = weights[:, :, PROJ : PROJ + 2].transpose(0, 2, 1).astype(F32)
    wide_in = wide_in.reshape(layers, D, 2 * FF)
    wide_down = wide_down.reshape(layers, FF, D)
    one, weighted = slot_tables(plan, mine(routes), mine(gate_weights))

    offset = shard_index * tokens
    position = (offset + jnp.arange(tokens, dtype=jnp.int32)).astype(F32)
    frequency = rope_base ** (-jnp.arange(HD // 2, dtype=F32) / (HD // 2))
    angles = position[:, None] * frequency[None, :]
    cosine, sine = jnp.cos(angles), jnp.sin(angles)
    cosine = jnp.tile(jnp.concatenate([cosine, cosine], axis=1), (micro, 1))
    sine = jnp.tile(jnp.concatenate([-sine, sine], axis=1), (micro, 1))
    segment_all = mine(segments)[:, 0]
    segment_own = lax.dynamic_slice_in_dim(segment_all, offset, tokens, 1)
    query_place = offset + jnp.arange(tokens, dtype=jnp.int32)
    key_place = jnp.arange(length, dtype=jnp.int32)
    allowed = (segment_own[:, :, None] == segment_all[:, None, :]) & (
        query_place[:, None] >= key_place[None, :]
    )
    tables = (cosine, sine, allowed.astype(F32))

    hidden = mine(inputs).reshape(rows, D)
    kept = []
    for layer in range(layers):
        start = hidden.astype(BF16)
        middle, normed, low, queries, kv, mixed = attend_call(
            plan, layer, 2 + layer, start, gains[layer], tables, weights
        )
        hidden, sent, gate_up, hidden_low = moe_call(
            plan,
            layer,
            False,
            2 + layers + layer,
            normed,
            one,
            weighted,
            wide_in,
            wide_down,
            middle,
        )
        kept.append(((middle, start, low, queries, kv, mixed), sent, gate_up, hidden_low))
    output = hidden.reshape(micro, tokens, D)

    grad = mine(cotangent).reshape(rows, D)
    attention_terms = [None] * layers
    expert_terms = [None] * layers
    for layer in reversed(range(layers)):
        saved, sent, gate_up, hidden_low = kept[layer]
        grad_out = grad.astype(BF16)
        grad_moe, grad_sent, grad_both = moe_call(
            plan,
            layer,
            True,
            2 + 2 * layers + layer,
            grad_out,
            weighted,
            one,
            wide_in,
            wide_down,
            gate_up,
        )
        in_term = jnp.einsum(
            "rd,rf->df",
            sent.reshape(-1, D),
            grad_both.reshape(-1, 2 * FF),
            preferred_element_type=F32,
        ).astype(BF16)
        down_term = jnp.einsum(
            "rf,rd->fd",
            hidden_low.reshape(-1, FF),
            grad_sent.reshape(-1, D),
            preferred_element_type=F32,
        ).astype(BF16)
        expert_terms[layer] = (in_term, down_term)
        grad, attention_terms[layer] = return_call(
            plan,
            layer,
            2 + 3 * layers + layer,
            (grad_out, grad_moe),
            saved,
            gains[layer],
            tables,
            weights,
        )
    input_grad = grad.reshape(micro, tokens, D)

    if paired:
        term, gate_up_grad, down_grad = reduce_call(
            plan, 2 + 4 * layers, attention_terms, expert_terms
        )
    else:
        gate_up_grad, down_grad = collect_call(plan, 2 + 4 * layers, expert_terms)
        term = lax.psum_scatter(
            jnp.concatenate(attention_terms),
            ("section", "expert", "shard"),
            scatter_dimension=0,
            tiled=True,
        )
    query_grad, key_value_grad, gain_grad, output_weight_grad, gate_up_grad, down_grad = (
        part.astype(F32)[None]
        for part in (
            term[:, :WQ],
            term[:, WQ:PROJ],
            term[:, PROJ : PROJ + 2].T,
            term[:, WIN:],
            gate_up_grad,
            down_grad,
        )
    )
    return (
        output,
        input_grad,
        query_grad,
        key_value_grad,
        output_weight_grad,
        gain_grad,
        gate_up_grad,
        down_grad,
    )


def solution(mesh):
    placed = (
        P(None, ("expert", "shard"), None),
        P(None, "expert", None),
        P(None, ("expert", "shard"), None),
        P(None, ("expert", "shard"), None),
        P("section", ("expert", "shard"), None),
        P("section", ("expert", "shard"), None),
        P("section", ("expert", "shard"), None),
        P("section", None, ("expert", "shard")),
        P("section", "expert", "shard", None),
        P("section", "expert", "shard", None),
        P(None, ("expert", "shard"), None),
    )
    return jax.shard_map(
        shards,
        mesh=mesh,
        in_specs=placed,
        out_specs=(
            P("section", ("expert", "shard"), None),
            P("section", ("expert", "shard"), None),
            P("section", ("expert", "shard"), None),
            P("section", ("expert", "shard"), None),
            P("section", ("expert", "shard"), None),
            P("section", None, ("expert", "shard")),
            P("section", "expert", "shard", None),
            P("section", "expert", "shard", None),
        ),
        check_vma=False,
    )
```

time: 1460 us -> 1140 us (0.78)
  matrix products: 163 us -> 29.9 us
  local copies, waits for them, and re-layouts: 92.6 us -> 19.3 us
  other arithmetic: 73 us -> 32.8 us
  blocking collectives: 30.2 us -> 0 us
  waiting for transfers between devices: 30.2 us -> 0.01 us
    dot_general x22 -> x0, matrix products: 119 us -> none  [the longest x2 22.1 us: attend_backward(): jnp.einsum('mhqk,mhqd->mkhd', grad_raw, stacked, preferred_element_type=F32)]
    pallas_call x4 -> x8, Pallas kernels: 605 us -> 667 us  [the longest x4 541 us: moe_call(): pl.pallas_call(functools.partial(moe_kernel, plan, layer, backward), out_...]
    slice x18 -> x0, local copies, waits for them, and re-layouts: 37.7 us -> none  [the longest x1 10.6 us: attend_forward(): projected = jnp.dot(low, weight_in[layer], preferred_element_type=F32)]
    pallas_call x1, Pallas kernels: 217 us -> 183 us  [reduce_call(): pl.pallas_call(functools.partial(reduce_kernel, plan), out_shape=[jax.Sha...]
    unnamed x8 -> x0, waiting for transfers between devices: 30.2 us -> none
    all_gather x4 -> x0, blocking collectives: 30.2 us -> none  [attend_forward(): lax.all_gather(local_kv[i], 'shard', axis=0, tiled=True)]
    unnamed x214 -> x33, local copies, waits for them, and re-layouts: 30.8 us -> 4.61 us
    pallas_call x1, Pallas kernels: 211 us -> 190 us  [gather_call(): pl.pallas_call(functools.partial(gather_kernel, plan), out_shape=outs, in...]
  transfers between devices with their start and end apart: 5 -> 1, of which waited for: 2 -> 0; matrix products, arithmetic and copies ran while one was open for 10% -> 2% of each run, Pallas kernels for 15% -> 19%
where the time goes in v3:
time: 1140 us; the launch traced here: 1130 us
  Pallas kernels  1040 us (91%)
  other arithmetic  32.8 us (3%)
  matrix products  29.9 us (3%)
  local copies, waits for them, and re-layouts  19.3 us (2%)
    pallas_call x4, Pallas kernels, moe_call(): pl.pallas_call(functools.partial(moe_kernel, plan, layer, backward), out_...  541 us
    pallas_call x1, Pallas kernels, gather_call(): pl.pallas_call(functools.partial(gather_kernel, plan), out_shape=outs, in...  190 us
    pallas_call x1, Pallas kernels, reduce_call(): pl.pallas_call(functools.partial(reduce_kernel, plan), out_shape=[jax.Sha...  183 us
    pallas_call x2, Pallas kernels, return_call(): pl.pallas_call(functools.partial(return_kernel, plan, layer), out_shape=[...  74.8 us
    pallas_call x2, Pallas kernels, attend_call(): pl.pallas_call(functools.partial(attend_kernel, plan, layer), out_shape=[...  51.4 us
  transfers between devices with their start and end apart: 1, of which 0 were waited for; matrix products, arithmetic and copies ran while one was open for 2% of the time, Pallas kernels for 19%

profile of v3, /device:TPU:0, one launch (start us, length us, event | category | flops | bytes accessed | tf_op | source)
XLA Modules:
  0.0 1129.9 jit_solution(8935828426982193932)
XLA Ops:
  0.6 0.0 copy-start
  0.7 0.7 constant_dynamic-slice_fusion.2
  1.4 0.7 constant_dynamic-slice_fusion.1
  2.1 0.2 fusion.2
  2.3 0.6 copy.53
  2.9 6.3 all-to-all-start
  9.3 0.8 copy.51
  10.1 0.1 iota_compare_fusion.2
  10.2 0.9 convert_bitcast_fusion.5
  11.2 0.3 fusion.10
  11.5 0.1 pad_maximum_fusion
  11.6 4.0 convert_bitcast_fusion.1.refs_2_
  15.6 6.5 convert_bitcast_fusion.refs_1_
  22.2 0.1 convert_bitcast_fusion.3
  22.2 0.9 fusion.4.refs_0_
  23.1 190.3 %shard_map.170 = (bf16[2,4,4,96,3712]{4,3,2,1,0:T(8,128)(2,1)}, bf16[2,4,384,1536]{3,2,1,0:T(8,128)(2,1)}, bf16[2,4,192,1536]{3,2,1,0:T(8,128)(2,1)}) custom-call(bf16[96,3712]{1,0:T(8,128)(2,1)} %fusion.4.refs_0_, bf16[4,384,1536]{2,1,0:T(8,128)(2,1)} %convert_bitcast_fusion.refs_1_, bf16[4,192,1536]{2,1,0:T(8,128)(2,1)} %convert_bitcast_fusion.1.refs_2_), custom_call_target="tpu_custom_call" | custom-call | tf_op jit(solution)/shard_map/pallas_call | solution.py:778
  213.4 0.0 copy-start.7
  213.5 1.4 convert_bitcast_fusion.2
  214.8 0.1 slice_bitcast_fusion
  214.9 0.1 constant_dynamic-slice_fusion.4
  215.0 0.1 pad_maximum_fusion.1
  215.1 0.0 copy-done.7
  215.1 2.4 constant_dynamic-slice_fusion
  217.5 0.9 and_convert_fusion.refs_4_.refs_11_
  218.5 0.1 eq.62
  218.6 0.9 copy.56.refs_1_.refs_8_
  219.4 0.9 copy.52.refs_1_.refs_8_
  220.3 0.7 tile.20
  221.0 0.7 tile.8
  221.6 25.6 %shard_map.171 = (f32[256,1536]{1,0:T(8,128)}, bf16[256,1536]{1,0:T(8,128)(2,1)}, bf16[256,1536]{1,0:T(8,128)(2,1)}, bf16[256,1536]{1,0:T(8,128)(2,1)}, bf16[4,2...) custom-call(bf16[256,1536]{1,0:T(8,128)(2,1)} %bitcast.101, f32[2,1536]{1,0:T(2,128)} %copy.52.refs_1_.refs_8_, ...), custom_call_target="tpu_custom_call" | custom-call | tf_op jit(solution)/shard_map/pallas_call | solution.py:1300
  247.2 0.0 all-to-all-done
  247.2 0.1 select_bitcast_fusion
  247.4 0.3 broadcast_in_dim.84
  247.7 0.4 broadcast_in_dim.85
  248.1 0.3 eq.59
  248.5 1.0 eq.60
  249.5 1.2 select_convert_fusion
  250.7 1.0 convert_element_type.66.refs_1_.refs_2_
  251.7 133.6 %shard_map.172 = (f32[256,1536]{1,0:T(8,128)}, bf16[2,8,80,1536]{3,2,1,0:T(8,128)(2,1)}, bf16[2,640,1536]{2,1,0:T(8,128)(2,1)}, bf16[2,640,768]{2,1,0:T(8,128)(2,1)}) custom-call(bf16[256,1536]{1,0:T(8,128)(2,1)} %get-tuple-element.45.refs_0_, bf16[4,320,256]{2,1,0:T(8,128)(2,1)} %convert_element_type.66.refs_1_.refs_2_, ...), custom_call_target="tpu_custom_call" | custom-call | flops 99999997952 | bytes 30000000 | tf_op jit(solution)/shard_map/pallas_call | solution.py:485
  385.3 2.4 convert_element_type.68.refs_0_.refs_3_
  387.6 25.8 %shard_map.173 = (f32[256,1536]{1,0:T(8,128)}, bf16[256,1536]{1,0:T(8,128)(2,1)}, bf16[256,1536]{1,0:T(8,128)(2,1)}, bf16[256,1536]{1,0:T(8,128)(2,1)}, bf16[4,2...) custom-call(bf16[256,1536]{1,0:T(8,128)(2,1)} %convert_element_type.68.refs_0_.refs_3_, ...), custom_call_target="tpu_custom_call" | custom-call | tf_op jit(solution)/shard_map/pallas_call | solution.py:1300
  413.5 134.6 %shard_map.174 = (f32[256,1536]{1,0:T(8,128)}, bf16[2,8,80,1536]{3,2,1,0:T(8,128)(2,1)}, bf16[2,640,1536]{2,1,0:T(8,128)(2,1)}, bf16[2,640,768]{2,1,0:T(8,128)(2,1)}) custom-call(bf16[256,1536]{1,0:T(8,128)(2,1)} %get-tuple-element.50.refs_0_, bf16[4,320,256]{2,1,0:T(8,128)(2,1)} %convert_element_type.66.refs_1_.refs_2_, ...), custom_call_target="tpu_custom_call" | custom-call | flops 99999997952 | bytes 30000000 | tf_op jit(solution)/shard_map/pallas_call | solution.py:485
  548.1 134.9 %shard_map.175 = (f32[256,1536]{1,0:T(8,128)}, bf16[2,8,80,1536]{3,2,1,0:T(8,128)(2,1)}, bf16[2,640,1536]{2,1,0:T(8,128)(2,1)}) custom-call(bf16[256,1536]{1,0:T(8,128)(2,1)} %bitcast.113, bf16[4,320,256]{2,1,0:T(8,128)(2,1)} %get-tuple-element.112.refs_2_.refs_1_, bf16[4,320,256]{2,1,0:T(8,128)(2,1)} %convert_element_type.66.refs_1_.refs_2_, ...), custom_call_target="tpu_custom_call" | custom-call | flops 99999997952 | bytes 30000000 | tf_op jit(solution)/shard_map/pallas_call | solution.py:485
  683.0 37.5 %shard_map.176 = (f32[256,1536]{1,0:T(8,128)}, bf16[1536,3712]{1,0:T(8,128)(2,1)}) custom-call(bf16[256,1536]{1,0:T(8,128)(2,1)} %bitcast.114, f32[256,1536]{1,0:T(8,128)} %get-tuple-element.54.refs_1_, f32[256,1536]{1,0:T(8,128)} %get-tuple-element.51.refs_5_.refs_2_, bf16[256,1536]{1,0:T(8,128)(2,1)} %convert_element_type.68.refs_0_.refs_3_, ...), custom_call_target="tpu_custom_call" | custom-call | tf_op jit(solution)/shard_map/pallas_call | solution.py:1480
  720.5 2.4 convert_element_type.69.refs_0_
  722.9 10.1 convolution_convert_fusion
  733.0 0.0 copy-done.13
  733.0 4.7 convolution_convert_fusion.2
  737.7 138.0 %shard_map.177 = (f32[256,1536]{1,0:T(8,128)}, bf16[2,8,80,1536]{3,2,1,0:T(8,128)(2,1)}, bf16[2,640,1536]{2,1,0:T(8,128)(2,1)}) custom-call(bf16[256,1536]{1,0:T(8,128)(2,1)} %convert_element_type.69.refs_0_, bf16[4,320,256]{2,1,0:T(8,128)(2,1)} %get-tuple-element.112.refs_2_.refs_1_, bf16[4,320,256]{2,1,0:T(8,128)(2,1)} %convert_element_type.66.refs_1_.refs_2_, ...), custom_call_target="tpu_custom_call" | custom-call | flops 99999997952 | bytes 30000000 | tf_op jit(solution)/shard_map/pallas_call | solution.py:485
  875.8 0.0 copy-done.8
  875.8 0.0 copy-start.11
  875.8 10.1 convolution_convert_fusion.1
  885.9 4.7 convolution_convert_fusion.3
  890.6 37.3 %shard_map.178 = (f32[256,1536]{1,0:T(8,128)}, bf16[1536,3712]{1,0:T(8,128)(2,1)}) custom-call(bf16[256,1536]{1,0:T(8,128)(2,1)} %convert_element_type.69.refs_0_, f32[256,1536]{1,0:T(8,128)} %get-tuple-element.61.refs_1_, f32[256,1536]{1,0:T(8,128)} %get-tuple-element.48.refs_5_.refs_2_, bf16[256,1536]{1,0:T(8,128)(2,1)} %bitcast.102, ...), custom_call_target="tpu_custom_call" | custom-call | tf_op jit(solution)/shard_map/pallas_call | solution.py:1480
  927.9 182.6 %shard_map.179 = (f32[96,3712]{1,0:T(8,128)}, bf16[4,384,1536]{2,1,0:T(8,128)(2,1)}, bf16[4,192,1536]{2,1,0:T(8,128)(2,1)}) custom-call(bf16[4,4,96,3712]{3,2,1,0:T(8,128)(2,1)} %bitcast.100, bf16[4,4,96,3712]{3,2,1,0:T(8,128)(2,1)} %bitcast.99, bf16[4,384,1536]{2,1,0:T(8,128)(2,1)} %bitcast.104, bf16[4,192,1536]{2,1,0:T(8,128)(2,1)} %bitcast.116, ...), custom_call_target="tpu_custom_call" | custom-call | tf_op jit(solution)/shard_map/pallas_call | solution.py:1146
  1110.6 0.8 slice_bitcast_fusion.5
  1111.4 1.6 slice_bitcast_fusion.4
  1113.0 2.3 slice_bitcast_fusion.2
  1115.3 0.6 copy.59
  1115.9 7.6 bitcast_convert_fusion
  1123.5 2.8 bitcast_convert_fusion.1
  1126.3 1.1 copy.65
  1127.5 0.8 copy-done.4
  1128.3 1.1 copy.66
  (34 shorter events, 0.2 us)
Async XLA Ops:
  0.6 8.6 copy-start
  2.9 244.3 %all-to-all-start = ((f32[4,2,2,4,128]{4,3,2,1,0:T(4,128)}), f32[4,2,2,4,128]{4,3,2,1,0:T(4,128)S(1)}, u32[]{:S(2)}, u32[]{:S(2)}) async-start(f32[4,2,2,4,128]{4,3,2,1,0:T(4,128)} %copy.53), calls=%async_computation | async-start | bytes 65536 | tf_op jit(solution)/shard_map/all_to_all | solution.py:1519
  15.6 6.6 copy-start.5
  15.6 6.6 copy-start.6
  213.4 1.7 copy-start.7
  683.0 39.9 %copy-start.9 = (bf16[2,8,80,1536]{3,2,1,0:T(8,128)(2,1)S(1)}, bf16[2,8,80,1536]{3,2,1,0:T(8,128)(2,1)}, u32[]{:S(2)}) copy-start(bf16[2,8,80,1536]{3,2,1,0:T(8,128)(2,1)} %get-tuple-element.73) | copy-start | bytes 11796484
  722.9 10.1 copy-start.10
  722.9 10.1 copy-start.13
  737.7 138.0 %copy-start.8 = (bf16[2,8,80,1536]{3,2,1,0:T(8,128)(2,1)S(1)}, bf16[2,8,80,1536]{3,2,1,0:T(8,128)(2,1)}, u32[]{:S(2)}) copy-start(bf16[2,8,80,1536]{3,2,1,0:T(8,128)(2,1)} %get-tuple-element.69) | copy-start | bytes 11796484
  875.8 10.2 copy-start.11
  875.8 10.2 copy-start.12
  1115.9 7.6 copy-start.2
  1123.5 2.8 copy-start.3
  1126.3 2.0 copy-start.4
  1126.3 3.1 copy-start.1

commit v4 on v3

--- a/solution.py
+++ b/solution.py
@@ -1,4 +1,6 @@
 import functools
+import math
+from types import SimpleNamespace
 
 import jax
 import jax.numpy as jnp
@@ -30,7 +32,7 @@
 F32 = jnp.float32
 BF16 = jnp.bfloat16
 DMA = pltpu.SemaphoreType.DMA
-VMEM_LIMIT = 60 * 2**20
+VMEM_LIMIT = 62 * 2**20
 
 
 class Plan:
@@ -98,44 +100,16 @@
     return jnp.where(index <= 2 * short, near, far)
 
 
+NARROW = (((1,), (1,)), ((), ()))
+ACROSS = (((0,), (0,)), ((), ()))
 TILE = 256
 CUTS = 3
 CUT = D // CUTS
 
 
-def moe_kernel(plan, layer, backward, *refs):
-    if backward:
-        (rows_in, put, take, w_in, w_down, gate_up, out, sent_save, grad_save) = refs[:9]
-        scratch = refs[9:]
-    else:
-        (rows_in, put, take, w_in, w_down, base, out, sent_save, gate_up, hidden) = refs[:10]
-        scratch = refs[10:]
-    (
-        line,
-        sbuf,
-        xbuf,
-        ybuf,
-        rbuf,
-        pbuf,
-        qbuf,
-        win_v,
-        wdown_v,
-        gbuf,
-        zbuf,
-        line_recv,
-        line_right,
-        line_left,
-        to_send,
-        to_recv,
-        back_send,
-        back_recv,
-        sum_send,
-        sum_recv,
-        local_sem,
-        save_sem,
-    ) = scratch
+def moe_stages(plan, backward, r):
     x, z, s = me()
-    nz, ns, slots, many = plan.nz, plan.ns, plan.slots, plan.many
+    nz, ns, slots = plan.nz, plan.ns, plan.slots
     rank = x * ns + s
     own_expert = rank // plan.group
     own_turn = (rank % plan.group) // plan.halves
@@ -143,25 +117,17 @@
     part = ns // plan.halves
     own_source = x * part + s // plan.halves
     chunk = plan.tokens
-
-    load_in = pltpu.make_async_copy(w_in.at[layer], win_v, local_sem.at[0])
-    load_down = pltpu.make_async_copy(w_down.at[layer], wdown_v, local_sem.at[1])
-    load_in.start()
-    load_down.start()
-    if backward:
-        load_gate = pltpu.make_async_copy(gate_up, gbuf, local_sem.at[3])
-        load_gate.start()
-    greet_plane(plan, along=True)
+    own_copy = pltpu.make_async_copy(r.rows_in, r.line.at[z], r.own_sem.at[0])
 
     def along(block, piece, step, own):
         at = pl.ds(piece * chunk, chunk)
-        src = rows_in.at[at] if own else line.at[block, at]
-        sem = line_right if step > 0 else line_left
+        src = r.rows_in.at[at] if own else r.line.at[block, at]
+        sem = r.line_right if step > 0 else r.line_left
         return remote(
             src,
-            line.at[block, at],
+            r.line.at[block, at],
             sem.at[block, piece],
-            line_recv.at[block, piece],
+            r.line_recv.at[block, piece],
             (x, z + step, s),
         )
 
@@ -173,53 +139,54 @@
         to_x, to_s = owner(block, expert)
         here = (to_x == x) & (to_s == s)
         return here, remote(
-            sbuf.at[block, expert],
-            xbuf.at[block // 2, own_source],
-            to_send.at[block, expert],
-            to_recv.at[block // 2, own_source],
+            r.sbuf.at[block, expert],
+            r.xbuf.at[block // 2, own_source],
+            r.to_send.at[block, expert],
+            r.to_recv.at[block // 2, own_source],
             (to_x, z, to_s),
         )
 
-    def return_copy(block, half, source):
+    def return_copy(block, cut, source):
         to_x = source // part
         to_s = (source % part) * plan.halves + own_half
         here = (to_x == x) & (to_s == s)
         return here, remote(
-            ybuf.at[block // 2, half, source],
-            rbuf.at[block, half, own_expert],
-            back_send.at[block // 2, half, source],
-            back_recv.at[block, half, own_expert],
+            r.ybuf.at[block // 2, cut, source],
+            r.rbuf.at[block, cut, own_expert],
+            r.back_send.at[block // 2, cut, source],
+            r.back_recv.at[block, cut, own_expert],
             (to_x, z, to_s),
         )
 
-    def sum_copy(block, half):
+    def sum_copy(block, cut):
         rightward = (block > z).astype(jnp.int32)
         to = z - 1 + 2 * rightward
         into = jnp.where((rightward == 1) & (block == to), nz, block)
         return remote(
-            pbuf.at[block, half],
-            qbuf.at[into, half],
-            sum_send.at[block, half],
-            sum_recv.at[into, half],
+            r.pbuf.at[block, cut],
+            r.qbuf.at[into, cut],
+            r.sum_send.at[block, cut],
+            r.sum_recv.at[into, cut],
             (x, to, s),
         )
 
-    for piece in range(plan.micro):
-
-        @pl.when(z + 1 < nz)
-        def _():
-            along(z, piece, 1, True).start()
-
-        @pl.when(z > 0)
-        def _():
-            along(z, piece, -1, True).start()
-
-    own_copy = pltpu.make_async_copy(rows_in, line.at[z], local_sem.at[2])
-    own_copy.start()
-    own_copy.wait()
-
-    def stage_put(index):
+    def begin():
+        for piece in range(plan.micro):
+
+            @pl.when(z + 1 < nz)
+            def _():
+                along(z, piece, 1, True).start()
+
+            @pl.when(z > 0)
+            def _():
+                along(z, piece, -1, True).start()
+
+        own_copy.start()
+
+    def fetch(index):
         block = nearest(z, index, nz)
+        if index == 0:
+            own_copy.wait()
         for piece in range(plan.micro):
 
             @pl.when(block < z)
@@ -238,10 +205,13 @@
                 def _():
                     along(block, piece, -1, False).start()
 
+    def put(index):
+        block = nearest(z, index, nz)
+
         def lay(step, _):
             at = pl.ds(pl.multiple_of(step * TILE, TILE), TILE)
-            laid = jnp.dot(put[block], line[block, :, at], preferred_element_type=F32)
-            sbuf[block, :, :, at] = laid.astype(BF16).reshape(EXP_DEV, slots, TILE)
+            laid = jnp.dot(r.put[block], r.line[block, :, at], preferred_element_type=F32)
+            r.sbuf[block, :, :, at] = laid.astype(BF16).reshape(EXP_DEV, slots, TILE)
             return 0
 
         lax.fori_loop(0, D // TILE, lay, 0)
@@ -251,124 +221,117 @@
             @pl.when(here)
             def _():
                 pltpu.make_async_copy(
-                    sbuf.at[block, expert],
-                    xbuf.at[block // 2, own_source],
-                    to_recv.at[block // 2, own_source],
+                    r.sbuf.at[block, expert],
+                    r.xbuf.at[block // 2, own_source],
+                    r.to_recv.at[block // 2, own_source],
                 ).start()
 
             @pl.when(jnp.logical_not(here))
             def _():
                 copy.start()
 
-    def stage_expert(index):
-        block = nearest(z, index, nz)
+    def compute(block, now):
         pair = block // 2
         for source in range(plan.sources):
-            landed(xbuf.at[pair, source], to_recv.at[pair, source])
-        pltpu.make_async_copy(xbuf.at[pair], sent_save.at[pair], save_sem.at[0, pair]).start()
-        taken = xbuf[pair].reshape(many, D)
+            landed(r.xbuf.at[pair, source], r.to_recv.at[pair, source])
+        few = plan.sources // 2
+        span = few * slots
 
         def middle(step, _):
-            at = pl.multiple_of(step * TILE, TILE)
+            rows = pl.ds(pl.multiple_of(step * span, 16), span)
+            taken = r.xbuf[pair, pl.ds(step * few, few)].reshape(span, D)
             if backward:
                 grad_hidden = lax.dot_general(
-                    taken,
-                    wdown_v[pl.ds(at, TILE), :],
-                    (((1,), (1,)), ((), ())),
-                    preferred_element_type=F32,
+                    taken, r.wdown_v[...], NARROW, preferred_element_type=F32
                 )
-                gate = gbuf[pair, :, pl.ds(at, TILE)].astype(F32)
-                up = gbuf[pair, :, pl.ds(FF + at, TILE)].astype(F32)
+                gate = r.gbuf[pair, rows, :FF].astype(F32)
+                up = r.gbuf[pair, rows, FF:].astype(F32)
                 sig = 1.0 / (1.0 + jnp.exp(-gate))
                 gs = gate * sig
                 grad_gate = grad_hidden * up * (sig + gs * (1.0 - sig))
-                gbuf[pair, :, pl.ds(at, TILE)] = grad_gate.astype(BF16)
-                gbuf[pair, :, pl.ds(FF + at, TILE)] = (grad_hidden * gs).astype(BF16)
+                r.gbuf[pair, rows, :FF] = grad_gate.astype(BF16)
+                r.gbuf[pair, rows, FF:] = (grad_hidden * gs).astype(BF16)
             else:
-                gate = jnp.dot(taken, win_v[:, pl.ds(at, TILE)], preferred_element_type=F32)
-                up = jnp.dot(taken, win_v[:, pl.ds(FF + at, TILE)], preferred_element_type=F32)
-                gbuf[pair, :, pl.ds(at, TILE)] = gate.astype(BF16)
-                gbuf[pair, :, pl.ds(FF + at, TILE)] = up.astype(BF16)
-                zbuf[pair, :, pl.ds(at, TILE)] = (gate / (1.0 + jnp.exp(-gate)) * up).astype(BF16)
+                gate = jnp.dot(taken, r.win_v[:, :FF], preferred_element_type=F32)
+                up = jnp.dot(taken, r.win_v[:, FF:], preferred_element_type=F32)
+                r.gbuf[pair, rows, :FF] = gate.astype(BF16)
+                r.gbuf[pair, rows, FF:] = up.astype(BF16)
+                r.zbuf[pair, rows] = (gate / (1.0 + jnp.exp(-gate)) * up).astype(BF16)
             return 0
 
-        lax.fori_loop(0, FF // TILE, middle, 0)
-        if backward:
-            pltpu.make_async_copy(gbuf.at[pair], grad_save.at[pair], save_sem.at[1, pair]).start()
-        else:
-            pltpu.make_async_copy(gbuf.at[pair], gate_up.at[pair], save_sem.at[1, pair]).start()
-            pltpu.make_async_copy(zbuf.at[pair], hidden.at[pair], save_sem.at[2, pair]).start()
-
-        def last(step, _):
-            half = step // (CUT // TILE)
-            at = pl.multiple_of(step * TILE, TILE)
-            inside = pl.multiple_of((step % (CUT // TILE)) * TILE, TILE)
+        lax.fori_loop(0, 2, middle, 0)
+
+        def last(cut, _):
+            at = pl.ds(pl.multiple_of(cut * CUT, CUT), CUT)
             if backward:
                 result = lax.dot_general(
-                    gbuf[pair],
-                    win_v[pl.ds(at, TILE), :],
-                    (((1,), (1,)), ((), ())),
-                    preferred_element_type=F32,
+                    r.gbuf[pair], r.win_v[at, :], NARROW, preferred_element_type=F32
                 )
             else:
-                result = jnp.dot(
-                    zbuf[pair], wdown_v[:, pl.ds(at, TILE)], preferred_element_type=F32
-                )
-            ybuf[pair, half, :, :, pl.ds(inside, TILE)] = result.astype(BF16).reshape(
-                plan.sources, slots, TILE
-            )
-
+                result = jnp.dot(r.zbuf[pair], r.wdown_v[:, at], preferred_element_type=F32)
+            r.ybuf[pair, cut] = result.astype(BF16).reshape(plan.sources, slots, CUT)
+            if now:
+                return_cut(block, cut)
             return 0
 
-        lax.fori_loop(0, D // TILE, last, 0)
-
-    def give_back(index):
+        lax.fori_loop(0, CUTS, last, 0)
+
+    def return_cut(block, cut):
+        pair = block // 2
+        for source in range(plan.sources):
+            here, copy = return_copy(block, cut, source)
+
+            @pl.when(here)
+            def _():
+                pltpu.make_async_copy(
+                    r.ybuf.at[pair, cut, source],
+                    r.rbuf.at[block, cut, own_expert],
+                    r.back_recv.at[block, cut, own_expert],
+                ).start()
+
+            @pl.when(jnp.logical_not(here))
+            def _():
+                copy.start()
+
+    def own_turn_do(index, act):
         block = nearest(z, index, nz)
-        pair = block // 2
-        for half in range(CUTS):
-            for source in range(plan.sources):
-                here, copy = return_copy(block, half, source)
-
-                @pl.when(here)
-                def _():
-                    pltpu.make_async_copy(
-                        ybuf.at[pair, half, source],
-                        rbuf.at[block, half, own_expert],
-                        back_recv.at[block, half, own_expert],
-                    ).start()
-
-                @pl.when(jnp.logical_not(here))
-                def _():
-                    copy.start()
-
-    def stage_take(index):
+
+        @pl.when(block % 2 == own_turn)
+        def _():
+            act(block)
+
+    def give_back(block):
+        for cut in range(CUTS):
+            return_cut(block, cut)
+
+    def take(index):
         block = nearest(z, index, nz)
         origin = ((block < z) & (z == nz - 1)) | ((block > z) & (z == 0))
-        for half in range(CUTS):
+        for cut in range(CUTS):
             for expert in range(EXP_DEV):
-                landed(rbuf.at[block, half, expert], back_recv.at[block, half, expert])
+                landed(r.rbuf.at[block, cut, expert], r.back_recv.at[block, cut, expert])
             got = lax.dot_general(
-                take[block],
-                rbuf[block, half].reshape(EXP_DEV * slots, CUT),
+                r.take[block],
+                r.rbuf[block, cut].reshape(EXP_DEV * slots, CUT),
                 (((0,), (0,)), ((), ())),
                 preferred_element_type=F32,
             )
 
             @pl.when(block == z)
             def _():
-                at = pl.ds(half * CUT, CUT)
+                at = pl.ds(cut * CUT, CUT)
                 if backward:
-                    out[:, at] = got
+                    r.out[:, at] = got
                 else:
-                    out[:, at] = base[:, at] + got
+                    r.out[:, at] += got
 
             @pl.when(block != z)
             def _():
-                pbuf[block, half] = got.astype(BF16)
+                r.pbuf[block, cut] = got.astype(BF16)
 
             @pl.when(origin)
             def _():
-                sum_copy(block, half).start()
+                sum_copy(block, cut).start()
 
     def relay(turn):
         lower = z < nz // 2
@@ -380,55 +343,28 @@
 
         @pl.when((z > 0) & (z < nz - 1))
         def _():
-            for half in range(CUTS):
-                landed(qbuf.at[block, half], sum_recv.at[block, half])
-                pbuf[block, half] = (
-                    pbuf[block, half].astype(F32) + qbuf[block, half].astype(F32)
+            for cut in range(CUTS):
+                landed(r.qbuf.at[block, cut], r.sum_recv.at[block, cut])
+                r.pbuf[block, cut] = (
+                    r.pbuf[block, cut].astype(F32) + r.qbuf[block, cut].astype(F32)
                 ).astype(BF16)
-                sum_copy(block, half).start()
-
-    def own_turn_do(index, act):
-        @pl.when(nearest(z, index, nz) % 2 == own_turn)
-        def _():
-            act(index)
-
-    final = nz - 1
-    stage_put(0)
-    load_in.wait()
-    load_down.wait()
-    if backward:
-        load_gate.wait()
-    for index in range(1, nz):
-        stage_put(index)
-        own_turn_do(index - 1, stage_expert)
-        if 1 < index < final:
-            own_turn_do(index - 1, give_back)
-    for index in range(1, nz - 2):
-        stage_take(index)
-    own_turn_do(final, stage_expert)
-    own_turn_do(final, give_back)
-    stage_take(final)
-    own_turn_do(final - 1, give_back)
-    own_turn_do(0, give_back)
-    relay(0)
-    stage_take(final - 1)
-    stage_take(0)
-    for turn in (2, 1) if nz == 4 else range(1, nz - 1):
-        relay(turn)
-    for half in range(CUTS):
-        at = pl.ds(half * CUT, CUT)
-
-        @pl.when(z + 1 < nz)
-        def _():
-            landed(qbuf.at[z, half], sum_recv.at[z, half])
-            out[:, at] += qbuf[z, half].astype(F32)
-
-        @pl.when(z > 0)
-        def _():
-            landed(qbuf.at[nz, half], sum_recv.at[nz, half])
-            out[:, at] += qbuf[nz, half].astype(F32)
-
-    def drain(block, _):
+                sum_copy(block, cut).start()
+
+    def finish():
+        for cut in range(CUTS):
+            at = pl.ds(cut * CUT, CUT)
+
+            @pl.when(z + 1 < nz)
+            def _():
+                landed(r.qbuf.at[z, cut], r.sum_recv.at[z, cut])
+                r.out[:, at] += r.qbuf[z, cut].astype(F32)
+
+            @pl.when(z > 0)
+            def _():
+                landed(r.qbuf.at[nz, cut], r.sum_recv.at[nz, cut])
+                r.out[:, at] += r.qbuf[nz, cut].astype(F32)
+
+    def free_put(block):
         for piece in range(plan.micro):
 
             @pl.when((block <= z) & (z + 1 < nz))
@@ -446,78 +382,457 @@
             def _():
                 copy.wait_send()
 
-        @pl.when(block % 2 == own_turn)
-        def _():
-            for half in range(CUTS):
-                for source in range(plan.sources):
-                    here, copy = return_copy(block, half, source)
-
-                    @pl.when(jnp.logical_not(here))
-                    def _():
-                        copy.wait_send()
-
+    def free_back(block):
+        for cut in range(CUTS):
+            for source in range(plan.sources):
+                here, copy = return_copy(block, cut, source)
+
+                @pl.when(jnp.logical_not(here))
+                def _():
+                    copy.wait_send()
+
+    def free_sum(block):
         @pl.when(block != z)
         def _():
-            for half in range(CUTS):
-                sum_copy(block, half).wait_send()
-
+            for cut in range(CUTS):
+                sum_copy(block, cut).wait_send()
+
+    def free_all():
+        def free(block, _):
+            free_put(block)
+
+            @pl.when(block % 2 == own_turn)
+            def _():
+                free_back(block)
+
+            free_sum(block)
+            return 0
+
+        lax.fori_loop(0, nz, free, 0)
+
+    return SimpleNamespace(
+        begin=begin,
+        fetch=fetch,
+        put=put,
+        expert=lambda index, now=True: own_turn_do(index, lambda block: compute(block, now)),
+        give_back=lambda index: own_turn_do(index, give_back),
+        take=take,
+        relay=relay,
+        finish=finish,
+        free_put=lambda index: free_put(nearest(z, index, nz)),
+        free_back=lambda index: own_turn_do(index, free_back),
+        free_sum=lambda index: free_sum(nearest(z, index, nz)),
+        free_all=free_all,
+    )
+
+
+def late_relays(nz):
+    return (2, 1) if nz == 4 else range(1, nz - 1)
+
+
+def first_part(plan, stages, loaded):
+    last = plan.nz - 1
+    stages.fetch(0)
+    stages.put(0)
+    loaded()
+    for index in range(1, plan.nz):
+        stages.fetch(index)
+        stages.put(index)
+        stages.expert(index - 1, 1 < index < last)
+
+
+def second_part(plan, stages, steps=()):
+    last = plan.nz - 1
+    steps = iter(steps)
+
+    def another():
+        next(steps, lambda: None)()
+
+    for index in range(1, plan.nz - 2):
+        stages.take(index)
+    stages.expert(last)
+    another()
+    stages.take(last)
+    stages.give_back(last - 1)
+    stages.give_back(0)
+    another()
+    stages.relay(0)
+    stages.take(last - 1)
+    another()
+    stages.take(0)
+
+
+def weight_tiles(plan, given, hidden, grad_both, grad_rows, in_term, down_term, tile_v, sem):
+    counts = (D // TILE, FF // TILE)
+
+    def copy(tile):
+        if isinstance(tile, int) and tile >= counts[0]:
+            to = down_term.at[pl.ds((tile - counts[0]) * TILE, TILE)]
+        else:
+            to = in_term.at[pl.ds(pl.multiple_of(tile * TILE, TILE), TILE)]
+        return pltpu.make_async_copy(tile_v.at[tile % 2], to, sem.at[tile % 2])
+
+    def summed(left, right):
+        total = lax.dot_general(left(0), right(0), ACROSS, preferred_element_type=F32)
+        for pair in range(1, plan.blocks):
+            total += lax.dot_general(left(pair), right(pair), ACROSS, preferred_element_type=F32)
+        return total.astype(BF16)
+
+    def rows_of(ref, pair, at):
+        return ref[pair, :, :, at].reshape(plan.many, -1)
+
+    def in_tile(tile, _):
+        @pl.when(tile >= 2)
+        def _():
+            copy(tile % 2).wait()
+
+        at = pl.ds(pl.multiple_of(tile * TILE, TILE), TILE)
+        tile_v[tile % 2] = summed(lambda p: rows_of(given, p, at), lambda p: grad_both[p])
+        copy(tile).start()
         return 0
 
-    lax.fori_loop(0, nz, drain, 0)
-    for pair in range(plan.blocks):
-        pltpu.make_async_copy(xbuf.at[pair], sent_save.at[pair], save_sem.at[0, pair]).wait()
-        if backward:
-            pltpu.make_async_copy(gbuf.at[pair], grad_save.at[pair], save_sem.at[1, pair]).wait()
-        else:
-            pltpu.make_async_copy(gbuf.at[pair], gate_up.at[pair], save_sem.at[1, pair]).wait()
-            pltpu.make_async_copy(zbuf.at[pair], hidden.at[pair], save_sem.at[2, pair]).wait()
-
-
-def moe_call(plan, layer, backward, collective_id, rows_in, put, take, w_in, w_down, last):
-    nz, blocks, slots, many, sources = plan.nz, plan.blocks, plan.slots, plan.many, plan.sources
-    vmem = pl.BlockSpec(memory_space=pltpu.VMEM)
-    hbm = pl.BlockSpec(memory_space=pltpu.HBM)
-    saved = (blocks, sources, slots, D)
-    shape = jax.ShapeDtypeStruct
-    outs = [shape((plan.rows, D), F32), shape(saved, BF16), shape((blocks, many, 2 * FF), BF16)]
-    if not backward:
-        outs.append(shape((blocks, many, FF), BF16))
-    return pl.pallas_call(
-        functools.partial(moe_kernel, plan, layer, backward),
-        out_shape=outs,
-        in_specs=[vmem, vmem, vmem, hbm, hbm, hbm if backward else vmem],
-        out_specs=[vmem] + [hbm] * (len(outs) - 1),
-        scratch_shapes=[
-            pltpu.VMEM((nz, plan.rows, D), BF16),
-            pltpu.VMEM((nz, EXP_DEV, slots, D), BF16),
-            pltpu.VMEM(saved, BF16),
-            pltpu.VMEM((blocks, CUTS, sources, slots, CUT), BF16),
-            pltpu.VMEM((nz, CUTS, EXP_DEV, slots, CUT), BF16),
-            pltpu.VMEM((nz, CUTS, plan.rows, CUT), BF16),
-            pltpu.VMEM((nz + 1, CUTS, plan.rows, CUT), BF16),
-            pltpu.VMEM((D, 2 * FF), BF16),
-            pltpu.VMEM((FF, D), BF16),
-            pltpu.VMEM((blocks, many, 2 * FF), BF16),
-            pltpu.VMEM((blocks, many, FF), BF16),
-            DMA((nz, plan.micro)),
-            DMA((nz, plan.micro)),
-            DMA((nz, plan.micro)),
-            DMA((nz, EXP_DEV)),
-            DMA((blocks, sources)),
-            DMA((blocks, CUTS, sources)),
-            DMA((nz, CUTS, EXP_DEV)),
-            DMA((nz, CUTS)),
-            DMA((nz + 1, CUTS)),
-            DMA((4,)),
-            DMA((3, blocks)),
-        ],
+    def first():
+        lax.fori_loop(0, counts[0], in_tile, 0)
+
+    def second():
+        for step in range(counts[1]):
+            tile = counts[0] + step
+            copy(tile % 2).wait()
+            at = slice(step * TILE, (step + 1) * TILE)
+            tile_v[tile % 2] = summed(
+                lambda p: hidden[p, :, at], lambda p: grad_rows[p].reshape(plan.many, D)
+            )
+            copy(tile).start()
+
+    def finish():
+        for tile in range(sum(counts) - 2, sum(counts)):
+            copy(tile).wait()
+
+    return first, second, finish
+
+
+PASS_BUFFERS = ("line", "xbuf", "rbuf", "qbuf")
+PASS_SEMAPHORES = (
+    "own_sem",
+    "line_recv",
+    "line_right",
+    "line_left",
+    "to_send",
+    "to_recv",
+    "back_send",
+    "back_recv",
+    "sum_send",
+    "sum_recv",
+)
+SHARED_BUFFERS = ("sbuf", "ybuf", "pbuf", "win_v", "wdown_v", "gbuf", "zbuf")
+
+
+def pass_scratch(plan):
+    nz, blocks, slots, sources, rows = plan.nz, plan.blocks, plan.slots, plan.sources, plan.rows
+    return [
+        pltpu.VMEM((nz, rows, D), BF16),
+        pltpu.VMEM((blocks, sources, slots, D), BF16),
+        pltpu.VMEM((nz, CUTS, EXP_DEV, slots, CUT), BF16),
+        pltpu.VMEM((nz + 1, CUTS, rows, CUT), BF16),
+        DMA((1,)),
+        DMA((nz, plan.micro)),
+        DMA((nz, plan.micro)),
+        DMA((nz, plan.micro)),
+        DMA((nz, EXP_DEV)),
+        DMA((blocks, sources)),
+        DMA((blocks, CUTS, sources)),
+        DMA((nz, CUTS, EXP_DEV)),
+        DMA((nz, CUTS)),
+        DMA((nz + 1, CUTS)),
+    ]
+
+
+def shared_scratch(plan):
+    nz, blocks, slots, many = plan.nz, plan.blocks, plan.slots, plan.many
+    return [
+        pltpu.VMEM((nz, EXP_DEV, slots, D), BF16),
+        pltpu.VMEM((blocks, CUTS, plan.sources, slots, CUT), BF16),
+        pltpu.VMEM((nz, CUTS, plan.rows, CUT), BF16),
+        pltpu.VMEM((D, 2 * FF), BF16),
+        pltpu.VMEM((FF, D), BF16),
+        pltpu.VMEM((blocks, many, 2 * FF), BF16),
+        pltpu.VMEM((blocks, many, FF), BF16),
+    ]
+
+
+PASS_NAMES = PASS_BUFFERS + PASS_SEMAPHORES
+
+
+def named(names, refs):
+    return dict(zip(names, refs, strict=True))
+
+
+def run_copies(copies):
+    for copy in copies:
+        copy.start()
+
+    def wait():
+        for copy in copies:
+            copy.wait()
+
+    return wait
+
+
+def moe_kernel(plan, layer, *refs):
+    rows_in, put, take, w_in, w_down, base, result, sent, gate_up, hidden = refs[:10]
+    count = len(PASS_NAMES)
+    r = SimpleNamespace(
+        rows_in=rows_in,
+        put=put,
+        take=take,
+        **named(PASS_NAMES, refs[10 : 10 + count]),
+        **named(SHARED_BUFFERS, refs[10 + count : -3]),
+    )
+    out, load_sem, save_sem = refs[-3:]
+    r.out = out
+    loaded = run_copies(
+        [
+            pltpu.make_async_copy(w_in.at[layer], r.win_v, load_sem.at[0]),
+            pltpu.make_async_copy(w_down.at[layer], r.wdown_v, load_sem.at[1]),
+            pltpu.make_async_copy(base, out, load_sem.at[2]),
+        ]
+    )
+    greet_plane(plan, along=True)
+    stages = moe_stages(plan, False, r)
+    stages.begin()
+    first_part(plan, stages, loaded)
+    second_part(plan, stages)
+    saved = run_copies(
+        [
+            pltpu.make_async_copy(r.xbuf, sent, save_sem.at[0]),
+            pltpu.make_async_copy(r.gbuf, gate_up, save_sem.at[1]),
+            pltpu.make_async_copy(r.zbuf, hidden, save_sem.at[2]),
+        ]
+    )
+    for turn in late_relays(plan.nz):
+        stages.relay(turn)
+    stages.finish()
+    result[...] = out[...].astype(result.dtype)
+    stages.free_all()
+    saved()
+
+
+def moe_back_kernel(plan, layer, *refs):
+    rows_in, put, take, w_in, w_down, sent, gate_up, hidden, out, in_term, down_term = refs[:11]
+    count = len(PASS_NAMES)
+    r = SimpleNamespace(
+        rows_in=rows_in,
+        put=put,
+        take=take,
+        out=out,
+        **named(PASS_NAMES, refs[11 : 11 + count]),
+        **named(SHARED_BUFFERS, refs[11 + count : -4]),
+    )
+    given, tile_v, load_sem, tile_sem = refs[-4:]
+    loaded = run_copies(
+        [
+            pltpu.make_async_copy(w_in.at[layer], r.win_v, load_sem.at[0]),
+            pltpu.make_async_copy(w_down.at[layer], r.wdown_v, load_sem.at[1]),
+            pltpu.make_async_copy(gate_up, r.gbuf, load_sem.at[2]),
+            pltpu.make_async_copy(sent, given, load_sem.at[3]),
+            pltpu.make_async_copy(hidden, r.zbuf, load_sem.at[4]),
+        ]
+    )
+    greet_plane(plan, along=True)
+    stages = moe_stages(plan, True, r)
+    first, second, finish = weight_tiles(
+        plan, given, r.zbuf, r.gbuf, r.xbuf, in_term, down_term, tile_v, tile_sem
+    )
+    stages.begin()
+    first_part(plan, stages, loaded)
+    second_part(plan, stages, (first, second))
+    for turn in late_relays(plan.nz):
+        stages.relay(turn)
+    stages.finish()
+    stages.free_all()
+    finish()
+
+
+def moe_both_kernel(plan, layer, *refs):
+    rows_in, rows_back, one, weighted, w_in, w_down, base = refs[:7]
+    out, out_back, in_term, down_term = refs[7:11]
+    count = len(PASS_NAMES)
+    shared = named(SHARED_BUFFERS, refs[11 + 2 * count : -2])
+    ahead = SimpleNamespace(
+        rows_in=rows_in,
+        put=one,
+        take=weighted,
+        out=out,
+        **named(PASS_NAMES, refs[11 : 11 + count]),
+        **shared,
+    )
+    back = SimpleNamespace(
+        rows_in=rows_back,
+        put=weighted,
+        take=one,
+        out=out_back,
+        **named(PASS_NAMES, refs[11 + count : 11 + 2 * count]),
+        **shared,
+    )
+    load_sem, tile_sem = refs[-2:]
+    loaded = run_copies(
+        [
+            pltpu.make_async_copy(w_in.at[layer], ahead.win_v, load_sem.at[0]),
+            pltpu.make_async_copy(w_down.at[layer], ahead.wdown_v, load_sem.at[1]),
+            pltpu.make_async_copy(base, out, load_sem.at[2]),
+        ]
+    )
+    greet_plane(plan, along=True)
+    forward = moe_stages(plan, False, ahead)
+    backward = moe_stages(plan, True, back)
+    first, second, finish = weight_tiles(
+        plan,
+        ahead.xbuf,
+        back.zbuf,
+        back.gbuf,
+        back.xbuf,
+        in_term,
+        down_term,
+        ahead.line,
+        tile_sem,
+    )
+    nz, last = plan.nz, plan.nz - 1
+    forward.begin()
+    first_part(plan, forward, loaded)
+    backward.begin()
+    order = list(reversed(range(nz)))
+    relays = list(late_relays(nz))
+
+    def arrive():
+        for index in range(3, nz):
+            backward.fetch(index)
+
+    second_part(
+        plan,
+        forward,
+        (
+            lambda: backward.fetch(1),
+            lambda: backward.fetch(2),
+            arrive,
+        ),
+    )
+    backward.fetch(0)
+
+    def put(index):
+        forward.free_put(index)
+        backward.put(index)
+
+    def expert(index):
+        forward.free_back(index)
+        backward.expert(index)
+
+    def take(index):
+        forward.free_sum(index)
+        backward.take(index)
+
+    put(order[0])
+    for turn in relays[: len(relays) // 2]:
+        forward.relay(turn)
+    put(order[1])
+    expert(order[0])
+    for turn in relays[len(relays) // 2 :]:
+        forward.relay(turn)
+    put(order[2])
+    expert(order[1])
+    forward.finish()
+    take(order[0])
+    for place in range(3, nz):
+        put(order[place])
+        expert(order[place - 1])
+        take(order[place - 2])
+    backward.relay(0)
+    expert(order[-1])
+    first()
+    take(order[-2])
+    for turn in relays:
+        backward.relay(turn)
+    second()
+    take(order[-1])
+    backward.finish()
+    backward.free_all()
+    finish()
+
+
+def moe_specs(plan, collective_id):
+    return dict(
         compiler_params=pltpu.CompilerParams(
             collective_id=collective_id, has_side_effects=True, vmem_limit_bytes=VMEM_LIMIT
         ),
-        cost_estimate=pl.CostEstimate(
-            flops=100_000_000_000, bytes_accessed=30_000_000, transcendentals=0
-        ),
-    )(rows_in, put, take, w_in, w_down, last)
+    )
+
+
+def saved_shapes(plan):
+    return [
+        jax.ShapeDtypeStruct((plan.blocks, plan.sources, plan.slots, D), BF16),
+        jax.ShapeDtypeStruct((plan.blocks, plan.many, 2 * FF), BF16),
+        jax.ShapeDtypeStruct((plan.blocks, plan.many, FF), BF16),
+    ]
+
+
+TERMS = [jax.ShapeDtypeStruct((D, 2 * FF), BF16), jax.ShapeDtypeStruct((FF, D), BF16)]
+
+
+def moe_call(plan, layer, kind, collective_id, rows_in, put, take, w_in, w_down, base):
+    vmem = pl.BlockSpec(memory_space=pltpu.VMEM)
+    hbm = pl.BlockSpec(memory_space=pltpu.HBM)
+    return pl.pallas_call(
+        functools.partial(moe_kernel, plan, layer),
+        out_shape=[jax.ShapeDtypeStruct((plan.rows, D), kind)] + saved_shapes(plan),
+        in_specs=[vmem] * 3 + [hbm] * 3,
+        out_specs=[vmem] + [hbm] * 3,
+        scratch_shapes=pass_scratch(plan) + shared_scratch(plan) + [pltpu.VMEM((plan.rows, D), F32), DMA((3,)), DMA((3,))],
+        **moe_specs(plan, collective_id),
+    )(rows_in, put, take, w_in, w_down, base)
+
+
+def moe_back_call(plan, layer, collective_id, rows_in, put, take, w_in, w_down, saved):
+    vmem = pl.BlockSpec(memory_space=pltpu.VMEM)
+    hbm = pl.BlockSpec(memory_space=pltpu.HBM)
+    out, *terms = pl.pallas_call(
+        functools.partial(moe_back_kernel, plan, layer),
+        out_shape=[jax.ShapeDtypeStruct((plan.rows, D), F32)] + TERMS,
+        in_specs=[vmem] * 3 + [hbm] * 5,
+        out_specs=[vmem] + [hbm] * 2,
+        scratch_shapes=pass_scratch(plan)
+        + shared_scratch(plan)
+        + [
+            pltpu.VMEM((plan.blocks, plan.sources, plan.slots, D), BF16),
+            pltpu.VMEM((2, TILE, D), BF16),
+            DMA((5,)),
+            DMA((2,)),
+        ],
+        **moe_specs(plan, collective_id),
+    )(rows_in, put, take, w_in, w_down, *saved)
+    return out, terms
+
+
+def both_fit(plan):
+    scratch = pass_scratch(plan) * 2 + shared_scratch(plan)
+    words = sum(
+        math.prod(part.shape) for part in scratch if getattr(part, "dtype", None) == BF16
+    )
+    return 2 * words + 10 * 2**20 < VMEM_LIMIT and plan.rows == TILE
+
+
+def moe_both_call(plan, layer, collective_id, rows_in, rows_back, one, weighted, w_in, w_down, base):
+    vmem = pl.BlockSpec(memory_space=pltpu.VMEM)
+    hbm = pl.BlockSpec(memory_space=pltpu.HBM)
+    out, out_back, *terms = pl.pallas_call(
+        functools.partial(moe_both_kernel, plan, layer),
+        out_shape=[jax.ShapeDtypeStruct((plan.rows, D), F32)] * 2 + TERMS,
+        in_specs=[vmem, hbm, vmem, vmem] + [hbm] * 3,
+        out_specs=[vmem] * 2 + [hbm] * 2,
+        scratch_shapes=pass_scratch(plan) * 2
+        + shared_scratch(plan)
+        + [DMA((3,)), DMA((2,))],
+        **moe_specs(plan, collective_id),
+    )(rows_in, rows_back, one, weighted, w_in, w_down, base)
+    return out, out_back, terms
 
 
 def expert_spread(plan, ins, outs, send, recv, pass_send, pass_recv):
@@ -547,20 +862,18 @@
             (to // ns, z, to % ns),
         )
 
-    def start():
-        for which in range(2):
-            for expert in range(EXP_DEV):
-                here, copy = first(expert, which)
-
-                @pl.when(here)
-                def _():
-                    pltpu.make_async_copy(
-                        ins[which].at[expert], outs[which].at[x, s], recv.at[x, s, which]
-                    ).start()
-
-                @pl.when(jnp.logical_not(here))
-                def _():
-                    copy.start()
+    def start(expert, which):
+        here, copy = first(expert, which)
+
+        @pl.when(here)
+        def _():
+            pltpu.make_async_copy(
+                ins[which].at[expert], outs[which].at[x, s], recv.at[x, s, which]
+            ).start()
+
+        @pl.when(jnp.logical_not(here))
+        def _():
+            copy.start()
 
     def pass_on():
         for layer, k in own:
@@ -606,7 +919,9 @@
 def spread_kernel(plan, *refs):
     greet_plane(plan)
     start, pass_on, finish = expert_spread(plan, refs[:2], refs[2:4], *refs[4:])
-    start()
+    for which in range(2):
+        for expert in range(EXP_DEV):
+            start(expert, which)
     pass_on()
     finish()
 
@@ -630,39 +945,112 @@
 
 
 def gather_kernel(plan, *refs):
-    piece, wide_ins, out, wide_outs = refs[0], refs[1:3], refs[3], refs[4:6]
-    line_recv, right, left, copy_sem, plane_recv, to_core, to_x, to_y = refs[6:14]
+    piece, table, wide_ins = refs[0], refs[1], refs[2:4]
+    out, table_out, wide_outs = refs[4], refs[5], refs[6:8]
+    (line_recv, right, left, copy_sem, plane_recv, to_core, to_x, to_y) = refs[8:16]
+    (up_recv, up_right, up_left, table_send, table_recv) = refs[16:21]
+    wide_v, low_v, load_sem = refs[21:23], refs[23:25], refs[25]
     x, z, s = me()
     nz = plan.nz
+    row, side = s // 2, s % 2
     over = (s + 2) % 4
+    loads = [
+        pltpu.make_async_copy(wide_ins[which].at[expert], wide_v[which].at[expert], load_sem.at[which, expert])
+        for which in range(2)
+        for expert in range(EXP_DEV)
+    ]
+    for load in loads:
+        load.start()
     greet_plane(plan, along=True)
-    start, pass_on, finish = expert_spread(plan, wide_ins, wide_outs, *refs[14:])
-    size = piece.shape[0] // 2
-    whole = pl.ds(0, 2 * size)
-    parts = (pl.ds(0, size), pl.ds(size, size))
-    core = (x, z, s + 1 - 2 * (s % 2))
+    start, pass_on, finish = expert_spread(plan, low_v, wide_outs, *refs[26:])
+    third = piece.shape[0] // 3
+    parts = (
+        (pl.ds(0, 2 * third), pl.ds(0, third), pl.ds(third, third)),
+        (
+            pl.ds(2 * third, third),
+            pl.ds(2 * third, third // 2),
+            pl.ds(2 * third + third // 2, third // 2),
+        ),
+    )
+    core = (x, z, s + 1 - 2 * side)
     across_x = (1 - x, z, s)
     across_y = (x, z, over)
 
     def along(block, step, own):
-        place = out.at[x, block, s]
+        rows = parts[0][0]
+        place = out.at[x, block, s, rows]
         sem = right if step > 0 else left
         return remote(
-            piece if own else place, place, sem.at[block], line_recv.at[block], (x, z + step, s)
-        )
-
-    def passed(layer, block, shard, rows, kind, sem, to, own=False):
+            piece.at[rows] if own else place,
+            place,
+            sem.at[block],
+            line_recv.at[block],
+            (x, z + step, s),
+        )
+
+    def upward(block, layer, to_row, step, own=False):
+        rows = parts[1][0]
+        place = out.at[layer, block, to_row * 2 + side, rows]
+        sem = up_right if step > 0 else up_left
+        return remote(
+            piece.at[rows] if own else place,
+            place,
+            sem.at[block, layer, to_row],
+            up_recv.at[block, layer, to_row],
+            (x, z + step, s),
+        )
+
+    def passed(layer, block, shard, part, kind, sem, to, own=False):
+        rows = parts[part][kind]
         place = out.at[layer, block, shard, rows]
         return remote(
-            piece if own else place,
+            piece.at[rows] if own else place,
             place,
-            sem.at[layer, block, shard // 2],
-            plane_recv.at[layer, block, shard, kind],
+            sem.at[layer, block, shard // 2, part],
+            plane_recv.at[layer, block, shard, part, kind],
             to,
         )
 
-    def arrived(layer, block, shard, rows, kind):
-        landed(out.at[layer, block, shard, rows], plane_recv.at[layer, block, shard, kind])
+    def arrived(layer, block, shard, part, kind):
+        landed(
+            out.at[layer, block, shard, parts[part][kind]],
+            plane_recv.at[layer, block, shard, part, kind],
+        )
+
+    def column_copies(block, part, own=False, ways=3):
+        ways = ((to_x, across_x), (to_y, across_y), (to_core, core))[:ways]
+        return [passed(x, block, s, part, 0, sem, to, own) for sem, to in ways]
+
+    def neighbour_copies(block, part):
+        return [
+            passed(1 - x, block, s, part, 1, to_y, across_y),
+            passed(1 - x, block, s, part, 0, to_core, core),
+            passed(x, block, over, part, 2, to_x, across_x),
+            passed(x, block, over, part, 0, to_core, core),
+        ]
+
+    def send_up(block, layer, to_row, own=False):
+        @pl.when((block <= z) & (z + 1 < nz))
+        def _():
+            upward(block, layer, to_row, 1, own).start()
+
+        @pl.when((block >= z) & (z > 0))
+        def _():
+            upward(block, layer, to_row, -1, own).start()
+
+    def neighbours_of(block, part):
+        copies = neighbour_copies(block, part)
+        arrived(1 - x, block, s, part, 0)
+        copies[0].start()
+        copies[1].start()
+        arrived(x, block, over, part, 0)
+        copies[2].start()
+        copies[3].start()
+
+    def opposite_of(block, part):
+        arrived(1 - x, block, over, part, 1)
+        arrived(1 - x, block, over, part, 2)
+        passed(1 - x, block, over, part, 0, to_core, core).start()
 
     @pl.when(z + 1 < nz)
     def _():
@@ -672,15 +1060,29 @@
     def _():
         along(z, -1, True).start()
 
+    send_up(z, x, row, True)
     own = pltpu.make_async_copy(piece, out.at[x, z, s], copy_sem.at[0])
     own.start()
-    start()
-
-    def column_copies(block, own=False):
-        ways = ((to_x, across_x), (to_y, across_y), (to_core, core))
-        return [passed(x, block, s, whole, 0, sem, to, own) for sem, to in ways]
-
-    def column(index):
+    for part in (1, 0):
+        for copy in column_copies(z, part, True):
+            copy.start()
+
+    def table_copy(step):
+        to = (z + step) % nz
+        return remote(
+            table.at[to], table_out.at[z], table_send.at[step - 1], table_recv.at[z], (x, to, s)
+        )
+
+    for step in range(1, nz):
+        table_copy(step).start()
+    table_out[z] = table[z]
+    neighbours_of(z, 1)
+    send_up(z, 1 - x, row)
+    send_up(z, x, 1 - row)
+    opposite_of(z, 1)
+    send_up(z, 1 - x, 1 - row)
+
+    def column(index, _):
         block = nearest(z, index, nz)
 
         @pl.when(block < z)
@@ -699,58 +1101,40 @@
             def _():
                 along(block, -1, False).start()
 
-        @pl.when(block == z)
-        def _():
-            for copy in column_copies(block, True):
-                copy.start()
-
-        @pl.when(block != z)
-        def _():
-            for copy in column_copies(block):
-                copy.start()
-
-    def neighbour_copies(block):
-        return [
-            passed(1 - x, block, s, parts[0], 1, to_y, across_y),
-            passed(1 - x, block, s, whole, 0, to_core, core),
-            passed(x, block, over, parts[1], 2, to_x, across_x),
-            passed(x, block, over, whole, 0, to_core, core),
-        ]
-
-    def neighbours(index):
-        block = nearest(z, index, nz)
-        copies = neighbour_copies(block)
-        arrived(1 - x, block, s, whole, 0)
-        copies[0].start()
-        copies[1].start()
-        arrived(x, block, over, whole, 0)
-        copies[2].start()
-        copies[3].start()
-
-    def opposite(index):
-        block = nearest(z, index, nz)
-        arrived(1 - x, block, over, parts[0], 1)
-        arrived(1 - x, block, over, parts[1], 2)
-        passed(1 - x, block, over, whole, 0, to_core, core).start()
-
-    def each(act):
-        def body(index, _):
-            act(index)
-            return 0
-
-        lax.fori_loop(0, nz, body, 0)
-
-    each(column)
-    each(neighbours)
-    each(opposite)
+        for copy in column_copies(block, 0):
+            copy.start()
+        for layer in range(2):
+            for to_row in range(2):
+                upward(block, layer, to_row, 1).wait_recv()
+                send_up(block, layer, to_row)
+                passed(layer, block, to_row * 2 + side, 1, 0, to_core, core).start()
+        return 0
+
+    def neighbours(index, _):
+        neighbours_of(nearest(z, index, nz), 0)
+        return 0
+
+    def opposite(index, _):
+        opposite_of(nearest(z, index, nz), 0)
+        return 0
+
+    for place, load in enumerate(loads):
+        which, expert = place // EXP_DEV, place % EXP_DEV
+        load.wait()
+        low_v[which][expert] = wide_v[which][expert].astype(BF16)
+        start(expert, which)
+    lax.fori_loop(1, nz, column, 0)
+    lax.fori_loop(0, nz, neighbours, 0)
+    lax.fori_loop(0, nz, opposite, 0)
     own.wait()
     pass_on()
+    for step in range(1, nz):
+        block = (z + step) % nz
+        landed(table_out.at[block], table_recv.at[block])
+        table_copy(step).wait_send()
 
     def drain(block, _):
-        other = s + 1 - 2 * (s % 2)
-        for layer in range(2):
-            for row in range(2):
-                arrived(layer, block, row * 2 + other % 2, whole, 0)
+        other = s + 1 - 2 * side
 
         @pl.when((block <= z) & (z + 1 < nz))
         def _():
@@ -760,41 +1144,75 @@
         def _():
             along(block, -1, False).wait_send()
 
-        for copy in column_copies(block) + neighbour_copies(block):
-            copy.wait_send()
-        passed(1 - x, block, over, whole, 0, to_core, core).wait_send()
+        for layer in range(2):
+            for to_row in range(2):
+                for part in range(2):
+                    arrived(layer, block, to_row * 2 + other % 2, part, 0)
+                    passed(layer, block, to_row * 2 + side, part, 0, to_core, core).wait_send()
+
+                @pl.when((block <= z) & (z + 1 < nz))
+                def _():
+                    upward(block, layer, to_row, 1).wait_send()
+
+                @pl.when((block >= z) & (z > 0))
+                def _():
+                    upward(block, layer, to_row, -1).wait_send()
+
+        def plane(part):
+            for copy in column_copies(block, part, ways=2):
+                copy.wait_send()
+            passed(1 - x, block, s, part, 1, to_y, across_y).wait_send()
+            passed(x, block, over, part, 2, to_x, across_x).wait_send()
+
+        plane(0)
+
+        @pl.when(block == z)
+        def _():
+            plane(1)
+
         return 0
 
     lax.fori_loop(0, nz, drain, 0)
     finish()
 
 
-def gather_call(plan, collective_id, attention, experts):
+def gather_call(plan, collective_id, attention, table, experts):
     hbm = pl.BlockSpec(memory_space=pltpu.HBM)
     vmem = pl.BlockSpec(memory_space=pltpu.VMEM)
     nx, nz, ns = plan.nx, plan.nz, plan.ns
-    outs = [jax.ShapeDtypeStruct((nx, nz, ns) + attention.shape, BF16)]
+    outs = [
+        jax.ShapeDtypeStruct((nx, nz, ns) + attention.shape, BF16),
+        jax.ShapeDtypeStruct(table.shape, F32),
+    ]
     outs += [jax.ShapeDtypeStruct((nx, ns) + part.shape[1:], BF16) for part in experts]
     return pl.pallas_call(
         functools.partial(gather_kernel, plan),
         out_shape=outs,
-        in_specs=[vmem] * 3,
-        out_specs=[hbm] * 3,
+        in_specs=[vmem, vmem, hbm, hbm],
+        out_specs=[hbm, vmem, hbm, hbm],
         scratch_shapes=[
             DMA((nz,)),
             DMA((nz,)),
             DMA((nz,)),
             DMA((1,)),
-            DMA((nx, nz, ns, 3)),
-            DMA((nx, nz, 2)),
-            DMA((nx, nz, 2)),
-            DMA((nx, nz, 2)),
+            DMA((nx, nz, ns, 2, 3)),
+            DMA((nx, nz, 2, 2)),
+            DMA((nx, nz, 2, 2)),
+            DMA((nx, nz, 2, 2)),
+            DMA((nz, nx, 2)),
+            DMA((nz, nx, 2)),
+            DMA((nz, nx, 2)),
+            DMA((nz - 1,)),
+            DMA((nz,)),
         ]
+        + [pltpu.VMEM(part.shape, F32) for part in experts]
+        + [pltpu.VMEM(part.shape, BF16) for part in experts]
+        + [DMA((2, EXP_DEV))]
         + spread_scratch(plan),
         compiler_params=pltpu.CompilerParams(
             collective_id=collective_id, has_side_effects=True, vmem_limit_bytes=VMEM_LIMIT
         ),
-    )(attention, *experts)
+    )(attention, table, *experts)
 
 
 def expert_collect(plan, ins, outs, parts, stage, load, swap_send, swap_recv, send, recv):
@@ -1178,10 +1596,6 @@
     )(*grads, *values)
 
 
-NARROW = (((1,), (1,)), ((), ()))
-ACROSS = (((0,), (0,)), ((), ()))
-
-
 def greet_shards(plan):
     x, z, s = me()
     barrier = pltpu.get_barrier_semaphore()
@@ -1325,9 +1739,9 @@
 def return_kernel(plan, layer, *refs):
     (grad_out, grad_moe, middle, start, low, queries, kv, mixed) = refs[:8]
     (gains, cosine, sine, mask, weights) = refs[8:13]
-    (grad_in, terms) = refs[13:15]
-    (win_v, wout_v, branch, grad_mixed, both, part, got, in_v, out_v) = refs[15:24]
-    (load_sem, save_in, save_out, send, recv) = refs[24:]
+    (result, terms) = refs[13:15]
+    (win_v, wout_v, branch, grad_mixed, both, part, got, in_v, out_v, grad_in) = refs[15:25]
+    (load_sem, save_in, save_out, send, recv) = refs[25:]
     x, z, s = me()
     tokens, rows, micro, ns = plan.tokens, plan.rows, plan.micro, plan.ns
     length = ns * tokens
@@ -1457,6 +1871,7 @@
     scaled = grad_normed * gains[0:1, :]
     inner = jnp.mean(scaled * hidden, axis=1, keepdims=True)
     grad_in[...] += inverse * scaled - hidden * (inverse * inverse * inverse * inner)
+    result[...] = grad_in[...].astype(result.dtype)
     gain_one = jnp.sum(grad_normed * hidden * inverse, axis=0, keepdims=True)
     place = lax.broadcasted_iota(jnp.int32, (128, D), 0)
     rows_of = jnp.where(place == 0, gain_one, jnp.where(place == 1, gain_two, 0.0))
@@ -1480,7 +1895,7 @@
     return pl.pallas_call(
         functools.partial(return_kernel, plan, layer),
         out_shape=[
-            shape((rows, D), F32),
+            shape((rows, D), BF16 if layer > 0 else F32),
             shape((D, WIN + D), BF16),
         ],
         in_specs=[vmem] * 12 + [hbm],
@@ -1495,6 +1910,7 @@
             pltpu.VMEM(exchange, BF16),
             pltpu.VMEM((D, WIN), BF16),
             pltpu.VMEM((WQ, D), BF16),
+            pltpu.VMEM((rows, D), F32),
             DMA((2,)),
             DMA((D // 256,)),
             DMA((WQ // 256,)),
@@ -1507,7 +1923,7 @@
     )(*grads, *saved, gains, *tables, weights)
 
 
-def slot_tables(plan, routes, gates):
+def slot_table(plan, routes, gates):
     experts, nz = plan.experts, plan.nz
     named = routes[..., None] == jnp.arange(experts, dtype=jnp.int32)
     gate = jnp.sum(jnp.where(named, gates[..., None], 0.0), axis=2)
@@ -1516,7 +1932,12 @@
     rank = jnp.einsum("ut,mte->mue", earlier, named.astype(BF16), preferred_element_type=F32)
     table = jnp.stack([jnp.where(named, rank, -1.0), gate])
     table = table.reshape(2, plan.micro, plan.tokens, nz, EXP_DEV).transpose(3, 0, 1, 4, 2)
-    table = lax.all_to_all(table, "expert", split_axis=0, concat_axis=0, tiled=True)
+    return table.reshape(nz, -1, plan.tokens)
+
+
+def slot_places(plan, table):
+    nz = plan.nz
+    table = table.reshape(nz, 2, plan.micro, EXP_DEV, plan.tokens)
     rank, gate = table[:, 0], table[:, 1]
     first = jnp.arange(plan.micro, dtype=F32)[:, None, None] * plan.capacity
     place = jnp.where(rank >= 0, rank + first, -1.0).transpose(0, 2, 1, 3)
@@ -1551,24 +1972,29 @@
     def mine(value):
         return lax.dynamic_slice_in_dim(value, section * micro, micro, 0)
 
-    paired = plan.nx == 2 and plan.ns == 4 and query_weight.shape[1] % 32 == 0
+    paired = plan.nx == 2 and plan.ns == 4 and query_weight.shape[1] % 96 == 0
     gain_columns = jnp.pad(norm_gains[0].T, ((0, 0), (0, PAD - 2)))
     attention_weights = jnp.concatenate(
         [query_weight[0], key_value_weight[0], gain_columns, output_weight[0]], axis=1
     ).astype(BF16)
-    expert_weights = (expert_gate_up[0].astype(BF16), expert_down[0].astype(BF16))
+    table = slot_table(plan, mine(routes), mine(gate_weights))
     if paired:
-        weights, wide_in, wide_down = gather_call(plan, 1, attention_weights, expert_weights)
+        weights, table, wide_in, wide_down = gather_call(
+            plan, 1, attention_weights, table, (expert_gate_up[0], expert_down[0])
+        )
     else:
         weights = lax.all_gather(
             attention_weights, ("section", "expert", "shard"), axis=0, tiled=True
         )
-        wide_in, wide_down = spread_call(plan, 1, *expert_weights)
+        table = lax.all_to_all(table, "expert", split_axis=0, concat_axis=0, tiled=True)
+        wide_in, wide_down = spread_call(
+            plan, 1, expert_gate_up[0].astype(BF16), expert_down[0].astype(BF16)
+        )
     weights = weights.reshape(layers, D, WIN + D)
     gains = weights[:, :, PROJ : PROJ + 2].transpose(0, 2, 1).astype(F32)
     wide_in = wide_in.reshape(layers, D, 2 * FF)
     wide_down = wide_down.reshape(layers, FF, D)
-    one, weighted = slot_tables(plan, mine(routes), mine(gate_weights))
+    one, weighted = slot_places(plan, table)
 
     offset = shard_index * tokens
     position = (offset + jnp.arange(tokens, dtype=jnp.int32)).astype(F32)
@@ -1587,64 +2013,66 @@
     tables = (cosine, sine, allowed.astype(F32))
 
     hidden = mine(inputs).reshape(rows, D)
-    kept = []
+    grad = mine(cotangent).reshape(rows, D)
+    kept, passed = [], []
+    attention_terms = [None] * layers
+    expert_terms = [None] * layers
     for layer in range(layers):
         start = hidden.astype(BF16)
         middle, normed, low, queries, kv, mixed = attend_call(
             plan, layer, 2 + layer, start, gains[layer], tables, weights
         )
-        hidden, sent, gate_up, hidden_low = moe_call(
-            plan,
-            layer,
-            False,
-            2 + layers + layer,
-            normed,
-            one,
-            weighted,
-            wide_in,
-            wide_down,
-            middle,
-        )
-        kept.append(((middle, start, low, queries, kv, mixed), sent, gate_up, hidden_low))
+        kept.append((middle, start, low, queries, kv, mixed))
+        if layer == layers - 1 and both_fit(plan):
+            hidden, grad_moe, expert_terms[layer] = moe_both_call(
+                plan,
+                layer,
+                2 + layers + layer,
+                normed,
+                grad,
+                one,
+                weighted,
+                wide_in,
+                wide_down,
+                middle,
+            )
+            passed.append(None)
+        else:
+            hidden, *saved = moe_call(
+                plan,
+                layer,
+                F32 if layer == layers - 1 else BF16,
+                2 + layers + layer,
+                normed,
+                one,
+                weighted,
+                wide_in,
+                wide_down,
+                middle,
+            )
+            passed.append(saved)
     output = hidden.reshape(micro, tokens, D)
 
-    grad = mine(cotangent).reshape(rows, D)
-    attention_terms = [None] * layers
-    expert_terms = [None] * layers
     for layer in reversed(range(layers)):
-        saved, sent, gate_up, hidden_low = kept[layer]
         grad_out = grad.astype(BF16)
-        grad_moe, grad_sent, grad_both = moe_call(
-            plan,
-            layer,
-            True,
-            2 + 2 * layers + layer,
-            grad_out,
-            weighted,
-            one,
-            wide_in,
-            wide_down,
-            gate_up,
-        )
-        in_term = jnp.einsum(
-            "rd,rf->df",
-            sent.reshape(-1, D),
-            grad_both.reshape(-1, 2 * FF),
-            preferred_element_type=F32,
-        ).astype(BF16)
-        down_term = jnp.einsum(
-            "rf,rd->fd",
-            hidden_low.reshape(-1, FF),
-            grad_sent.reshape(-1, D),
-            preferred_element_type=F32,
-        ).astype(BF16)
-        expert_terms[layer] = (in_term, down_term)
+        if passed[layer] is not None:
+            grad_moe, expert_terms[layer] = moe_back_call(
+                plan,
+                layer,
+                2 + 2 * layers + layer,
+                grad_out,
+                weighted,
+                one,
+                wide_in,
+                wide_down,
+                passed[layer],
+            )
         grad, attention_terms[layer] = return_call(
             plan,
             layer,
             2 + 3 * layers + layer,
             (grad_out, grad_moe),
-            saved,
+            kept[layer],
             gains[layer],
             tables,
             weights,

time: 1140 us -> 1020 us (0.89)
  Pallas kernels: 1040 us -> 972 us
  matrix products: 29.9 us -> 0.2 us
  other arithmetic: 32.8 us -> 18 us
    pallas_call x4 -> x3, Pallas kernels: 541 us -> 488 us  [the longest x1 227 us: moe_both_call(): pl.pallas_call(functools.partial(moe_both_kernel, plan, layer), out_shape...]
    dot_general x5 -> x1, matrix products: 29.9 us -> 0.2 us  [slot_table(): jnp.einsum('ut,mte->mue', earlier, named.astype(BF16), preferred_element_...]
    pallas_call x1, Pallas kernels: 190 us -> 171 us  [gather_call(): pl.pallas_call(functools.partial(gather_kernel, plan), out_shape=outs, in...]
    convert_element_type x6 -> x2, other arithmetic: 17.5 us -> 2.13 us  [the longest x1 1.18 us: slot_places(): weighted = weighted.astype(BF16).reshape(shape)]
  transfers between devices with their start and end apart: 1 -> 0, of which waited for: 0 -> 0; matrix products, arithmetic and copies ran while one was open for 2% -> 0% of each run, Pallas kernels for 19% -> 0%
where the time goes in v4:
time: 1020 us; the launch traced here: 1010 us
  Pallas kernels  972 us (95%)
  local copies, waits for them, and re-layouts  20.6 us (2%)
  other arithmetic  18 us (2%)
    pallas_call x1, Pallas kernels, moe_both_call(): pl.pallas_call(functools.partial(moe_both_kernel, plan, layer), out_shape...  227 us
    pallas_call x1, Pallas kernels, reduce_call(): pl.pallas_call(functools.partial(reduce_kernel, plan), out_shape=[jax.Sha...  185 us
    pallas_call x1, Pallas kernels, gather_call(): pl.pallas_call(functools.partial(gather_kernel, plan), out_shape=outs, in...  171 us
    pallas_call x1, Pallas kernels, moe_call(): pl.pallas_call(functools.partial(moe_kernel, plan, layer), out_shape=[jax...  131 us
    pallas_call x1, Pallas kernels, moe_back_call(): pl.pallas_call(functools.partial(moe_back_kernel, plan, layer), out_shape...  129 us
    pallas_call x2, Pallas kernels, return_call(): pl.pallas_call(functools.partial(return_kernel, plan, layer), out_shape=[...  78.1 us
    pallas_call x2, Pallas kernels, attend_call(): pl.pallas_call(functools.partial(attend_kernel, plan, layer), out_shape=[...  50.6 us

profile of v4, /device:TPU:0, one launch (start us, length us, event | category | flops | bytes accessed | tf_op | source)
XLA Modules:
  0.0 1012.2 jit_solution(15228902168153087408)
XLA Ops:
  0.6 0.0 copy-start
  0.7 0.0 copy-start.5
  0.7 0.0 copy-start.6
  0.7 0.7 copy-done
  1.3 0.1 constant_dynamic-slice_fusion.2
  1.5 0.1 eq.62
  1.5 0.7 constant_dynamic-slice_fusion.4
  2.3 0.7 constant_dynamic-slice_fusion.3
  3.0 0.2 fusion.2
  3.2 0.6 copy.42
  3.8 0.8 copy.41
  4.6 0.1 iota_compare_fusion.2
  4.7 0.9 convert_bitcast_fusion.3
  5.7 0.3 fusion.10
  6.0 0.1 pad_maximum_fusion.1
  6.1 0.7 tile.20
  6.7 0.1 pad_maximum_fusion
  6.8 0.7 tile.8
  7.5 0.9 and_convert_fusion.refs_4_.refs_11_
  8.4 0.0 copy-done.5
  8.4 0.0 copy-done.6
  8.4 0.0 copy-start.7
  8.5 0.1 convert_bitcast_fusion.1
  8.5 0.9 fusion.4.refs_0_
  9.4 0.7 copy-done.7
  10.1 0.5 copy-done.8
  10.6 1.2 constant_dynamic-slice_fusion
  11.8 170.7 %shard_map.170 = (bf16[2,4,4,96,3712]{4,3,2,1,0:T(8,128)(2,1)}, f32[4,16,128]{2,1,0:T(8,128)}, bf16[2,4,384,1536]{3,2,1,0:T(8,128)(2,1)}, bf16[2,4,192,1536]{3,2,1,0:T(8,128)(2,1)}) custom-call(bf16[96,3712]{1,0:T(8,128)(2,1)} %fusion.4.refs_0_, f32[4,16,128]{2,1,0:T(8,128)} %bitcast.111, f32[4,384,1536]{2,1,0:T(8,128)} %bitcast.91, f32[4,192,1536]{2,1,0:T(8,128)} %bitcast.98), custom_call_target="tpu_custom_call" | custom-call | tf_op jit(solution)/shard_map/pallas_call | solution.py:1188
  182.5 0.7 slice_bitcast_fusion.6
  183.2 0.8 select_bitcast_fusion
  184.0 0.3 broadcast_in_dim.84
  184.4 0.4 broadcast_in_dim.85
  184.8 0.3 eq.59
  185.2 1.0 eq.60
  186.2 1.2 select_convert_fusion
  187.4 0.9 convert_element_type.34.refs_1_.refs_2_
  188.4 1.2 convert_bitcast_fusion
  189.6 0.1 slice_bitcast_fusion
  189.7 0.9 copy.46.refs_1_.refs_8_
  190.6 0.9 copy.43.refs_1_.refs_8_
  191.4 24.7 %shard_map.171 = (f32[256,1536]{1,0:T(8,128)}, bf16[256,1536]{1,0:T(8,128)(2,1)}, bf16[256,1536]{1,0:T(8,128)(2,1)}, bf16[256,1536]{1,0:T(8,128)(2,1)}, bf16[4,2...) custom-call(bf16[256,1536]{1,0:T(8,128)(2,1)} %bitcast.92, f32[2,1536]{1,0:T(2,128)} %copy.43.refs_1_.refs_8_, ...), custom_call_target="tpu_custom_call" | custom-call | tf_op jit(solution)/shard_map/pallas_call | solution.py:1714
  216.1 131.3 %shard_map.172 = (bf16[256,1536]{1,0:T(8,128)(2,1)}, bf16[2,8,80,1536]{3,2,1,0:T(8,128)(2,1)}, bf16[2,640,1536]{2,1,0:T(8,128)(2,1)}, bf16[2,640,768]{2,1,0:T(8,128)(2,1)}) custom-call(bf16[256,1536]{1,0:T(8,128)(2,1)} %get-tuple-element.43.refs_0_, bf16[4,320,256]{2,1,0:T(8,128)(2,1)} %convert_element_type.34.refs_1_.refs_2_, ...), custom_call_target="tpu_custom_call" | custom-call | tf_op jit(solution)/shard_map/pallas_call | solution.py:783
  347.4 25.9 %shard_map.173 = (f32[256,1536]{1,0:T(8,128)}, bf16[256,1536]{1,0:T(8,128)(2,1)}, bf16[256,1536]{1,0:T(8,128)(2,1)}, bf16[256,1536]{1,0:T(8,128)(2,1)}, bf16[4,2...) custom-call(bf16[256,1536]{1,0:T(8,128)(2,1)} %get-tuple-element.48.refs_0_.refs_3_, f32[2,1536]{1,0:T(2,128)} %copy.46.refs_1_.refs_8_, ...), custom_call_target="tpu_custom_call" | custom-call | tf_op jit(solution)/shard_map/pallas_call | solution.py:1714
  373.3 227.4 %shard_map.174 = (f32[256,1536]{1,0:T(8,128)}, f32[256,1536]{1,0:T(8,128)}, bf16[1536,1536]{1,0:T(8,128)(2,1)}, bf16[768,1536]{1,0:T(8,128)(2,1)}) custom-call(bf16[256,1536]{1,0:T(8,128)(2,1)} %get-tuple-element.49.refs_0_, bf16[256,1536]{1,0:T(8,128)(2,1)} %bitcast.94, bf16[4,320,256]{2,1,0:T(8,128)(2,1)} %convert_element_type.34.refs_1_.refs_2_, ...), custom_call_target="tpu_custom_call" | custom-call | tf_op jit(solution)/shard_map/pallas_call | solution.py:825
  600.8 39.5 %shard_map.175 = (bf16[256,1536]{1,0:T(8,128)(2,1)}, bf16[1536,3712]{1,0:T(8,128)(2,1)}) custom-call(bf16[256,1536]{1,0:T(8,128)(2,1)} %bitcast.95, f32[256,1536]{1,0:T(8,128)} %get-tuple-element.52.refs_1_, f32[256,1536]{1,0:T(8,128)} %get-tuple-element.50.refs_6_.refs_2_, bf16[256,1536]{1,0:T(8,128)(2,1)} %get-tuple-element.48.refs_0_.refs_3_, ...), custom_call_target="tpu_custom_call" | custom-call | tf_op jit(solution)/shard_map/pallas_call | solution.py:1895
  640.3 128.9 %shard_map.176 = (f32[256,1536]{1,0:T(8,128)}, bf16[1536,1536]{1,0:T(8,128)(2,1)}, bf16[768,1536]{1,0:T(8,128)(2,1)}) custom-call(bf16[256,1536]{1,0:T(8,128)(2,1)} %get-tuple-element.57.refs_0_, bf16[4,320,256]{2,1,0:T(8,128)(2,1)} %get-tuple-element.100.refs_2_.refs_3_.refs_1_, bf16[4,320,256]{2,1,0:T(8,128)(2,1)} %convert_element_type.34.refs_1_.refs_2_, ...), custom_call_target="tpu_custom_call" | custom-call | tf_op jit(solution)/shard_map/pallas_call | solution.py:796
  769.3 38.6 %shard_map.177 = (f32[256,1536]{1,0:T(8,128)}, bf16[1536,3712]{1,0:T(8,128)(2,1)}) custom-call(bf16[256,1536]{1,0:T(8,128)(2,1)} %get-tuple-element.57.refs_0_, f32[256,1536]{1,0:T(8,128)} %get-tuple-element.61.refs_1_, f32[256,1536]{1,0:T(8,128)} %get-tuple-element.47.refs_5_.refs_2_, bf16[256,1536]{1,0:T(8,128)(2,1)} %bitcast.93, ...), custom_call_target="tpu_custom_call" | custom-call | tf_op jit(solution)/shard_map/pallas_call | solution.py:1895
  807.8 185.1 %shard_map.178 = (f32[96,3712]{1,0:T(8,128)}, bf16[4,384,1536]{2,1,0:T(8,128)(2,1)}, bf16[4,192,1536]{2,1,0:T(8,128)(2,1)}) custom-call(bf16[4,4,96,3712]{3,2,1,0:T(8,128)(2,1)} %bitcast.90, bf16[4,4,96,3712]{3,2,1,0:T(8,128)(2,1)} %bitcast.89, bf16[4,384,1536]{2,1,0:T(8,128)(2,1)} %bitcast.97, bf16[4,192,1536]{2,1,0:T(8,128)(2,1)} %bitcast.108, ...), custom_call_target="tpu_custom_call" | custom-call | tf_op jit(solution)/shard_map/pallas_call | solution.py:1564
  992.9 0.8 slice_bitcast_fusion.5
  993.7 0.6 copy.49
  994.4 1.6 slice_bitcast_fusion.4
  996.0 2.3 slice_bitcast_fusion.2
  998.3 0.0 copy-start.2
  998.3 7.6 bitcast_convert_fusion
  1005.8 0.0 copy-done.2
  1005.8 0.0 copy-start.3
  1005.9 2.8 bitcast_convert_fusion.1
  1008.7 0.0 copy-done.3
  1008.7 0.0 copy-start.4
  1008.7 0.0 copy-start.1
  1008.7 1.1 copy.55
  1009.8 0.8 copy-done.4
  1010.7 1.1 copy.56
  1011.8 0.0 copy-done.1
  (13 shorter events, 0.1 us)
Async XLA Ops:
  0.6 0.7 copy-start
  0.7 7.8 copy-start.5
  0.7 7.8 copy-start.6
  8.4 1.7 copy-start.7
  8.5 2.1 copy-start.8
  998.3 7.6 copy-start.2
  1005.8 2.8 copy-start.3
  1008.7 2.0 copy-start.4
  1008.7 3.1 copy-start.1

commit v5 on v4

--- a/solution.py
+++ b/solution.py
@@ -1338,14 +1338,15 @@
     )(*values)
 
 
-ADDS = (0, 0, 0, 0, 8, 8, 8)
-DEPTH = 1
+ADDS = 5
+OWN_UP = 4
 
 
 def reduce_kernel(plan, *refs):
-    grads, wide_ins, out, wide_outs = refs[0:2], refs[2:6], refs[6], refs[7:9]
-    scratch = refs[9:]
-    mine, given, x_one, y_one, y_two, x_two, chain = scratch[:7]
+    grads, wide_ins, outs, wide_outs = refs[0:2], refs[2:6], refs[6:10], refs[10:12]
+    scratch = refs[12:]
+    (mine, given, x_one, y_one, y_two, x_two, chain) = scratch[:7]
+    (up, x_up, y_up, y_up_two, x_up_two) = scratch[7:12]
     (
         load_sem,
         core_send,
@@ -1360,19 +1361,29 @@
         y_two_recv,
         chain_send,
         chain_recv,
-    ) = scratch[7:20]
-    parts, stage = scratch[20:24], scratch[24:28]
+        up_send,
+        up_recv,
+        plane_send,
+        plane_recv,
+    ) = scratch[12:29]
+    parts, stage = scratch[29:33], scratch[33:37]
     x, z, s = me()
     nz = plan.nz
     row, side = s // 2, s % 2
     core = (x, z, s + 1 - 2 * side)
     across_x = (1 - x, z, s)
     across_y = (x, z, (s + 2) % 4)
-    size = grads[0].shape[2] // 2
+    third = grads[0].shape[2] // 3
     greet_plane(plan, along=True)
-    count, start, add, finish = expert_collect(plan, wide_ins, wide_outs, parts, stage, *scratch[28:])
+    count, start, add, finish = expert_collect(
+        plan, wide_ins, wide_outs, parts, stage, *scratch[37:]
+    )
     both = range(2)
-    low, high = pl.ds(0, size), pl.ds(size, size)
+    most = pl.ds(0, 2 * third)
+    low, high = pl.ds(0, third), pl.ds(third, third)
+    rest = pl.ds(2 * third, third)
+    rest_low = pl.ds(2 * third, third // 2)
+    rest_high = pl.ds(2 * third + third // 2, third // 2)
 
     def load(layer, block, to_row):
         return pltpu.make_async_copy(
@@ -1426,20 +1437,44 @@
             across_x,
         )
 
-    def send_chain(block):
+    def onward(block):
         rightward = (block > z).astype(jnp.int32)
         to = z - 1 + 2 * rightward
-        into = jnp.where((rightward == 1) & (block == to), nz, block)
+        return to, jnp.where((rightward == 1) & (block == to), nz, block)
+
+    def send_chain(block):
+        to, into = onward(block)
         return remote(
-            mine.at[x, block, row],
+            mine.at[x, block, row, most],
             chain.at[into],
             chain_send.at[block],
             chain_recv.at[into],
             (x, to, s),
         )
 
-    def gain(target, at, other):
-        target[at] = (target[at].astype(F32) + other.astype(F32)).astype(BF16)
+    def send_up(block, layer, to_row):
+        to, into = onward(block)
+        return remote(
+            mine.at[layer, block, to_row, rest],
+            up.at[into, layer, to_row],
+            up_send.at[block, layer, to_row],
+            up_recv.at[into, layer, to_row],
+            (x, to, s),
+        )
+
+    def plane_copy(step, place):
+        if step == 0:
+            src, dst, to = mine.at[1 - x, z, place, rest_low], x_up.at[place], across_x
+        elif step == 1:
+            src, dst, to = mine.at[place, z, 1 - row, rest_high], y_up.at[place], across_y
+        elif step == 2:
+            src, dst, to = mine.at[x, z, 1 - row, rest_low], y_up_two.at[0], across_y
+        else:
+            src, dst, to = mine.at[1 - x, z, row, rest_high], x_up_two.at[0], across_x
+        return remote(src, dst, plane_send.at[step, place], plane_recv.at[step, place], to)
+
+    def gain(at, other):
+        mine[at] = (mine[at].astype(F32) + other.astype(F32)).astype(BF16)
 
     def begin(index):
         block = nearest(z, nz - 1 - index, nz)
@@ -1448,38 +1483,90 @@
                 load(layer, block, to_row).start()
                 give(layer, block, to_row).start()
 
+    def is_origin(block):
+        return ((block < z) & (z == nz - 1)) | ((block > z) & (z == 0))
+
     def stage_core(index):
         block = nearest(z, nz - 1 - index, nz)
         for layer in both:
             for to_row in both:
                 load(layer, block, to_row).wait()
                 give(layer, block, to_row).wait_recv()
-                gain(mine, (layer, block, to_row), given[layer, block, to_row])
+                gain((layer, block, to_row), given[layer, block, to_row])
         for to_row in both:
             send_x_one(block, to_row).start()
         for layer in both:
             send_y_one(layer, block).start()
 
+        @pl.when(is_origin(block))
+        def _():
+            for layer in both:
+                for to_row in both:
+                    send_up(block, layer, to_row).start()
+
+    def relay_up(index):
+        block = nearest(z, nz - 1 - index, nz)
+
+        @pl.when((z > 0) & (z < nz - 1))
+        def _():
+            for layer in both:
+                for to_row in both:
+                    landed(up.at[block, layer, to_row], up_recv.at[block, layer, to_row])
+                    gain((layer, block, to_row, rest), up[block, layer, to_row])
+                    send_up(block, layer, to_row).start()
+
+    def own_up():
+        for layer in both:
+            for to_row in both:
+
+                @pl.when(z + 1 < nz)
+                def _():
+                    landed(up.at[z, layer, to_row], up_recv.at[z, layer, to_row])
+                    gain((layer, z, to_row, rest), up[z, layer, to_row])
+
+                @pl.when(z > 0)
+                def _():
+                    landed(up.at[nz, layer, to_row], up_recv.at[nz, layer, to_row])
+                    gain((layer, z, to_row, rest), up[nz, layer, to_row])
+
+        for place in both:
+            plane_copy(0, place).start()
+            plane_copy(1, place).start()
+
+    def up_first():
+        for place in both:
+            plane_copy(0, place).wait_recv()
+            gain((x, z, place, rest_low), x_up[place])
+            plane_copy(1, place).wait_recv()
+            gain((place, z, row, rest_high), y_up[place])
+        plane_copy(2, 0).start()
+        plane_copy(3, 0).start()
+
+    def up_second():
+        plane_copy(2, 0).wait_recv()
+        gain((x, z, row, rest_low), y_up_two[0])
+        plane_copy(3, 0).wait_recv()
+        gain((x, z, row, rest_high), x_up_two[0])
+
     def stage_first(index):
         block = nearest(z, nz - 1 - index, nz)
         for to_row in both:
             send_x_one(block, to_row).wait_recv()
-            gain(mine, (x, block, to_row, low), x_one[block, to_row])
+            gain((x, block, to_row, low), x_one[block, to_row])
         send_y_two(block).start()
         for layer in both:
             send_y_one(layer, block).wait_recv()
-            gain(mine, (layer, block, row, high), y_one[layer, block])
+            gain((layer, block, row, high), y_one[layer, block])
         send_x_two(block).start()
 
     def stage_second(index):
         block = nearest(z, nz - 1 - index, nz)
-        origin = ((block < z) & (z == nz - 1)) | ((block > z) & (z == 0))
         send_y_two(block).wait_recv()
-        gain(mine, (x, block, row, low), y_two[block])
+        gain((x, block, row, low), y_two[block])
         send_x_two(block).wait_recv()
-        gain(mine, (x, block, row, high), x_two[block])
-
-        @pl.when(origin)
+        gain((x, block, row, high), x_two[block])
+
+        @pl.when(is_origin(block))
         def _():
             send_chain(block).start()
 
@@ -1493,16 +1580,20 @@
             begin(index + 2)
         if index == 0:
             start()
-        if DEPTH <= index < nz + DEPTH:
-            stage_first(index - DEPTH)
-        if DEPTH + 1 <= index < nz + DEPTH + 1:
-            stage_second(index - DEPTH - 1)
-        while adds < count and adds < ADDS[index]:
+        if 1 <= index < nz + 1:
+            stage_first(index - 1)
+        if 1 <= index < nz:
+            relay_up(index - 1)
+        if 2 <= index < nz + 2:
+            stage_second(index - 2)
+        if index == OWN_UP:
+            own_up()
+        if index == OWN_UP + 1:
+            up_first()
+        while adds < count and index >= ADDS:
             add(adds)
             adds += 1
-    while adds < count:
-        add(adds)
-        adds += 1
+    up_second()
 
     def relay(turn, _):
         lower = z < nz // 2
@@ -1515,28 +1606,32 @@
         @pl.when((z > 0) & (z < nz - 1))
         def _():
             landed(chain.at[block], chain_recv.at[block])
-            gain(mine, (x, block, row), chain[block])
+            gain((x, block, row, most), chain[block])
             send_chain(block).start()
 
         return 0
 
     lax.fori_loop(0, nz - 1, relay, 0)
-    out[...] = mine[x, z, row].astype(F32)
-
-    @pl.when(z + 1 < nz)
-    def _():
-        landed(chain.at[z], chain_recv.at[z])
-        out[...] += chain[z].astype(F32)
-
-    @pl.when(z > 0)
-    def _():
-        landed(chain.at[nz], chain_recv.at[nz])
-        out[...] += chain[nz].astype(F32)
+    columns = (slice(0, WQ), slice(WQ, PROJ), slice(PROJ, WIN), slice(WIN, WIN + D))
+    for out, at in zip(outs, columns):
+        out[...] = mine[x, z, row, :, at].astype(F32)
+    for place, there in ((z, z + 1 < nz), (nz, z > 0)):
+
+        @pl.when(there)
+        def _():
+            landed(chain.at[place], chain_recv.at[place])
+            for out, at in zip(outs, columns):
+                out[: 2 * third] += chain[place, :, at].astype(F32)
 
     def drain(block, _):
         for layer in both:
             for to_row in both:
                 give(layer, block, to_row).wait_send()
+
+                @pl.when(block != z)
+                def _():
+                    send_up(block, layer, to_row).wait_send()
+
             send_y_one(layer, block).wait_send()
         for to_row in both:
             send_x_one(block, to_row).wait_send()
@@ -1550,6 +1645,8 @@
         return 0
 
     lax.fori_loop(0, nz, drain, 0)
+    for step, place in ((0, 0), (0, 1), (1, 0), (1, 1), (2, 0), (3, 0)):
+        plane_copy(step, place).wait_send()
     finish()
 
 
@@ -1559,22 +1656,28 @@
     vmem = pl.BlockSpec(memory_space=pltpu.VMEM)
     grads = [part.reshape(nz, ns, -1, part.shape[1]) for part in attention]
     values = [part.reshape(ns, part.shape[0] // ns, D) for layer in terms for part in layer]
-    size = grads[0].shape[2:]
-    half = (size[0] // 2, size[1])
+    held = [(EXP_DEV,) + part.shape[1:] for part in values[:2]]
+    rows, width = grads[0].shape[2:]
+    third = rows // 3
     return pl.pallas_call(
         functools.partial(reduce_kernel, plan),
-        out_shape=[jax.ShapeDtypeStruct(size, F32)]
-        + [jax.ShapeDtypeStruct((EXP_DEV,) + part.shape[1:], BF16) for part in values[:2]],
+        out_shape=[jax.ShapeDtypeStruct((rows, part), F32) for part in (WQ, 2 * WK, PAD, D)]
+        + [jax.ShapeDtypeStruct(shape, BF16) for shape in held],
         in_specs=[hbm] * 6,
-        out_specs=[vmem, hbm, hbm],
+        out_specs=[vmem] * 4 + [hbm] * 2,
         scratch_shapes=[
-            pltpu.VMEM((nx, nz, 2) + size, BF16),
-            pltpu.VMEM((nx, nz, 2) + size, BF16),
-            pltpu.VMEM((nz, 2) + half, BF16),
-            pltpu.VMEM((nx, nz) + half, BF16),
-            pltpu.VMEM((nz,) + half, BF16),
-            pltpu.VMEM((nz,) + half, BF16),
-            pltpu.VMEM((nz + 1,) + size, BF16),
+            pltpu.VMEM((nx, nz, 2, rows, width), BF16),
+            pltpu.VMEM((nx, nz, 2, rows, width), BF16),
+            pltpu.VMEM((nz, 2, third, width), BF16),
+            pltpu.VMEM((nx, nz, third, width), BF16),
+            pltpu.VMEM((nz, third, width), BF16),
+            pltpu.VMEM((nz, third, width), BF16),
+            pltpu.VMEM((nz + 1, 2 * third, width), BF16),
+            pltpu.VMEM((nz + 1, nx, 2, third, width), BF16),
+            pltpu.VMEM((2, third // 2, width), BF16),
+            pltpu.VMEM((2, third // 2, width), BF16),
+            pltpu.VMEM((1, third // 2, width), BF16),
+            pltpu.VMEM((1, third // 2, width), BF16),
             DMA((nx, nz, 2)),
             DMA((nx, nz, 2)),
             DMA((nx, nz, 2)),
@@ -1588,6 +1691,10 @@
             DMA((nz,)),
             DMA((nz,)),
             DMA((nz + 1,)),
+            DMA((nz, nx, 2)),
+            DMA((nz + 1, nx, 2)),
+            DMA((4, 2)),
+            DMA((4, 2)),
         ]
         + collect_scratch(plan, values),
         compiler_params=pltpu.CompilerParams(
@@ -2080,8 +2187,8 @@
     input_grad = grad.reshape(micro, tokens, D)
 
     if paired:
-        term, gate_up_grad, down_grad = reduce_call(
-            plan, 2 + 4 * layers, attention_terms, expert_terms
+        query_grad, key_value_grad, gain_grad, output_weight_grad, gate_up_grad, down_grad = (
+            reduce_call(plan, 2 + 4 * layers, attention_terms, expert_terms)
         )
     else:
         gate_up_grad, down_grad = collect_call(plan, 2 + 4 * layers, expert_terms)
@@ -2091,13 +2198,20 @@
             scatter_dimension=0,
             tiled=True,
         )
+        query_grad, key_value_grad, gain_grad, output_weight_grad = (
+            term[:, :WQ],
+            term[:, WQ:PROJ],
+            term[:, PROJ:WIN],
+            term[:, WIN:],
+        )
+    gain_grad = gain_grad[:, :2].T
     query_grad, key_value_grad, gain_grad, output_weight_grad, gate_up_grad, down_grad = (
         part.astype(F32)[None]
         for part in (
-            term[:, :WQ],
-            term[:, WQ:PROJ],
-            term[:, PROJ : PROJ + 2].T,
-            term[:, WIN:],
+            query_grad,
+            key_value_grad,
+            gain_grad,
+            output_weight_grad,
             gate_up_grad,
             down_grad,
         )

time: 1020 us -> 997 us (0.977)
  Pallas kernels: 972 us -> 951 us
    pallas_call x1, Pallas kernels: 185 us -> 164 us  [reduce_call(): pl.pallas_call(functools.partial(reduce_kernel, plan), out_shape=[jax.Sha...]
where the time goes in v5:
time: 997 us; the launch traced here: 989 us
  Pallas kernels  951 us (95%)
  local copies, waits for them, and re-layouts  19.3 us (2%)
  other arithmetic  17.4 us (2%)
    pallas_call x1, Pallas kernels, moe_both_call(): pl.pallas_call(functools.partial(moe_both_kernel, plan, layer), out_shape...  227 us
    pallas_call x1, Pallas kernels, gather_call(): pl.pallas_call(functools.partial(gather_kernel, plan), out_shape=outs, in...  171 us
    pallas_call x1, Pallas kernels, reduce_call(): pl.pallas_call(functools.partial(reduce_kernel, plan), out_shape=[jax.Sha...  164 us
    pallas_call x1, Pallas kernels, moe_call(): pl.pallas_call(functools.partial(moe_kernel, plan, layer), out_shape=[jax...  131 us
    pallas_call x1, Pallas kernels, moe_back_call(): pl.pallas_call(functools.partial(moe_back_kernel, plan, layer), out_shape...  130 us
    pallas_call x2, Pallas kernels, return_call(): pl.pallas_call(functools.partial(return_kernel, plan, layer), out_shape=[...  77.4 us
    pallas_call x2, Pallas kernels, attend_call(): pl.pallas_call(functools.partial(attend_kernel, plan, layer), out_shape=[...  50.6 us

profile of v5, /device:TPU:0, one launch (start us, length us, event | category | flops | bytes accessed | tf_op | source)
XLA Modules:
  0.0 989.2 jit_solution(10951514606350263230)
XLA Ops:
  0.6 0.0 copy-start
  0.7 0.0 copy-start.5
  0.7 0.0 copy-start.6
  0.7 0.7 copy-done
  1.3 0.1 constant_dynamic-slice_fusion.2
  1.5 0.1 eq.62
  1.5 0.7 constant_dynamic-slice_fusion.4
  2.3 0.7 constant_dynamic-slice_fusion.3
  3.0 0.2 fusion.2
  3.2 0.6 copy.42
  3.8 0.8 copy.41
  4.6 0.1 iota_compare_fusion.2
  4.7 0.9 convert_bitcast_fusion.3
  5.7 0.3 fusion.10
  6.0 0.1 pad_maximum_fusion.1
  6.1 0.7 tile.20
  6.7 0.1 pad_maximum_fusion
  6.8 0.7 tile.8
  7.5 0.9 and_convert_fusion.refs_4_.refs_11_
  8.4 0.0 copy-done.5
  8.4 0.0 copy-done.6
  8.4 0.0 copy-start.9
  8.5 0.1 convert_bitcast_fusion.1
  8.5 0.9 fusion.4.refs_0_
  9.4 0.7 copy-done.9
  10.1 0.5 copy-done.10
  10.6 1.2 constant_dynamic-slice_fusion
  11.8 170.7 %shard_map.170 = (bf16[2,4,4,96,3712]{4,3,2,1,0:T(8,128)(2,1)}, f32[4,16,128]{2,1,0:T(8,128)}, bf16[2,4,384,1536]{3,2,1,0:T(8,128)(2,1)}, bf16[2,4,192,1536]{3,2,1,0:T(8,128)(2,1)}) custom-call(bf16[96,3712]{1,0:T(8,128)(2,1)} %fusion.4.refs_0_, f32[4,16,128]{2,1,0:T(8,128)} %bitcast.111, f32[4,384,1536]{2,1,0:T(8,128)} %bitcast.88, f32[4,192,1536]{2,1,0:T(8,128)} %bitcast.95), custom_call_target="tpu_custom_call" | custom-call | tf_op jit(solution)/shard_map/pallas_call | solution.py:1188
  182.5 0.7 slice_bitcast_fusion.3
  183.2 0.8 select_bitcast_fusion
  184.1 0.3 broadcast_in_dim.84
  184.4 0.4 broadcast_in_dim.85
  184.8 0.3 eq.59
  185.2 1.0 eq.60
  186.2 1.2 select_convert_fusion
  187.4 0.9 convert_element_type.34.refs_1_.refs_2_
  188.4 1.2 convert_bitcast_fusion
  189.6 0.1 slice_bitcast_fusion
  189.7 0.9 copy.46.refs_1_.refs_8_
  190.6 0.9 copy.43.refs_1_.refs_8_
  191.4 24.7 %shard_map.171 = (f32[256,1536]{1,0:T(8,128)}, bf16[256,1536]{1,0:T(8,128)(2,1)}, bf16[256,1536]{1,0:T(8,128)(2,1)}, bf16[256,1536]{1,0:T(8,128)(2,1)}, bf16[4,2...) custom-call(bf16[256,1536]{1,0:T(8,128)(2,1)} %bitcast.89, f32[2,1536]{1,0:T(2,128)} %copy.43.refs_1_.refs_8_, ...), custom_call_target="tpu_custom_call" | custom-call | tf_op jit(solution)/shard_map/pallas_call | solution.py:1821
  216.1 131.3 %shard_map.172 = (bf16[256,1536]{1,0:T(8,128)(2,1)}, bf16[2,8,80,1536]{3,2,1,0:T(8,128)(2,1)}, bf16[2,640,1536]{2,1,0:T(8,128)(2,1)}, bf16[2,640,768]{2,1,0:T(8,128)(2,1)}) custom-call(bf16[256,1536]{1,0:T(8,128)(2,1)} %get-tuple-element.46.refs_0_, bf16[4,320,256]{2,1,0:T(8,128)(2,1)} %convert_element_type.34.refs_1_.refs_2_, ...), custom_call_target="tpu_custom_call" | custom-call | tf_op jit(solution)/shard_map/pallas_call | solution.py:783
  347.4 25.9 %shard_map.173 = (f32[256,1536]{1,0:T(8,128)}, bf16[256,1536]{1,0:T(8,128)(2,1)}, bf16[256,1536]{1,0:T(8,128)(2,1)}, bf16[256,1536]{1,0:T(8,128)(2,1)}, bf16[4,2...) custom-call(bf16[256,1536]{1,0:T(8,128)(2,1)} %get-tuple-element.51.refs_0_.refs_3_, f32[2,1536]{1,0:T(2,128)} %copy.46.refs_1_.refs_8_, ...), custom_call_target="tpu_custom_call" | custom-call | tf_op jit(solution)/shard_map/pallas_call | solution.py:1821
  373.3 227.3 %shard_map.174 = (f32[256,1536]{1,0:T(8,128)}, f32[256,1536]{1,0:T(8,128)}, bf16[1536,1536]{1,0:T(8,128)(2,1)}, bf16[768,1536]{1,0:T(8,128)(2,1)}) custom-call(bf16[256,1536]{1,0:T(8,128)(2,1)} %get-tuple-element.52.refs_0_, bf16[256,1536]{1,0:T(8,128)(2,1)} %bitcast.91, bf16[4,320,256]{2,1,0:T(8,128)(2,1)} %convert_element_type.34.refs_1_.refs_2_, ...), custom_call_target="tpu_custom_call" | custom-call | tf_op jit(solution)/shard_map/pallas_call | solution.py:825
  600.6 39.9 %shard_map.175 = (bf16[256,1536]{1,0:T(8,128)(2,1)}, bf16[1536,3712]{1,0:T(8,128)(2,1)}) custom-call(bf16[256,1536]{1,0:T(8,128)(2,1)} %bitcast.92, f32[256,1536]{1,0:T(8,128)} %get-tuple-element.55.refs_1_, f32[256,1536]{1,0:T(8,128)} %get-tuple-element.53.refs_6_.refs_2_, bf16[256,1536]{1,0:T(8,128)(2,1)} %get-tuple-element.51.refs_0_.refs_3_, ...), custom_call_target="tpu_custom_call" | custom-call | tf_op jit(solution)/shard_map/pallas_call | solution.py:2002
  640.5 129.6 %shard_map.176 = (f32[256,1536]{1,0:T(8,128)}, bf16[1536,1536]{1,0:T(8,128)(2,1)}, bf16[768,1536]{1,0:T(8,128)(2,1)}) custom-call(bf16[256,1536]{1,0:T(8,128)(2,1)} %get-tuple-element.60.refs_0_, bf16[4,320,256]{2,1,0:T(8,128)(2,1)} %get-tuple-element.106.refs_2_.refs_3_.refs_1_, bf16[4,320,256]{2,1,0:T(8,128)(2,1)} %convert_element_type.34.refs_1_.refs_2_, ...), custom_call_target="tpu_custom_call" | custom-call | tf_op jit(solution)/shard_map/pallas_call | solution.py:796
  770.2 37.5 %shard_map.177 = (f32[256,1536]{1,0:T(8,128)}, bf16[1536,3712]{1,0:T(8,128)(2,1)}) custom-call(bf16[256,1536]{1,0:T(8,128)(2,1)} %get-tuple-element.60.refs_0_, f32[256,1536]{1,0:T(8,128)} %get-tuple-element.64.refs_1_, f32[256,1536]{1,0:T(8,128)} %get-tuple-element.50.refs_5_.refs_2_, bf16[256,1536]{1,0:T(8,128)(2,1)} %bitcast.90, ...), custom_call_target="tpu_custom_call" | custom-call | tf_op jit(solution)/shard_map/pallas_call | solution.py:2002
  807.7 164.1 %shard_map.178 = (f32[96,1536]{1,0:T(8,128)}, f32[96,512]{1,0:T(8,128)}, f32[96,128]{1,0:T(8,128)}, f32[96,1536]{1,0:T(8,128)}, bf16[4,384,1536]{2,1,0:T(8,128)(2,1)}, /*index=5*/bf16[4,192,1536]{2,1,0:T(8,128)(2,1)}) custom-call(bf16[4,4,96,3712]{3,2,1,0:T(8,128)(2,1)} %bitcast.87, bf16[4,4,96,3712]{3,2,1,0:T(8,128)(2,1)} %bitcast.86, ...), custom_call_target="tpu_custom_call" | custom-call | tf_op jit(solution)/shard_map/pallas_call | solution.py:1662
  971.8 0.8 slice_bitcast_fusion.2
  972.6 0.6 copy.49
  973.3 4.6 bitcast_convert_fusion.1
  977.9 0.0 copy-done.2
  977.9 5.1 bitcast_convert_fusion
  983.0 0.0 copy-done.3
  983.0 1.1 copy.58
  984.1 0.8 copy-done.4
  985.0 1.1 copy.59
  986.1 0.3 copy-done.8
  986.4 0.8 copy.60
  987.2 0.0 copy-done.11
  987.2 0.7 copy.61
  987.9 0.0 copy-done.7
  987.9 0.8 copy.62
  988.7 0.0 copy-done.1
  (20 shorter events, 0.1 us)
Async XLA Ops:
  0.6 0.7 copy-start
  0.7 7.8 copy-start.5
  0.7 7.8 copy-start.6
  8.4 1.7 copy-start.9
  8.5 2.1 copy-start.10
  973.3 4.6 copy-start.2
  977.9 5.1 copy-start.3
  983.0 2.0 copy-start.4
  985.0 1.4 copy-start.8
  985.0 2.3 copy-start.11
  985.0 3.8 copy-start.1
  986.4 1.5 copy-start.7

commit v6 on v5

--- a/solution.py
+++ b/solution.py
@@ -1942,6 +1942,21 @@
 
     lax.fori_loop(0, WQ // 256, out_tile, 0)
     load_in.wait()
+
+    def query_tile(step, _):
+        at = pl.ds(pl.multiple_of(step * 256, 256), 256)
+        in_v[at, :WQ] = lax.dot_general(
+            low[:, at], both[:, :WQ], ACROSS, preferred_element_type=F32
+        ).astype(BF16)
+        return 0
+
+    lax.fori_loop(0, D // 256, query_tile, 0)
+    grad_normed = []
+    for step in range(D // 512):
+        at = slice(step * 512, (step + 1) * 512)
+        grad_normed.append(
+            lax.dot_general(both[:, :WQ], win_v[at, :WQ], NARROW, preferred_element_type=F32)
+        )
     for m in range(micro):
         for step in range(1, ns):
             landed(got.at[(s + step) % ns, m], recv.at[(s + step) % ns, m])
@@ -1956,21 +1971,18 @@
             ).astype(BF16)
         both[span, WQ + WK :] = total[:, WK:].astype(BF16)
 
-    def in_tile(step, _):
-        at = pl.ds(pl.multiple_of(step * 256, 256), 256)
-        in_v[at, : WQ + 2 * WK] = lax.dot_general(
-            low[:, at], both[...], ACROSS, preferred_element_type=F32
+    def key_tile(step, _):
+        at = pl.ds(pl.multiple_of(step * 512, 512), 512)
+        in_v[at, WQ:PROJ] = lax.dot_general(
+            low[:, at], both[:, WQ:], ACROSS, preferred_element_type=F32
         ).astype(BF16)
         return 0
 
-    lax.fori_loop(0, D // 256, in_tile, 0)
-    grad_normed = []
+    lax.fori_loop(0, D // 512, key_tile, 0)
     for step in range(D // 512):
         at = slice(step * 512, (step + 1) * 512)
-        grad_normed.append(
-            lax.dot_general(
-                both[...], win_v[at, : WQ + 2 * WK], NARROW, preferred_element_type=F32
-            )
+        grad_normed[step] += lax.dot_general(
+            both[:, WQ:], win_v[at, WQ:PROJ], NARROW, preferred_element_type=F32
         )
     grad_normed = jnp.concatenate(grad_normed, axis=1)
     hidden = start[...].astype(F32)

time: 997 us -> 995 us (level)
  no operation moved by 1% of the time
where the time goes in v6:
time: 995 us; the launch traced here: 987 us
  Pallas kernels  949 us (95%)
  local copies, waits for them, and re-layouts  19.3 us (2%)
  other arithmetic  17.4 us (2%)
    pallas_call x1, Pallas kernels, moe_both_call(): pl.pallas_call(functools.partial(moe_both_kernel, plan, layer), out_shape...  227 us
    pallas_call x1, Pallas kernels, gather_call(): pl.pallas_call(functools.partial(gather_kernel, plan), out_shape=outs, in...  171 us
    pallas_call x1, Pallas kernels, reduce_call(): pl.pallas_call(functools.partial(reduce_kernel, plan), out_shape=[jax.Sha...  165 us
    pallas_call x1, Pallas kernels, moe_call(): pl.pallas_call(functools.partial(moe_kernel, plan, layer), out_shape=[jax...  131 us
    pallas_call x1, Pallas kernels, moe_back_call(): pl.pallas_call(functools.partial(moe_back_kernel, plan, layer), out_shape...  130 us
    pallas_call x2, Pallas kernels, return_call(): pl.pallas_call(functools.partial(return_kernel, plan, layer), out_shape=[...  73.4 us
    pallas_call x2, Pallas kernels, attend_call(): pl.pallas_call(functools.partial(attend_kernel, plan, layer), out_shape=[...  50.6 us

profile of v6, /device:TPU:0, one launch (start us, length us, event | category | flops | bytes accessed | tf_op | source)
XLA Modules:
  0.0 986.8 jit_solution(18126447024447405305)
XLA Ops:
  0.6 0.0 copy-start
  0.7 0.0 copy-start.5
  0.7 0.0 copy-start.6
  0.7 0.7 copy-done
  1.3 0.1 constant_dynamic-slice_fusion.2
  1.5 0.1 eq.62
  1.5 0.7 constant_dynamic-slice_fusion.4
  2.3 0.7 constant_dynamic-slice_fusion.3
  3.0 0.2 fusion.2
  3.2 0.6 copy.42
  3.8 0.8 copy.41
  4.6 0.1 iota_compare_fusion.2
  4.7 0.9 convert_bitcast_fusion.3
  5.7 0.3 fusion.10
  6.0 0.1 pad_maximum_fusion.1
  6.1 0.7 tile.20
  6.7 0.1 pad_maximum_fusion
  6.8 0.7 tile.8
  7.5 0.9 and_convert_fusion.refs_4_.refs_11_
  8.4 0.0 copy-done.5
  8.4 0.0 copy-done.6
  8.4 0.0 copy-start.9
  8.5 0.1 convert_bitcast_fusion.1
  8.5 0.9 fusion.4.refs_0_
  9.4 0.7 copy-done.9
  10.1 0.5 copy-done.10
  10.6 1.2 constant_dynamic-slice_fusion
  11.8 170.7 %shard_map.170 = (bf16[2,4,4,96,3712]{4,3,2,1,0:T(8,128)(2,1)}, f32[4,16,128]{2,1,0:T(8,128)}, bf16[2,4,384,1536]{3,2,1,0:T(8,128)(2,1)}, bf16[2,4,192,1536]{3,2,1,0:T(8,128)(2,1)}) custom-call(bf16[96,3712]{1,0:T(8,128)(2,1)} %fusion.4.refs_0_, f32[4,16,128]{2,1,0:T(8,128)} %bitcast.111, f32[4,384,1536]{2,1,0:T(8,128)} %bitcast.88, f32[4,192,1536]{2,1,0:T(8,128)} %bitcast.95), custom_call_target="tpu_custom_call" | custom-call | tf_op jit(solution)/shard_map/pallas_call | solution.py:1188
  182.5 0.7 slice_bitcast_fusion.3
  183.2 0.8 select_bitcast_fusion
  184.1 0.3 broadcast_in_dim.84
  184.4 0.4 broadcast_in_dim.85
  184.8 0.3 eq.59
  185.2 1.0 eq.60
  186.2 1.2 select_convert_fusion
  187.4 0.9 convert_element_type.34.refs_1_.refs_2_
  188.4 1.2 convert_bitcast_fusion
  189.6 0.1 slice_bitcast_fusion
  189.7 0.9 copy.46.refs_1_.refs_8_
  190.6 0.9 copy.43.refs_1_.refs_8_
  191.4 24.7 %shard_map.171 = (f32[256,1536]{1,0:T(8,128)}, bf16[256,1536]{1,0:T(8,128)(2,1)}, bf16[256,1536]{1,0:T(8,128)(2,1)}, bf16[256,1536]{1,0:T(8,128)(2,1)}, bf16[4,2...) custom-call(bf16[256,1536]{1,0:T(8,128)(2,1)} %bitcast.89, f32[2,1536]{1,0:T(2,128)} %copy.43.refs_1_.refs_8_, ...), custom_call_target="tpu_custom_call" | custom-call | tf_op jit(solution)/shard_map/pallas_call | solution.py:1821
  216.1 131.3 %shard_map.172 = (bf16[256,1536]{1,0:T(8,128)(2,1)}, bf16[2,8,80,1536]{3,2,1,0:T(8,128)(2,1)}, bf16[2,640,1536]{2,1,0:T(8,128)(2,1)}, bf16[2,640,768]{2,1,0:T(8,128)(2,1)}) custom-call(bf16[256,1536]{1,0:T(8,128)(2,1)} %get-tuple-element.46.refs_0_, bf16[4,320,256]{2,1,0:T(8,128)(2,1)} %convert_element_type.34.refs_1_.refs_2_, ...), custom_call_target="tpu_custom_call" | custom-call | tf_op jit(solution)/shard_map/pallas_call | solution.py:783
  347.4 25.9 %shard_map.173 = (f32[256,1536]{1,0:T(8,128)}, bf16[256,1536]{1,0:T(8,128)(2,1)}, bf16[256,1536]{1,0:T(8,128)(2,1)}, bf16[256,1536]{1,0:T(8,128)(2,1)}, bf16[4,2...) custom-call(bf16[256,1536]{1,0:T(8,128)(2,1)} %get-tuple-element.51.refs_0_.refs_3_, f32[2,1536]{1,0:T(2,128)} %copy.46.refs_1_.refs_8_, ...), custom_call_target="tpu_custom_call" | custom-call | tf_op jit(solution)/shard_map/pallas_call | solution.py:1821
  373.3 227.3 %shard_map.174 = (f32[256,1536]{1,0:T(8,128)}, f32[256,1536]{1,0:T(8,128)}, bf16[1536,1536]{1,0:T(8,128)(2,1)}, bf16[768,1536]{1,0:T(8,128)(2,1)}) custom-call(bf16[256,1536]{1,0:T(8,128)(2,1)} %get-tuple-element.52.refs_0_, bf16[256,1536]{1,0:T(8,128)(2,1)} %bitcast.91, bf16[4,320,256]{2,1,0:T(8,128)(2,1)} %convert_element_type.34.refs_1_.refs_2_, ...), custom_call_target="tpu_custom_call" | custom-call | tf_op jit(solution)/shard_map/pallas_call | solution.py:825
  600.6 38.2 %shard_map.175 = (bf16[256,1536]{1,0:T(8,128)(2,1)}, bf16[1536,3712]{1,0:T(8,128)(2,1)}) custom-call(bf16[256,1536]{1,0:T(8,128)(2,1)} %bitcast.92, f32[256,1536]{1,0:T(8,128)} %get-tuple-element.55.refs_1_, f32[256,1536]{1,0:T(8,128)} %get-tuple-element.53.refs_6_.refs_2_, bf16[256,1536]{1,0:T(8,128)(2,1)} %get-tuple-element.51.refs_0_.refs_3_, ...), custom_call_target="tpu_custom_call" | custom-call | tf_op jit(solution)/shard_map/pallas_call | solution.py:2014
  638.9 130.1 %shard_map.176 = (f32[256,1536]{1,0:T(8,128)}, bf16[1536,1536]{1,0:T(8,128)(2,1)}, bf16[768,1536]{1,0:T(8,128)(2,1)}) custom-call(bf16[256,1536]{1,0:T(8,128)(2,1)} %get-tuple-element.60.refs_0_, bf16[4,320,256]{2,1,0:T(8,128)(2,1)} %get-tuple-element.106.refs_2_.refs_3_.refs_1_, bf16[4,320,256]{2,1,0:T(8,128)(2,1)} %convert_element_type.34.refs_1_.refs_2_, ...), custom_call_target="tpu_custom_call" | custom-call | tf_op jit(solution)/shard_map/pallas_call | solution.py:796
  769.0 35.1 %shard_map.177 = (f32[256,1536]{1,0:T(8,128)}, bf16[1536,3712]{1,0:T(8,128)(2,1)}) custom-call(bf16[256,1536]{1,0:T(8,128)(2,1)} %get-tuple-element.60.refs_0_, f32[256,1536]{1,0:T(8,128)} %get-tuple-element.64.refs_1_, f32[256,1536]{1,0:T(8,128)} %get-tuple-element.50.refs_5_.refs_2_, bf16[256,1536]{1,0:T(8,128)(2,1)} %bitcast.90, ...), custom_call_target="tpu_custom_call" | custom-call | tf_op jit(solution)/shard_map/pallas_call | solution.py:2014
  804.2 165.2 %shard_map.178 = (f32[96,1536]{1,0:T(8,128)}, f32[96,512]{1,0:T(8,128)}, f32[96,128]{1,0:T(8,128)}, f32[96,1536]{1,0:T(8,128)}, bf16[4,384,1536]{2,1,0:T(8,128)(2,1)}, /*index=5*/bf16[4,192,1536]{2,1,0:T(8,128)(2,1)}) custom-call(bf16[4,4,96,3712]{3,2,1,0:T(8,128)(2,1)} %bitcast.87, bf16[4,4,96,3712]{3,2,1,0:T(8,128)(2,1)} %bitcast.86, ...), custom_call_target="tpu_custom_call" | custom-call | tf_op jit(solution)/shard_map/pallas_call | solution.py:1662
  969.4 0.8 slice_bitcast_fusion.2
  970.2 0.6 copy.49
  970.9 4.6 bitcast_convert_fusion.1
  975.5 0.0 copy-done.2
  975.5 5.1 bitcast_convert_fusion
  980.6 0.0 copy-done.3
  980.6 1.1 copy.58
  981.7 0.8 copy-done.4
  982.6 1.1 copy.59
  983.7 0.3 copy-done.8
  984.0 0.8 copy.60
  984.8 0.0 copy-done.11
  984.8 0.7 copy.61
  985.5 0.0 copy-done.7
  985.5 0.8 copy.62
  986.3 0.0 copy-done.1
  (20 shorter events, 0.1 us)
Async XLA Ops:
  0.6 0.7 copy-start
  0.7 7.8 copy-start.5
  0.7 7.8 copy-start.6
  8.4 1.7 copy-start.9
  8.5 2.1 copy-start.10
  970.9 4.6 copy-start.2
  975.5 5.1 copy-start.3
  980.6 2.0 copy-start.4
  982.5 1.4 copy-start.8
  982.6 2.3 copy-start.11
  982.6 3.8 copy-start.1
  984.0 1.5 copy-start.7
